TPU v7x, 32 devices: a whole 2x2x4 slice. The times are simulated.
32 devices in a mesh: gx: 2 (over x), gy: 4 (over z), scene: 4 (over y, core).
Axes of the slice: x: 2, y: 2, z: 4, core: 2. Of those that a mesh axis runs over, the one named last changes fastest.
Arguments:
- field_in: bfloat16 [4, 32, 32, 64, 256], P('scene', None, 'gx', 'gy'), may hold values from -6 to 6
- grad_pre: bfloat16 [4, 32, 32, 64, 256], P('scene', None, 'gx', 'gy'), may hold values from -6 to 6
- spec_weight: bfloat16 [24, 24, 13, 2, 1024], P('gx', 'gy'), may hold values from -6 to 6
- point_weight: bfloat16 [32, 32], replicated, may hold values from -1 to 1
Outputs:
- grad_field: bfloat16 [4, 32, 32, 64, 256], P('scene', None, 'gx', 'gy')
- grad_spec: float32 [24, 24, 13, 2, 1024], P('gx', 'gy', None, None, 'scene')
All inputs are finite; a program needn't handle non-finite values.
Results may differ from a plain program's by a relative error of at most 0.0045.
Values may be sent and summed in bfloat16 or wider, within the bound.
No kernel may reach another device: no remote copies, remote signals or barrier semaphores. Data moves between devices by JAX's collectives and lax.ppermute only.
A program may use at most 128 MiB of HBM per device.

v0:
```python
import math

import jax
import jax.numpy as jnp
from jax import lax
from jax.sharding import PartitionSpec as P

MX = 24
MY = 24
MZ = 13


def angle_table(index, modes, positions, length):
    signed_freq = jnp.where(index < modes // 2, index, index - modes)
    turns = jnp.mod(signed_freq[..., None] * positions, length)
    return turns.astype(jnp.float32) * (2.0 * math.pi / length)


def z_tables(modes_z, length):
    angles = angle_table(
        jnp.arange(modes_z, dtype=jnp.int32),
        2 * modes_z,
        jnp.arange(length, dtype=jnp.int32),
        length,
    )
    cosine = jnp.cos(angles)
    sine = jnp.sin(angles)
    forward_z = jnp.concatenate([cosine, -sine], 0).T.astype(jnp.bfloat16)
    inverse_z = jnp.stack([cosine, -sine], 0)
    return (forward_z, inverse_z)


def plane_table(kx_index, ky_index, local_x, local_y, total_x, total_y):
    angle_x = angle_table(kx_index, MX, local_x, total_x)
    angle_y = angle_table(ky_index, MY, local_y, total_y)
    theta = (angle_x[:, :, None] + angle_y[:, None, :]).reshape(kx_index.shape[0], -1)
    cosine = jnp.cos(theta)
    sine = jnp.sin(theta)
    first = jnp.stack([cosine, sine], 1)
    second = jnp.stack([-sine, cosine], 1)
    return jnp.stack([first, second], 1).reshape(kx_index.shape[0] * 2, -1)


def owner_modes(rows, owner_rows, modes_xd, modes_yd, groups_y):
    owner = rows // owner_rows
    within = rows % owner_rows
    kx_index = owner // groups_y * modes_xd + within // modes_yd
    ky_index = owner % groups_y * modes_yd + within % modes_yd
    return (kx_index, ky_index)


def body(field_in, grad_pre, spec_weight, point_weight):
    highest = lax.Precision.HIGHEST
    scenes_here, channels, cells_x, cells_y, cells_z = field_in.shape
    groups_x = lax.axis_size("gx")
    groups_y = lax.axis_size("gy")
    total_x = cells_x * groups_x
    total_y = cells_y * groups_y
    cell_count = cells_x * cells_y
    norm = float(total_x * total_y * cells_z) ** (-0.5)
    modes_xd = MX // groups_x
    modes_yd = MY // groups_y
    owner_rows = modes_xd * modes_yd
    local_x = lax.axis_index("gx") * cells_x + jnp.arange(cells_x, dtype=jnp.int32)
    local_y = lax.axis_index("gy") * cells_y + jnp.arange(cells_y, dtype=jnp.int32)
    forward_z, inverse_z = z_tables(MZ, cells_z)
    z_parts = forward_z.reshape(cells_z, 2, MZ)
    field_z = jnp.einsum(
        "scnz,zpk->sckpn",
        field_in.reshape(scenes_here, channels, cell_count, cells_z),
        z_parts,
        preferred_element_type=jnp.float32,
    )
    pre_z = jnp.einsum(
        "scnz,zpk->sckpn",
        grad_pre.reshape(scenes_here, channels, cell_count, cells_z),
        z_parts,
        preferred_element_type=jnp.float32,
    )
    along_z = jnp.stack([field_z, pre_z], 1)
    data_rows = along_z.reshape(scenes_here * 2 * channels * MZ, 2 * cell_count)
    contract_last = (((1,), (1,)), ((), ()))
    rows = jnp.arange(lax.axis_size(("gx", "gy")) * owner_rows, dtype=jnp.int32)
    kx_index, ky_index = owner_modes(rows, owner_rows, modes_xd, modes_yd, groups_y)
    table = plane_table(kx_index, ky_index, local_x, local_y, total_x, total_y)
    term = lax.dot_general(
        table, data_rows, contract_last, precision=highest, preferred_element_type=jnp.float32
    )
    spectra = lax.psum_scatter(
        term.reshape(lax.axis_size(("gx", "gy")) * owner_rows, -1),
        ("gx", "gy"),
        scatter_dimension=0,
        tiled=True,
    )
    scaled = spectra.reshape(modes_xd, modes_yd, 2, scenes_here, 2, channels, MZ) * norm
    z_weight = jnp.where(jnp.arange(MZ, dtype=jnp.int32) == 0, 1.0, 2.0).astype(jnp.float32)
    field_hat = scaled[:, :, :, :, 0]
    grad_out = scaled[:, :, :, :, 1] * z_weight
    hat_re = field_hat[:, :, 0]
    hat_im = field_hat[:, :, 1]
    out_re = grad_out[:, :, 0]
    out_im = grad_out[:, :, 1]
    weights = spec_weight.astype(jnp.float32).reshape(modes_xd, modes_yd, MZ, 2, channels, channels)
    weight_re = weights[:, :, :, 0]
    weight_im = weights[:, :, :, 1]
    mode_re = jnp.einsum("abkio,absok->absik", weight_re, out_re, precision=highest) + jnp.einsum(
        "abkio,absok->absik", weight_im, out_im, precision=highest
    )
    mode_im = jnp.einsum("abkio,absok->absik", weight_re, out_im, precision=highest) - jnp.einsum(
        "abkio,absok->absik", weight_im, out_re, precision=highest
    )
    mode_flat = jnp.stack([mode_re, mode_im], 2).astype(jnp.bfloat16).reshape(owner_rows, -1)
    grad_re = jnp.einsum("absok,absik->abkio", out_re, hat_re, precision=highest) + jnp.einsum(
        "absok,absik->abkio", out_im, hat_im, precision=highest
    )
    grad_im = jnp.einsum("absok,absik->abkio", out_im, hat_re, precision=highest) - jnp.einsum(
        "absok,absik->abkio", out_re, hat_im, precision=highest
    )
    grad_local = jnp.stack([grad_re, grad_im], 3).reshape(
        modes_xd, modes_yd, MZ, 2, channels * channels
    )
    grad_spec = lax.psum_scatter(grad_local, "scene", scatter_dimension=4, tiled=True)
    contract_first = (((0,), (0,)), ((), ()))
    gathered = lax.all_gather(mode_flat, ("gx", "gy"), axis=0, tiled=True)
    mode_total = gathered.shape[0]
    values = gathered.astype(jnp.float32).reshape(mode_total * 2, -1)
    rows = jnp.arange(mode_total, dtype=jnp.int32)
    kx_index, ky_index = owner_modes(rows, owner_rows, modes_xd, modes_yd, groups_y)
    table = plane_table(kx_index, ky_index, local_x, local_y, total_x, total_y)
    back_modes = lax.dot_general(
        values, table, contract_first, precision=highest, preferred_element_type=jnp.float32
    )
    back_parts = back_modes.reshape(scenes_here, channels, MZ, 2, cell_count)
    spectral_grad = jnp.einsum("sckpn,pkz->scnz", back_parts, inverse_z, precision=highest) * norm
    spectral_grad = spectral_grad.reshape(scenes_here, channels, cells_x, cells_y, cells_z)
    local_grad = jnp.einsum(
        "oi,soxyz->sixyz", point_weight, grad_pre, preferred_element_type=jnp.float32
    )
    grad_field = (spectral_grad + local_grad).astype(jnp.bfloat16)
    return (grad_field, grad_spec)


def solution(mesh):
    return jax.shard_map(
        body,
        mesh=mesh,
        in_specs=(
            P("scene", None, "gx", "gy", None),
            P("scene", None, "gx", "gy", None),
            P("gx", "gy", None, None, None),
            P(),
        ),
        out_specs=(P("scene", None, "gx", "gy", None), P("gx", "gy", None, None, "scene")),
        check_vma=False,
    )
```

profile of v0, /device:TPU:0, one launch (start us, length us, event | category | flops | bytes accessed | tf_op | source)
XLA Modules:
  0.0 364.0 jit_solution(2994219292997482209)
XLA Ops:
  7.5 3.7 %convolution_bitcast_fusion = f32[1,1,32,13,2,256]{5,3,2,4,1,0:T(8,128)S(1)} fusion(bf16[32,256,256,1]{2,1,0,3:T(8,128)(2,1)} %bitcast.154, bf16[256,2,13,1]{0,2,1,3:T(8,128)(2,1)S(1)} %reshape.471), kind=kOutput, calls=%fused_computation.19 | convolution fusion | flops 109051904 | bytes 5059584 | tf_op jit(solution)/shard_map/scnz,zpk->sckpn/dot_general | solution.py:74
  11.2 1.3 convolution_bitcast_fusion.1
  12.5 0.3 pad_maximum_fusion.2
  12.8 1.6 copy.60
  14.3 1.3 copy.91
  15.8 2.3 add_sine_fusion
  18.1 0.2 maximum_bitcast_fusion
  18.5 2.5 copy.59
  21.0 2.0 copy.90
  23.1 9.2 %fusion.63 = f32[1152,832]{1,0:T(8,128)} fusion(f32[1152,512]{1,0:T(8,128)S(1)} %bitcast.151, f32[832,512]{1,0:T(8,128)S(1)} %bitcast.160), kind=kOutput, calls=%fused_computation.128 | convolution fusion | flops 5888802816 | bytes 7897088 | tf_op jit(solution)/shard_map/dot_general | solution.py:86
  32.3 4.9 %reshape.461 = f32[576,1664]{1,0:T(8,128)} reshape(f32[1152,832]{1,0:T(8,128)} %fusion.63) | data formatting | bytes 7667712 | tf_op jit(solution)/shard_map/reshape | solution.py:90
  37.3 0.3 reduce-scatter.5.cloned.1.call-start
  37.6 84.7 %reduce-scatter.7.cloned.1.call-done = f32[72,1664]{1,0:T(8,128)} async-done(((f32[576,1664]{1,0:T(8,128)}), f32[72,1664]{1,0:T(8,128)}) %reduce-scatter.7.cloned.1.call-update) | async-done | bytes 479248
  122.3 1.1 broadcast_multiply_fusion
  123.4 7.3 %mul.212 = f32[12,6,2,1,2,32,13]{6,5,4,2,1,0,3:T(8,128)} reshape(f32[72,1664]{1,0:T(8,128)S(1)} %broadcast_multiply_fusion) | data formatting | bytes 958464 | tf_op jit(solution)/shard_map/mul | solution.py:95
  130.7 2.1 slice_bitcast_fusion.6
  132.8 0.9 copy-done.1
  133.7 1.7 fusion.9
  135.4 1.2 slice_bitcast_fusion.9
  136.6 2.6 copy.70
  139.2 1.3 copy.72
  140.5 3.8 %slice_bitcast_fusion.13 = (f32[12,6,13,32]{2,3,1,0:T(8,128)}, f32[12,6,32,13,1]{3,2,1,0,4:T(8,128)}, f32[12,6,32,13,1]{3,2,1,0,4:T(8,128)S(1)}, f32[12,6,13,32]{2,3,1,0:T(8,128)}) fusion(f32[12,6,2,1,32,13]{5,4,2,1,0,3:T(8,128)} %fusion.9), kind=kLoop, calls=%fused_computation.28 | loop fusion | bytes 718848 | tf_op jit(solution)/shard_map/transpose.20
  144.3 2.6 copy.71
  146.9 2.6 copy.73
  149.5 12.4 %multiply_add_fusion = (f32[12,6,13,32,32]{4,3,2,1,0:T(8,128)}, f32[12,6,13,32,32]{4,3,2,1,0:T(8,128)}) fusion(f32[12,6,13,32]{3,2,1,0:T(8,128)} %copy.73, f32[12,6,13,32]{3,2,1,0:T(8,128)} %copy.72, f32[12,6,13,32]{3,2,1,0:T(8,128)} %copy.71, f32[12,6,13,32]{3,2,1,0:T(8,128)} %copy.70), kind=kLoop, calls=%fused_computation.1 | loop fusion | flops 5750784 | bytes 8146944 | tf_op jit(solution)/shard_map/add | solution.py:113
  161.9 12.8 %stack.72 = f32[12,6,13,1,1024]{4,2,1,0,3:T(8,128)} reshape(f32[12,6,13,32,32]{4,3,2,1,0:T(8,128)} %get-tuple-element.12) | data formatting | bytes 7667712 | tf_op jit(solution)/shard_map/stack | solution.py:119
  174.6 12.8 %stack.73 = f32[12,6,13,1,1024]{4,2,1,0,3:T(8,128)} reshape(f32[12,6,13,32,32]{4,3,2,1,0:T(8,128)} %get-tuple-element.13) | data formatting | bytes 7667712 | tf_op jit(solution)/shard_map/stack | solution.py:119
  187.4 9.5 %pad_maximum_fusion = f32[12,6,13,2,1024]{4,2,1,0,3:T(8,128)} fusion(f32[12,6,13,1,1024]{4,2,1,0,3:T(8,128)} %stack.73, f32[12,6,13,1,1024]{4,2,1,0,3:T(8,128)} %stack.72), kind=kLoop, calls=%fused_computation.2 | loop fusion | flops 1916928 | bytes 15335424 | tf_op jit(solution)/shard_map/stack | solution.py:119
  196.9 2.0 copy.64
  198.9 20.0 %reshape.463 = bf16[12,6,13,2,32,32]{5,4,3,2,1,0:T(8,128)(2,1)} reshape(bf16[12,6,13,2,1024]{4,3,2,1,0:T(2,128)(2,1)} %param.6) | data formatting | bytes 7667712 | tf_op jit(solution)/shard_map/reshape | solution.py:103
  218.9 0.8 fusion.40
  219.6 0.7 copy.78
  220.3 0.7 copy.80
  221.1 14.6 %fusion.2 = f32[12,6,13,1,32]{4,3,2,1,0:T(1,128)S(1)} fusion(f32[12,6,32,13,1]{2,4,3,1,0:T(1,128)S(1)} %copy.78, bf16[12,6,13,2,32,32]{5,4,3,2,1,0:T(8,128)(2,1)} %reshape.463), kind=kOutput, calls=%fused_computation.9 | convolution fusion | flops 11501568 | bytes 7907328 | tf_op jit(solution)/shard_map/abkio,absok->absik/dot_general | solution.py:106
  235.6 23.3 %fusion.4 = f32[12,6,13,1,32]{4,3,2,1,0:T(1,128)S(1)} fusion(f32[12,6,32,13,1]{2,4,3,1,0:T(1,128)S(1)} %copy.80, bf16[12,6,13,2,32,32]{5,4,3,2,1,0:T(8,128)(2,1)} %reshape.463), kind=kOutput, calls=%fused_computation.11 | convolution fusion | flops 11501568 | bytes 7907328 | tf_op jit(solution)/shard_map/abkio,absok->absik/dot_general | solution.py:106
  259.1 12.0 %fusion.3 = f32[12,6,13,1,32]{4,3,2,1,0:T(1,128)S(1)} fusion(f32[12,6,32,13,1]{2,4,3,1,0:T(1,128)S(1)} %copy.78, bf16[12,6,13,2,32,32]{5,4,3,2,1,0:T(8,128)(2,1)S(1)} %bitcast.157), kind=kOutput, calls=%fused_computation.10 | convolution fusion | flops 11501568 | bytes 8266752 | tf_op jit(solution)/shard_map/abkio,absok->absik/dot_general | solution.py:109
  271.1 12.2 %fusion.1 = f32[12,6,13,1,32]{4,3,2,1,0:T(1,128)S(1)} fusion(f32[12,6,32,13,1]{2,4,3,1,0:T(1,128)S(1)} %copy.80, bf16[12,6,13,2,32,32]{5,4,3,2,1,0:T(8,128)(2,1)S(1)} %bitcast.157), kind=kOutput, calls=%fused_computation.8 | convolution fusion | flops 11501568 | bytes 8266752 | tf_op jit(solution)/shard_map/abkio,absok->absik/dot_general | solution.py:109
  283.5 1.1 copy.62
  284.6 2.7 convert_element_type.56
  287.3 37.2 %all_gather.3 = bf16[576,832]{1,0:T(8,128)(2,1)} all-gather(bf16[72,832]{1,0:T(8,128)(2,1)} %convert_element_type.56), channel_id=1, replica_groups=mesh['gx'=2,'gy'=4,'scene'=4] {'gx','gy'}, dimensions={0}, use_global_device_ids=true | all-gather | bytes 1078272 | tf_op jit(solution)/shard_map/all_gather | solution.py:124
  324.6 2.7 reshape.465
  327.3 1.5 copy.63
  328.8 1.4 reshape.466
  330.2 2.0 fusion.11
  332.1 7.7 %bitcast_multiply_fusion = f32[32,256,256]{2,1,0:T(8,128)S(1)} fusion(f32[32,13,2,256]{3,0,2,1:T(8,128)S(1)} %fusion.11, f32[1,13,256]{2,1,0:T(8,128)} %get-tuple-element.25, f32[1,13,256]{2,1,0:T(8,128)} %get-tuple-element.24), kind=kOutput, calls=%fused_computation.5 | convolution fusion | flops 656415232 | bytes 9267200 | tf_op jit(solution)/shard_map/sckpn,pkz->scnz/dot_general | solution.py:134
  339.9 7.9 %fusion = bf16[1,32,16,16,256]{4,1,3,2,0:T(8,128)(2,1)S(1)} fusion(f32[1,32,16,16,256]{4,3,2,1,0:T(8,128)S(1)} %bitcast.153, bf16[32,16,16,256]{3,2,1,0:T(8,128)(2,1)S(1)} %bitcast.155, bf16[32,32]{1,0:T(8,128)(2,1)S(1)} %copy-done), kind=kOutput, calls=%fused_computation.4 | convolution fusion | flops 138412032 | bytes 16779264 | tf_op jit(solution)/shard_map/oi,soxyz->sixyz/dot_general | solution.py:136
  347.8 4.4 %copy.74 = bf16[1,32,16,16,256]{4,3,2,1,0:T(8,128)(2,1)} copy(bf16[1,32,16,16,256]{4,1,3,2,0:T(8,128)(2,1)S(1)} %fusion) | data formatting | bytes 8388608
  352.2 4.7 %copy.75 = f32[12,6,13,2,256]{4,3,2,1,0:T(2,128)} copy(f32[12,6,13,2,256]{4,2,1,0,3:T(8,128)} %reduce-scatter.5.cloned.1.call-done) | data formatting | bytes 3833856
  (41 shorter events, 1.2 us)
Async XLA Ops:
  7.2 332.7 %copy-start = (bf16[32,32]{1,0:T(8,128)(2,1)S(1)}, bf16[32,32]{1,0:T(8,128)(2,1)}, u32[]{:S(2)}) copy-start(bf16[32,32]{1,0:T(8,128)(2,1)} %param.7) | copy-start | bytes 6148
  7.2 115.1 %reduce-scatter.7.cloned.1.call-start = ((), (), s32[]{:S(2)}) async-start(), calls=%async_computation.3 | async-start | bytes 4313088
  7.5 3.7 %copy-start.6 = (bf16[1,32,16,16,256]{4,3,2,1,0:T(8,128)(2,1)S(1)}, bf16[1,32,16,16,256]{4,3,2,1,0:T(8,128)(2,1)}, u32[]{:S(2)}) copy-start(bf16[1,32,16,16,256]{4,3,2,1,0:T(8,128)(2,1)} %param.4) | copy-start | bytes 12582916
  21.0 2.2 copy-start.4
  37.3 314.9 %reduce-scatter.5.cloned.1.call-start = ((), (), s32[]{:S(2)}) async-start(), calls=%async_computation.2 | async-start | bytes 11796480 | tf_op jit(solution)/shard_map/reduce_scatter | solution.py:122
  130.7 3.1 copy-start.1
  198.9 20.8 %copy-start.5 = (f32[12,6,32,13,1]{3,2,1,0,4:T(8,128)S(1)}, f32[12,6,32,13,1]{3,2,1,0,4:T(8,128)}, u32[]{:S(2)}) copy-start(f32[12,6,32,13,1]{3,2,1,0,4:T(8,128)} %get-tuple-element.17) | copy-start | bytes 359428
  221.0 38.0 %slice-start = ((s8[15335424]{0:T(1024)(128)(4,1)}), s8[4194304]{0:T(1024)(128)(4,1)S(1)}, s32[]{:S(2)}) async-start(s8[15335424]{0:T(1024)(128)(4,1)} %bitcast.156), calls=%async_computation.4 | async-start | bytes 8388608
  221.1 38.0 %slice-start.1 = ((s8[15335424]{0:T(1024)(128)(4,1)}), s8[4194304]{0:T(1024)(128)(4,1)S(1)}, s32[]{:S(2)}) async-start(s8[15335424]{0:T(1024)(128)(4,1)} %bitcast.156), calls=%async_computation.5 | async-start | bytes 8388608
  235.6 23.4 %slice-start.2 = ((s8[15335424]{0:T(1024)(128)(4,1)}), s8[4194304]{0:T(1024)(128)(4,1)S(1)}, s32[]{:S(2)}) async-start(s8[15335424]{0:T(1024)(128)(4,1)} %bitcast.156), calls=%async_computation.6 | async-start | bytes 8388608
  235.6 23.4 %slice-start.3 = ((s8[15335424]{0:T(1024)(128)(4,1)}), s8[2752512]{0:T(1024)(128)(4,1)S(1)}, s32[]{:S(2)}) async-start(s8[15335424]{0:T(1024)(128)(4,1)} %bitcast.156), calls=%async_computation.7 | async-start | bytes 5505024
  284.6 45.5 %copy-start.3 = (f32[512,1152]{1,0:T(8,128)S(1)}, f32[512,1152]{1,0:T(8,128)}, u32[]{:S(2)}) copy-start(f32[512,1152]{1,0:T(8,128)} %copy.64) | copy-start | bytes 7077892
  332.1 7.8 %copy-start.2 = (bf16[1,32,16,16,256]{4,3,2,1,0:T(8,128)(2,1)S(1)}, bf16[1,32,16,16,256]{4,3,2,1,0:T(8,128)(2,1)}, u32[]{:S(2)}) copy-start(bf16[1,32,16,16,256]{4,3,2,1,0:T(8,128)(2,1)} %param.5) | copy-start | bytes 12582916
Sparse Core Ops, SparseCore 0:
  37.4 84.8 reduce-scatter.6
  197.0 78.0 reduce-scatter.4
where the time goes:
time: 369 us; the launch traced here: 364 us
  local copies, waits for them, and re-layouts  104 us (28%)
  matrix products  93.8 us (25%)
  waiting for transfers between devices  84.7 us (23%)
  blocking collectives  37.2 us (10%)
  other arithmetic  28.9 us (8%)
  between operations  14.6 us (4%)
    unnamed x3, waiting for transfers between devices  84.7 us
    all_gather x1, blocking collectives, body(): gathered = lax.all_gather(mode_flat, ('gx', 'gy'), axis=0, tiled=True)  37.2 us
    another operation x2, local copies, waits for them, and re-layouts, body(): jnp.stack([grad_re, grad_im], 3)  25.5 us
    dot_general x1, matrix products, body(): jnp.einsum('abkio,absok->absik', weight_im, out_im, precision=highest)  23.3 us
    reshape x1, local copies, waits for them, and re-layouts, body(): spec_weight.astype(jnp.float32)  20 us
    another operation x9, local copies, waits for them, and re-layouts  16.8 us
    dot_general x1, matrix products, body(): jnp.einsum('abkio,absok->absik', weight_re, out_re, precision=highest)  14.6 us
    unnamed x26, local copies, waits for them, and re-layouts  13.6 us
  transfers between devices with their start and end apart: 2, of which 1 were waited for; matrix products, arithmetic and copies ran while one was open for 32% of the time, Pallas kernels for 0%

commit v1 on v0

v1 whole, which is shorter than its diff:
```python
import functools
import math

import jax
import jax.numpy as jnp
import ml_dtypes
import numpy as np
from jax import lax
from jax.experimental import pallas as pl
from jax.experimental.pallas import tpu as pltpu
from jax.sharding import PartitionSpec as P

MX = 24
MY = 24
MZ = 13
LANES = 128
SPLIT = False
NT = (((1,), (1,)), ((), ()))
BF16 = ml_dtypes.bfloat16


def angles(xp, index, modes, positions, length):
    freq = xp.where(index < modes // 2, index, index - modes)
    turns = (freq[..., None] * positions) % length
    return turns.astype(np.float32) * np.float32(2.0 * math.pi / length)


def mode_angles(xp, rows, sizes, local_x, local_y):
    groups, groups_y, modes_xd, modes_yd, total_x, total_y = sizes
    owner = xp.repeat(xp.arange(groups, dtype=np.int32), rows)
    within = xp.tile(xp.arange(rows, dtype=np.int32), groups)
    kx = owner // groups_y * modes_xd + xp.minimum(within // modes_yd, modes_xd - 1)
    ky = owner % groups_y * modes_yd + within % modes_yd
    angle_x = angles(xp, kx, MX, local_x, total_x)
    angle_y = angles(xp, ky, MY, local_y, total_y)
    theta = (angle_x[:, :, None] + angle_y[:, None, :]).reshape(owner.shape[0], -1)
    return theta, (within < modes_xd * modes_yd)[:, None]


def split16(values):
    high = values.astype(BF16)
    low = (values - high.astype(np.float32)).astype(BF16)
    return high, low


def device_cells(xp, me, groups_y, cells_x, cells_y):
    local_x = me // groups_y * cells_x + xp.arange(cells_x, dtype=np.int32)
    local_y = me % groups_y * cells_y + xp.arange(cells_y, dtype=np.int32)
    return local_x, local_y


def forward_table(xp, first, rows, sizes, cells_x, cells_y):
    groups_y = sizes[1]
    parts = []
    for t in range(4):
        device = first + quad_offset(t, groups_y)
        theta, real = mode_angles(
            xp, rows, sizes, *device_cells(xp, device, groups_y, cells_x, cells_y)
        )
        both = xp.concatenate([xp.cos(theta), xp.sin(theta)], 1)
        parts.append(xp.stack(split16(xp.where(real, both, np.float32(0)))))
    return xp.stack(parts)


def inverse_table(xp, me, rows, sizes, cells_x, cells_y):
    theta, real = mode_angles(
        xp, rows, sizes, *device_cells(xp, me, sizes[1], cells_x, cells_y)
    )
    cosine = xp.where(real, xp.cos(theta), np.float32(0))
    sine = xp.where(real, xp.sin(theta), np.float32(0))
    return xp.concatenate([cosine.T, sine.T], 0).astype(BF16)


def quad_offset(t, groups_y):
    return t // 2 * groups_y + t % 2


def quad_of(r, groups_y):
    return r // groups_y % 2 * 2 + r % groups_y % 2


def z_angles(length):
    return angles(np, np.arange(MZ, dtype=np.int32), 2 * MZ, np.arange(length, dtype=np.int32), length)


def forward_z_table(length, block, kz_pad):
    theta = z_angles(length)
    parts = np.stack([np.cos(theta), -np.sin(theta)], 1)
    table = np.zeros((block, kz_pad, 2, block, length), np.float32)
    for c in range(block):
        table[c, :MZ, :, c] = parts
    return table.reshape(block, kz_pad * 2 * block, length).astype(BF16)


def inverse_z_table(length, per_tile, slot, norm):
    theta = z_angles(length)
    parts = np.stack([np.cos(theta), -np.sin(theta)], 0) * np.float32(norm)
    table = np.zeros((per_tile, 2, slot, per_tile, length), np.float32)
    for c in range(per_tile):
        table[c, :, :MZ, c] = parts
    high, low = split16(table.reshape(LANES, per_tile * length))
    return np.concatenate([high, low], 0)


def order_table(channels, kz_pad, per_tile, slot):
    table = np.zeros((kz_pad, 2, channels, channels // per_tile, per_tile, 2, slot), np.float32)
    for kz in range(MZ):
        for part in range(2):
            for c in range(channels):
                table[kz, part, c, c // per_tile, c % per_tile, part, kz] = 1
    return table.reshape(kz_pad * 2 * channels, -1).astype(BF16)


def spread_table(channels, half, copies):
    table = np.zeros((half, 2, channels, half, 2, copies.shape[0]), np.float32)
    for h in range(half):
        for part in range(2):
            table[h, part, copies, h, part, np.arange(copies.shape[0])] = 1
    return table.reshape(half * 2 * channels, -1).astype(BF16)


def gather_table(channels, copies):
    table = np.zeros((channels, channels, copies, channels), np.float32)
    for i in range(channels):
        table[i, :, :, i] = 1
    return table.reshape(channels * channels, -1).astype(BF16)


def cell_tables(channels, per_tile, cells_y):
    rows = np.zeros((per_tile, channels // per_tile, cells_y, channels), np.float32)
    for c in range(channels):
        rows[c % per_tile, c // per_tile, :, c] = 1
    columns = np.repeat(np.eye(channels, dtype=np.float32), cells_y, 1)
    return rows.reshape(-1, channels).astype(BF16), columns.astype(BF16)


def full(shape):
    return pl.BlockSpec(shape, lambda *_: (0,) * len(shape))


def params(mib):
    return pltpu.CompilerParams(vmem_limit_bytes=mib * 1024 * 1024)


def along_z_kernel(count, block, kz_pad, channels, info_ref, *refs):
    fields, z_ref = refs[:count], refs[count]
    outs, held = refs[count + 1 : count + 5], refs[count + 5]
    step = pl.program_id(0)
    for w, x_ref in enumerate(fields):
        total = None
        for c in range(block):
            term = lax.dot_general(z_ref[c], x_ref[c], NT, preferred_element_type=jnp.float32)
            total = term if total is None else total + term
        for k in range(2 * kz_pad):
            here = pl.multiple_of(k * channels + step * block, 8)
            held[w, pl.ds(here, block)] = total[k * block : (k + 1) * block]

    @pl.when(step == pl.num_programs(0) - 1)
    def _():
        for t in range(4):
            span = outs[t].shape[1]
            here = pl.multiple_of(jnp.bitwise_xor(info_ref[1], t) * span, 16)
            for w in range(count):
                outs[t][w] = held[w, pl.ds(here, span)].astype(jnp.bfloat16)


def along_z(info, fields, z_table, kz_pad, block):
    channels, cells, length = fields[0].shape
    count = len(fields)
    span = kz_pad * 2 * channels // 4
    chunk = jax.ShapeDtypeStruct((count, span, cells), jnp.bfloat16)
    return pl.pallas_call(
        functools.partial(along_z_kernel, count, block, kz_pad, channels),
        out_shape=[chunk] * 4,
        grid_spec=pltpu.PrefetchScalarGridSpec(
            num_scalar_prefetch=1,
            grid=(channels // block,),
            in_specs=[pl.BlockSpec((block, cells, length), lambda i, info: (i, 0, 0))] * count
            + [full(z_table.shape)],
            out_specs=[full(chunk.shape)] * 4,
            scratch_shapes=[pltpu.VMEM((count, kz_pad * 2 * channels, cells), jnp.float32)],
        ),
        compiler_params=params(12 * count),
        cost_estimate=pl.CostEstimate(
            flops=4 * count * cells * length * kz_pad * channels * block,
            bytes_accessed=2 * count * fields[0].size,
            transcendentals=0,
        ),
        name="along_z",
    )(info, *fields, z_table)


def plane_kernel(groups, rows, channels, info_ref, t_ref, *refs):
    sources, outs, (data, sums) = refs[:4], refs[4 : 4 + groups], refs[4 + groups :]
    count, span, cells = sources[0].shape
    step = pl.program_id(0)

    @pl.when(step == 0)
    def _():
        for t in range(4):
            place = jnp.bitwise_xor(info_ref[1], t)
            for w in range(count):
                value = sources[t][w]
                turned = []
                for k in range(0, span, 2 * channels):
                    turned += [value[k + channels : k + 2 * channels], -value[k : k + channels]]
                data[place, w * span : (w + 1) * span, :cells] = value
                data[place, w * span : (w + 1) * span, cells:] = jnp.concatenate(turned, 0)

    here = data[step]
    term = lax.dot_general(t_ref[0, 0, 0], here, NT, preferred_element_type=jnp.float32)
    term += lax.dot_general(t_ref[0, 0, 1], here, NT, preferred_element_type=jnp.float32)

    @pl.when(step == 0)
    def _():
        sums[...] = term

    @pl.when(step > 0)
    def _():
        sums[...] += term

    @pl.when(step == pl.num_programs(0) - 1)
    def _():
        for r in range(groups):
            own = pl.ds(pl.multiple_of(jnp.bitwise_xor(info_ref[0], r) * rows, 8), rows)
            for w in range(count):
                for j in range(span // LANES):
                    lane = w * span + j * LANES
                    outs[r][w, j] = sums[own, lane : lane + LANES].astype(jnp.bfloat16)


def plane(info, sources, table, groups, rows, channels):
    count, span, cells = sources[0].shape
    chunk = jax.ShapeDtypeStruct((count, span // LANES, rows, LANES), jnp.bfloat16)
    return pl.pallas_call(
        functools.partial(plane_kernel, groups, rows, channels),
        out_shape=[chunk] * groups,
        grid_spec=pltpu.PrefetchScalarGridSpec(
            num_scalar_prefetch=1,
            grid=(4,),
            in_specs=[
                pl.BlockSpec((1, 1) + table.shape[2:], lambda i, info: (info[2], i, 0, 0, 0))
            ]
            + [full(s.shape) for s in sources],
            out_specs=[full(chunk.shape)] * groups,
            scratch_shapes=[
                pltpu.VMEM((4, count * span, 2 * cells), jnp.bfloat16),
                pltpu.VMEM((groups * rows, count * span), jnp.float32),
            ],
        ),
        compiler_params=params(14 * count),
        cost_estimate=pl.CostEstimate(
            flops=32 * cells * count * span * groups * rows,
            bytes_accessed=2 * table[0].size,
            transcendentals=0,
        ),
        name="plane",
    )(info, table, *sources)


def add_sources(chunks, w, tile, mine, groups_y, held):
    per_quad = chunks[0].shape[1]
    for t in range(4):

        @pl.when(tile // per_quad == jnp.bitwise_xor(mine, t))
        def _(t=t):
            refs = [c for r, c in enumerate(chunks) if quad_of(r, groups_y) == t]
            total = refs[0][w, tile % per_quad].astype(jnp.float32)
            for ref in refs[1:]:
                total = total + ref[w, tile % per_quad].astype(jnp.float32)
            held[...] = total


def total_kernel(groups, groups_y, w, info_ref, *refs):
    scale_ref, out_ref, held = refs[groups:]
    add_sources(refs[:groups], w, pl.program_id(0), info_ref[1], groups_y, held)
    out_ref[0] = (held[...] * scale_ref[0]).astype(jnp.bfloat16)


def total(info, chunks, w, scale, groups_y):
    _, _, rows, _ = chunks[0].shape
    tiles = scale.shape[0]
    return pl.pallas_call(
        functools.partial(total_kernel, len(chunks), groups_y, w),
        out_shape=jax.ShapeDtypeStruct((tiles, rows, LANES), jnp.bfloat16),
        grid_spec=pltpu.PrefetchScalarGridSpec(
            num_scalar_prefetch=1,
            grid=(tiles,),
            in_specs=[full(c.shape) for c in chunks]
            + [pl.BlockSpec((1, 1, LANES), lambda i, info: (i, 0, 0))],
            out_specs=pl.BlockSpec((1, rows, LANES), lambda i, info: (i, 0, 0)),
            scratch_shapes=[pltpu.VMEM((rows, LANES), jnp.float32)],
        ),
        compiler_params=params(8),
        name="total",
    )(info, *chunks, scale)


def mix_kernel(groups, groups_y, w, info_ref, *refs):
    scale_ref, low_ref, high_ref, spread_ref, gather_ref, sum_ref, out_ref, held = refs[groups:]
    add_sources(refs[:groups], w, pl.program_id(0), info_ref[1], groups_y, held)
    values = (held[...] * scale_ref[0]).astype(jnp.bfloat16)
    sum_ref[0] = values
    rows = values.shape[0]
    wide = jnp.dot(values, spread_ref[...], preferred_element_type=jnp.float32)
    products = []
    for h, w_ref in enumerate((low_ref, high_ref)):
        out_re = wide[:, (2 * h) * LANES : (2 * h + 1) * LANES]
        out_im = wide[:, (2 * h + 1) * LANES : (2 * h + 2) * LANES]
        real, imag = [], []
        for k in range(w_ref.shape[3] // LANES):
            lane = slice(k * LANES, (k + 1) * LANES)
            w_re = w_ref[0, 0, :, lane].astype(jnp.float32)
            w_im = w_ref[0, 1, :, lane].astype(jnp.float32)
            real.append(w_re * out_re + w_im * out_im)
            imag.append(w_re * out_im - w_im * out_re)
        products += [jnp.concatenate(real, 1), jnp.concatenate(imag, 1)]
    sums = jnp.dot(
        jnp.concatenate(products, 0).astype(jnp.bfloat16),
        gather_ref[...],
        preferred_element_type=jnp.float32,
    )
    count = len(products)
    which = lax.broadcasted_iota(jnp.int32, (rows, LANES), 1) // (LANES // count)
    out = sums[:rows]
    for k in range(1, count):
        out = jnp.where(which == k, sums[k * rows : (k + 1) * rows], out)
    out_ref[0] = out.astype(jnp.bfloat16)


def mix(info, chunks, w, scale, weight, spread, gather, groups_y):
    _, _, rows, _ = chunks[0].shape
    tiles = scale.shape[0]
    last = weight.shape[0] - 1
    w_block = (1,) + weight.shape[1:]
    tile = pl.BlockSpec((1, rows, LANES), lambda i, info: (i, 0, 0))
    shape = jax.ShapeDtypeStruct((tiles, rows, LANES), jnp.bfloat16)
    return pl.pallas_call(
        functools.partial(mix_kernel, len(chunks), groups_y, w),
        out_shape=[shape, shape],
        grid_spec=pltpu.PrefetchScalarGridSpec(
            num_scalar_prefetch=1,
            grid=(tiles,),
            in_specs=[full(c.shape) for c in chunks]
            + [
                pl.BlockSpec((1, 1, LANES), lambda i, info: (i, 0, 0)),
                pl.BlockSpec(w_block, lambda i, info: (2 * i, 0, 0, 0)),
                pl.BlockSpec(w_block, lambda i, info: (jnp.minimum(2 * i + 1, last), 0, 0, 0)),
                full(spread.shape),
                full(gather.shape),
            ],
            out_specs=[tile, tile],
            scratch_shapes=[pltpu.VMEM((rows, LANES), jnp.float32)],
        ),
        compiler_params=params(16),
        cost_estimate=pl.CostEstimate(
            flops=8 * tiles * rows * gather.size, bytes_accessed=2 * weight.size, transcendentals=0
        ),
        name="mix",
    )(info, *chunks, scale, weight, weight, spread, gather)


def outer_kernel(scenes, info_ref, *refs):
    spectra, (spread_ref, pick_ref, out_ref) = refs[:scenes], refs[scenes:]
    rows, wide = out_ref.shape[2:]
    fields = jnp.dot(
        jnp.concatenate([ref[0, 0] for ref in spectra], 0),
        pick_ref[0],
        preferred_element_type=jnp.float32,
    )
    grads = jnp.dot(
        jnp.concatenate([ref[1, 0] for ref in spectra], 0),
        spread_ref[...],
        preferred_element_type=jnp.float32,
    )
    for h in range(out_ref.shape[0]):
        for k in range(wide // LANES):
            real, imag = 0.0, 0.0
            for s in range(scenes):
                here = slice(s * rows, (s + 1) * rows)
                lane = 2 * h * wide + k * LANES
                hat_re = fields[here, lane : lane + LANES]
                hat_im = fields[here, lane + wide : lane + wide + LANES]
                out_re = grads[here, 2 * h * LANES : (2 * h + 1) * LANES]
                out_im = grads[here, (2 * h + 1) * LANES : (2 * h + 2) * LANES]
                real += out_re * hat_re + out_im * hat_im
                imag += out_im * hat_re - out_re * hat_im
            out_ref[h, 0, :, k * LANES : (k + 1) * LANES] = real
            out_ref[h, 1, :, k * LANES : (k + 1) * LANES] = imag


def outer(info, spectra, spread, pick):
    _, tiles, rows, _ = spectra[0].shape
    wide = pick.shape[2] // 4
    block = pl.BlockSpec((2, 1, rows, LANES), lambda i, info: (0, i, 0, 0))
    return pl.pallas_call(
        functools.partial(outer_kernel, len(spectra)),
        out_shape=jax.ShapeDtypeStruct((2 * tiles, 2, rows, wide), jnp.float32),
        grid_spec=pltpu.PrefetchScalarGridSpec(
            num_scalar_prefetch=1,
            grid=(tiles,),
            in_specs=[block] * len(spectra)
            + [
                full(spread.shape),
                pl.BlockSpec((1,) + pick.shape[1:], lambda i, info: (info[4], 0, 0)),
            ],
            out_specs=pl.BlockSpec((2, 2, rows, wide), lambda i, info: (i, 0, 0, 0)),
        ),
        compiler_params=params(16),
        cost_estimate=pl.CostEstimate(
            flops=2 * tiles * rows * 4 * LANES * 12 * LANES,
            bytes_accessed=16 * tiles * rows * wide + 8 * tiles * rows * LANES * len(spectra),
            transcendentals=0,
        ),
        name="outer",
    )(info, *spectra, spread, pick)


def inverse_kernel(groups, per_tile, info_ref, *refs):
    chunks = refs[:groups]
    t_ref, order_ref, z_ref, point_ref, row_ref, column_ref, grad_ref = refs[groups : groups + 7]
    out_ref, modes, held, mixing = refs[groups + 7 :]
    channels, here, cells_y, length = grad_ref.shape
    rows = chunks[0].shape[1]
    step = pl.program_id(0)
    tiles = channels // per_tile

    @pl.when(step == 0)
    def _():
        picked = lax.dot_general(row_ref[...], point_ref[...], NT, preferred_element_type=jnp.float32)
        spread = jnp.dot(
            picked.astype(jnp.bfloat16), column_ref[...], preferred_element_type=jnp.float32
        )
        row = lax.broadcasted_iota(jnp.int32, spread.shape, 0) % cells_y
        column = lax.broadcasted_iota(jnp.int32, spread.shape, 1) % cells_y
        mixing[...] = jnp.where(row == column, spread, 0.0).astype(jnp.bfloat16)

        for r in range(groups):
            own = pl.ds(pl.multiple_of(jnp.bitwise_xor(info_ref[0], r) * rows, 8), rows)
            for j in range(chunks[r].shape[0]):
                modes[own, j * LANES : (j + 1) * LANES] = chunks[r][j].astype(jnp.float32)
        sums = jnp.dot(
            t_ref[0], modes[...].astype(jnp.bfloat16), preferred_element_type=jnp.float32
        )
        cells = sums.shape[0] // 2
        cosine, sine = sums[:cells], sums[cells:]
        wide = sine.shape[1]
        lane = lax.broadcasted_iota(jnp.int32, sine.shape, 1)
        first = lane % (2 * channels) < channels
        turned = jnp.where(
            first, -pltpu.roll(sine, wide - channels, 1), pltpu.roll(sine, channels, 1)
        )
        back = (cosine + turned).astype(jnp.bfloat16)
        ordered = jnp.dot(back, order_ref[...], preferred_element_type=jnp.float32)
        held[...] = ordered.astype(jnp.bfloat16).reshape(held.shape)

    span = tiles * cells_y
    rows = []
    for x in range(here):
        back = held[step * here + x]
        rows += [back[:, k * LANES : (k + 1) * LANES] for k in range(tiles)]
    rows = jnp.concatenate(rows, 0)
    spectral = jnp.dot(
        jnp.concatenate([rows, rows], 1), z_ref[...], preferred_element_type=jnp.float32
    )
    for x in range(here):
        local = jnp.dot(
            mixing[...],
            grad_ref[:, x].reshape(channels * cells_y, length),
            preferred_element_type=jnp.float32,
        )
        for j in range(per_tile):
            both = (
                spectral[x * span : (x + 1) * span, j * length : (j + 1) * length]
                + local[j * span : (j + 1) * span]
            ).astype(jnp.bfloat16)
            for k in range(tiles):
                out_ref[k * per_tile + j, x] = both[k * cells_y : (k + 1) * cells_y]


def inverse(info, chunks, table, order, z_table, point, cell_rows, cell_columns, grad, per_tile, here):
    channels, cells_x, cells_y, length = grad.shape
    block = pl.BlockSpec((channels, here, cells_y, length), lambda i, info: (0, i, 0, 0))
    consts = (order, z_table, point, cell_rows, cell_columns)
    return pl.pallas_call(
        functools.partial(inverse_kernel, len(chunks), per_tile),
        out_shape=jax.ShapeDtypeStruct(grad.shape, jnp.bfloat16),
        grid_spec=pltpu.PrefetchScalarGridSpec(
            num_scalar_prefetch=1,
            grid=(cells_x // here,),
            in_specs=[full(c.shape) for c in chunks]
            + [pl.BlockSpec((1,) + table.shape[1:], lambda i, info: (info[3], 0, 0))]
            + [full(c.shape) for c in consts]
            + [block],
            out_specs=block,
            scratch_shapes=[
                pltpu.VMEM((table.shape[2], order.shape[0]), jnp.float32),
                pltpu.VMEM((cells_x, cells_y, order.shape[1]), jnp.bfloat16),
                pltpu.VMEM((channels * cells_y, channels * cells_y), jnp.bfloat16),
            ],
        ),
        compiler_params=params(32),
        cost_estimate=pl.CostEstimate(
            flops=2 * grad.size * channels * cells_y, bytes_accessed=4 * grad.size, transcendentals=0
        ),
        name="inverse",
    )(info, *chunks, table, *consts, grad)


def flip(value, axes, size, r):
    return lax.ppermute(value, axes, [(i, i ^ r) for i in range(size)])


def body(field_in, grad_pre, spec_weight, point_weight):
    _, channels, cells_x, cells_y, cells_z = field_in.shape
    groups_x, groups_y = lax.axis_size("gx"), lax.axis_size("gy")
    groups, scenes = groups_x * groups_y, lax.axis_size("scene")
    group_axes = ("gx", "gy")
    total_x, total_y = cells_x * groups_x, cells_y * groups_y
    cells = cells_x * cells_y
    norm = float(total_x * total_y * cells_z) ** -0.5
    modes_xd, modes_yd = spec_weight.shape[:2]
    modes = modes_xd * modes_yd
    rows = -(-modes // 8) * 8
    half = LANES // (2 * channels)
    tiles = -(-MZ // half)
    per_quad = -(-tiles // 4)
    kz_pad = 4 * per_quad * half
    block = 8
    slot = 16
    per_tile = LANES // (2 * slot)
    sizes = (groups, groups_y, modes_xd, modes_yd, total_x, total_y)

    me = lax.axis_index(group_axes)
    at_x, at_y = lax.axis_index("gx"), lax.axis_index("gy")
    quad = at_x % 2 * 2 + at_y % 2
    first = at_x // 2 * 2 * groups_y + at_y // 2 * 2
    firsts = [
        x * groups_y + y for x in range(0, groups_x, 2) for y in range(0, groups_y, 2)
    ]
    if len(firsts) * groups * rows * cells * 32 <= 1 << 25:
        forward_t = jnp.asarray(
            np.stack([forward_table(np, f, rows, sizes, cells_x, cells_y) for f in firsts])
        )
        inverse_t = jnp.asarray(
            np.stack([inverse_table(np, i, rows, sizes, cells_x, cells_y) for i in range(groups)])
        )
        forward_at, inverse_at = at_x // 2 * (groups_y // 2) + at_y // 2, me
    else:
        forward_t = forward_table(jnp, first, rows, sizes, cells_x, cells_y)[None]
        inverse_t = inverse_table(jnp, me, rows, sizes, cells_x, cells_y)[None]
        forward_at, inverse_at = 0 * me, 0 * me
    info = jnp.stack([me, quad, forward_at, inverse_at, lax.axis_index("scene")])

    z_table = jnp.asarray(forward_z_table(cells_z, block, kz_pad))
    inverse_z = jnp.asarray(inverse_z_table(cells_z, per_tile, slot, norm))
    order = jnp.asarray(order_table(channels, tiles * half, per_tile, slot))
    lane = np.arange(LANES)
    spread = jnp.asarray(spread_table(channels, half, lane % channels))
    gather = jnp.asarray(gather_table(channels, LANES // channels))
    here = channels // scenes
    pair = np.arange(here * channels)
    pick = jnp.asarray(
        np.stack([spread_table(channels, half, q * here + pair // channels) for q in range(scenes)])
    )
    cell_rows, cell_columns = (jnp.asarray(t) for t in cell_tables(channels, per_tile, cells_y))
    weight_z = np.full((tiles * half, 2 * channels), 2.0 * norm, np.float32)
    weight_z[0] = norm
    grad_scale = jnp.asarray(weight_z.reshape(tiles, 1, LANES))
    field_scale = jnp.full((tiles, 1, LANES), norm, jnp.float32)

    def spectra_of(fields):
        mine = along_z(info, fields, z_table, kz_pad, block)
        cells_of = [mine[0]] + [
            flip(mine[t], group_axes, groups, quad_offset(t, groups_y)) for t in range(1, 4)
        ]
        sums = plane(info, cells_of, forward_t, groups, rows, channels)
        return [sums[0]] + [flip(sums[r], group_axes, groups, r) for r in range(1, groups)]

    grad = grad_pre.reshape(channels, cells, cells_z)
    field = field_in.reshape(channels, cells, cells_z)
    if SPLIT:
        grad_got, field_got, at = spectra_of([grad]), spectra_of([field]), 0
    else:
        grad_got = spectra_of([grad, field])
        field_got, at = grad_got, 1
    weight = spec_weight.reshape(modes, MZ, 2, channels * channels)
    weight = jnp.pad(weight.transpose(1, 2, 0, 3), ((0, 0), (0, 0), (0, rows - modes), (0, 0)))
    grad_sum, mode_grad = mix(
        info, grad_got, 0, grad_scale, weight, spread, gather, groups_y
    )

    gathered = [mode_grad] + [flip(mode_grad, "gy", groups_y, r) for r in range(1, groups_y)]
    for r in range(1, groups_x):
        gathered += [flip(m, "gx", groups_x, r) for m in gathered[:groups_y]]

    field_sum = total(info, field_got, at, field_scale, groups_y)
    both = jnp.stack([field_sum, grad_sum])
    spectra = [both] + [flip(both, "scene", scenes, r) for r in range(1, scenes)]
    grads = outer(info, spectra, spread, pick)
    grad_spec = grads[:MZ, :, :modes].transpose(2, 0, 1, 3)
    grad_spec = grad_spec.reshape(modes_xd, modes_yd, MZ, 2, here * channels)

    grad_field = inverse(
        info,
        gathered,
        inverse_t,
        order,
        inverse_z,
        point_weight,
        cell_rows,
        cell_columns,
        grad_pre.reshape(channels, cells_x, cells_y, cells_z),
        per_tile,
        2,
    )
    return grad_field[None], grad_spec


def solution(mesh):
    return jax.shard_map(
        body,
        mesh=mesh,
        in_specs=(
            P("scene", None, "gx", "gy", None),
            P("scene", None, "gx", "gy", None),
            P("gx", "gy", None, None, None),
            P(),
        ),
        out_specs=(P("scene", None, "gx", "gy", None), P("gx", "gy", None, None, "scene")),
        check_vma=False,
    )
```

time: 369 us -> 87.6 us (0.24); the launches traced: 364 us -> 87.3 us
  local copies, waits for them, and re-layouts: 104 us -> 9.39 us
  matrix products: 93.8 us -> 0 us
  waiting for transfers between devices: 84.7 us -> 22.9 us
  blocking collectives: 37.2 us -> 0 us
  other arithmetic: 28.9 us -> 0.03 us
  starting transfers between devices: 0.34 us -> 27.6 us
  Pallas kernels: 0 us -> 26.5 us
  between operations: 14.6 us -> 0.92 us
    dot_general x10 -> x0, matrix products: 93.8 us -> none  [the longest x1 23.3 us: body(): jnp.einsum('abkio,absok->absik', weight_im, out_im, precision=highest)]
    unnamed x3 -> x0, waiting for transfers between devices: 84.7 us -> none
    another operation x14 -> x1, local copies, waits for them, and re-layouts: 47.6 us -> 0.08 us  [body(): jnp.stack([me, quad, forward_at, inverse_at, lax.axis_index('scene')])]
    all_gather x1 -> x0, blocking collectives: 37.2 us -> none  [body(): gathered = lax.all_gather(mode_flat, ('gx', 'gy'), axis=0, tiled=True)]
    ppermute x0 -> x20, starting transfers between devices: none -> 27.6 us  [flip(): return lax.ppermute(value, axes, [(i, i ^ r) for i in range(size)])]
    pallas_call x0 -> x6, Pallas kernels: none -> 26.5 us  [the longest x1 8.86 us: inverse(): pl.pallas_call(functools.partial(inverse_kernel, len(chunks), per_tile),...]
    reshape x4 -> x1, local copies, waits for them, and re-layouts: 27.6 us -> 1.26 us  [body(): weight = spec_weight.reshape(modes, MZ, 2, channels * channels)]
    ppermute x0 -> x20, waiting for transfers between devices: none -> 22.9 us  [flip(): return lax.ppermute(value, axes, [(i, i ^ r) for i in range(size)])]
  transfers between devices with their start and end apart: 2 -> 20, of which waited for: 1 -> 8; matrix products, arithmetic and copies ran while one was open for 32% -> 1% of each run, Pallas kernels for 0% -> 11%
where the time goes in v1:
time: 87.6 us; the launch traced here: 87.3 us
  starting transfers between devices  27.6 us (32%)
  Pallas kernels  26.5 us (30%)
  waiting for transfers between devices  22.9 us (26%)
  local copies, waits for them, and re-layouts  9.39 us (11%)
  between operations  0.92 us (1%)
    ppermute x20, starting transfers between devices, flip(): return lax.ppermute(value, axes, [(i, i ^ r) for i in range(size)])  27.6 us
    ppermute x20, waiting for transfers between devices, flip(): return lax.ppermute(value, axes, [(i, i ^ r) for i in range(size)])  22.9 us
    pallas_call x1, Pallas kernels, inverse(): pl.pallas_call(functools.partial(inverse_kernel, len(chunks), per_tile),...  8.86 us
    unnamed x34, local copies, waits for them, and re-layouts  5.68 us
    pallas_call x1, Pallas kernels, plane(): pl.pallas_call(functools.partial(plane_kernel, groups, rows, channels), o...  4.44 us
    pallas_call x1, Pallas kernels, mix(): pl.pallas_call(functools.partial(mix_kernel, len(chunks), groups_y, w), o...  4.4 us
    pallas_call x1, Pallas kernels, outer(): pl.pallas_call(functools.partial(outer_kernel, len(spectra)), out_shape=j...  4.11 us
    pallas_call x1, Pallas kernels, along_z(): pl.pallas_call(functools.partial(along_z_kernel, count, block, kz_pad, ch...  3.74 us
  transfers between devices with their start and end apart: 20, of which 8 were waited for; matrix products, arithmetic and copies ran while one was open for 1% of the time, Pallas kernels for 11%

profile of v1, /device:TPU:0, one launch (start us, length us, event | category | flops | bytes accessed | tf_op | source)
XLA Modules:
  0.0 87.3 jit_solution(77019025842457652)
XLA Ops:
  0.7 0.1 stack.29.info_ref
  0.8 2.2 %copy-done = bf16[1,32,16,16,256]{4,3,2,1,0:T(8,128)(2,1)S(1)} copy-done((bf16[1,32,16,16,256]{4,3,2,1,0:T(8,128)(2,1)S(1)}, bf16[1,32,16,16,256]{4,3,2,1,0:T(8,128)(2,1)}, u32[]{:S(2)}) %copy-start) | copy-done | bytes 4194328
  2.9 2.2 %copy-done.3 = bf16[1,32,16,16,256]{4,3,2,1,0:T(8,128)(2,1)S(1)} copy-done((bf16[1,32,16,16,256]{4,3,2,1,0:T(8,128)(2,1)S(1)}, bf16[1,32,16,16,256]{4,3,2,1,0:T(8,128)(2,1)}, u32[]{:S(2)}) %copy-start.3) | copy-done | bytes 4194328
  5.1 1.2 %copy-done.6 = bf16[8,256,256]{2,1,0:T(8,128)(2,1)S(1)} copy-done((bf16[8,256,256]{2,1,0:T(8,128)(2,1)S(1)}, bf16[8,256,256]{2,1,0:T(8,128)(2,1)}, u32[]{:S(2)}) %copy-start.6) | copy-done | bytes 1048600
  6.4 3.7 %along_z.1 = (bf16[2,256,256]{2,1,0:T(8,128)(2,1)S(1)}, bf16[2,256,256]{2,1,0:T(8,128)(2,1)S(1)}, bf16[2,256,256]{2,1,0:T(8,128)(2,1)S(1)}, bf16[2,256,256]{2,1,0:T(8,128)(2,1)S(1)}) custom-call(s32[5]{0:T(128)S(1)} %stack.29.info_ref, bf16[32,256,256]{2,1,0:T(8,128)(2,1)S(1)} %bitcast.19, bf16[32,256,256]{2,1,0:T(8,128)(2,1)S(1)} %bitcast.23, ...), custom_call_target="tpu_custom_call" | custom-call | flops 2147483648 | bytes 8388608 | tf_op jit(solution)/shard_map/along_z/pallas_call | solution.py:172
  10.1 3.1 %collective-permute-start = (bf16[2,256,256]{2,1,0:T(8,128)(2,1)S(1)}, bf16[2,256,256]{2,1,0:T(8,128)(2,1)S(1)}, u32[]{:S(2)}, u32[]{:S(2)}) collective-permute-start(bf16[2,256,256]{2,1,0:T(8,128)(2,1)S(1)} %get-tuple-element.17), channel_id=1, source_target_pairs={{0,4},{4,0},{8,12},{12,8},{16,20},{20,16},{24,28},{28,24},{1,5},{5... | collective-permute-start | bytes 786440 | tf_op jit(solution)/shard_map/ppermute | solution.py:511
  13.2 1.5 %collective-permute-start.1 = (bf16[2,256,256]{2,1,0:T(8,128)(2,1)S(1)}, bf16[2,256,256]{2,1,0:T(8,128)(2,1)S(1)}, u32[]{:S(2)}, u32[]{:S(2)}) collective-permute-start(bf16[2,256,256]{2,1,0:T(8,128)(2,1)S(1)} %get-tuple-element.18), channel_id=1, source_target_pairs={{0,16},{4,20},{8,24},{12,28},{16,0},{20,4},{24,8},{28,12},{1,17},{... | collective-permute-start | bytes 786440 | tf_op jit(solution)/shard_map/ppermute | solution.py:511
  14.7 0.1 collective-permute-start.2
  14.7 5.6 %collective-permute-done.refs_1_ = bf16[2,256,256]{2,1,0:T(8,128)(2,1)S(1)} collective-permute-done((bf16[2,256,256]{2,1,0:T(8,128)(2,1)S(1)}, bf16[2,256,256]{2,1,0:T(8,128)(2,1)S(1)}, u32[]{:S(2)}, u32[]{:S(2)}) %collective-permute-start) | collective-permute-done | bytes 262176 | tf_op jit(solution)/shard_map/ppermute | solution.py:511
  20.3 6.2 %collective-permute-done.1.refs_2_ = bf16[2,256,256]{2,1,0:T(8,128)(2,1)S(1)} collective-permute-done((bf16[2,256,256]{2,1,0:T(8,128)(2,1)S(1)}, bf16[2,256,256]{2,1,0:T(8,128)(2,1)S(1)}, u32[]{:S(2)}, u32[]{:S(2)}) %collective-permute-start.1) | collective-permute-done | bytes 262176 | tf_op jit(solution)/shard_map/ppermute | solution.py:511
  26.6 0.0 slice-start
  26.6 4.4 %plane.1 = (bf16[2,2,72,128]{3,2,1,0:T(8,128)(2,1)S(1)}, bf16[2,2,72,128]{3,2,1,0:T(8,128)(2,1)S(1)}, bf16[2,2,72,128]{3,2,1,0:T(8,128)(2,1)S(1)}, bf16[2,2,72,1...) custom-call(s32[5]{0:T(128)S(1)} %stack.29.info_ref, ...), custom_call_target="tpu_custom_call" | custom-call | flops 2415919104 | bytes 4718592 | tf_op jit(solution)/shard_map/plane/pallas_call | solution.py:235
  31.0 1.3 %collective-permute-start.3 = (bf16[2,2,72,128]{3,2,1,0:T(8,128)(2,1)S(1)}, bf16[2,2,72,128]{3,2,1,0:T(8,128)(2,1)S(1)}, u32[]{:S(2)}, u32[]{:S(2)}) collective-permute-start(bf16[2,2,72,128]{3,2,1,0:T(8,128)(2,1)S(1)} %get-tuple-element.21), channel_id=1, source_target_pairs={{0,4},{4,0},{8,12},{12,8},{16,20},{20,16},{24,28},{28,24},{1,5},{5... | collective-permute-start | bytes 221192 | tf_op jit(solution)/shard_map/ppermute | solution.py:511
  32.3 2.6 %collective-permute-start.4 = (bf16[2,2,72,128]{3,2,1,0:T(8,128)(2,1)S(1)}, bf16[2,2,72,128]{3,2,1,0:T(8,128)(2,1)S(1)}, u32[]{:S(2)}, u32[]{:S(2)}) collective-permute-start(bf16[2,2,72,128]{3,2,1,0:T(8,128)(2,1)S(1)} %get-tuple-element.22), channel_id=1, source_target_pairs={{0,8},{4,12},{8,0},{12,4},{16,24},{20,28},{24,16},{28,20},{1,9},{5... | collective-permute-start | bytes 221192 | tf_op jit(solution)/shard_map/ppermute | solution.py:511
  34.9 0.6 collective-permute-start.5
  35.5 1.5 %collective-permute-start.6 = (bf16[2,2,72,128]{3,2,1,0:T(8,128)(2,1)S(1)}, bf16[2,2,72,128]{3,2,1,0:T(8,128)(2,1)S(1)}, u32[]{:S(2)}, u32[]{:S(2)}) collective-permute-start(bf16[2,2,72,128]{3,2,1,0:T(8,128)(2,1)S(1)} %get-tuple-element.24), channel_id=1, source_target_pairs={{0,16},{4,20},{8,24},{12,28},{16,0},{20,4},{24,8},{28,12},{1,17},{... | collective-permute-start | bytes 221192 | tf_op jit(solution)/shard_map/ppermute | solution.py:511
  37.0 0.3 collective-permute-start.7
  37.3 3.7 %collective-permute-start.8 = (bf16[2,2,72,128]{3,2,1,0:T(8,128)(2,1)S(1)}, bf16[2,2,72,128]{3,2,1,0:T(8,128)(2,1)S(1)}, u32[]{:S(2)}, u32[]{:S(2)}) collective-permute-start(bf16[2,2,72,128]{3,2,1,0:T(8,128)(2,1)S(1)} %get-tuple-element.26), channel_id=1, source_target_pairs={{0,24},{4,28},{8,16},{12,20},{16,8},{20,12},{24,0},{28,4},{1,25},{... | collective-permute-start | bytes 221192 | tf_op jit(solution)/shard_map/ppermute | solution.py:511
  40.9 2.1 %collective-permute-start.9 = (bf16[2,2,72,128]{3,2,1,0:T(8,128)(2,1)S(1)}, bf16[2,2,72,128]{3,2,1,0:T(8,128)(2,1)S(1)}, u32[]{:S(2)}, u32[]{:S(2)}) collective-permute-start(bf16[2,2,72,128]{3,2,1,0:T(8,128)(2,1)S(1)} %get-tuple-element.27), channel_id=1, source_target_pairs={{0,28},{4,24},{8,20},{12,16},{16,12},{20,8},{24,4},{28,0},{1,29},{... | collective-permute-start | bytes 221192 | tf_op jit(solution)/shard_map/ppermute | solution.py:511
  43.1 0.0 slice-start.1
  43.1 1.3 %copy.22 = bf16[72,13,2,1024]{3,0,2,1:T(8,128)(2,1)S(1)} copy(bf16[72,13,2,1024]{3,2,1,0:T(2,128)(2,1)S(1)} %bitcast.27) | data formatting | bytes 7667712 | tf_op jit(solution)/shard_map/reshape | solution.py:587
  44.4 1.9 %collective-permute-done.8.refs_6_ = bf16[2,2,72,128]{3,2,1,0:T(8,128)(2,1)S(1)} collective-permute-done((bf16[2,2,72,128]{3,2,1,0:T(8,128)(2,1)S(1)}, bf16[2,2,72,128]{3,2,1,0:T(8,128)(2,1)S(1)}, u32[]{:S(2)}, u32[]{:S(2)}) %collective-permute-start.8) | collective-permute-done | bytes 73760 | tf_op jit(solution)/shard_map/ppermute | solution.py:511
  46.3 1.7 %collective-permute-done.9.refs_7_ = bf16[2,2,72,128]{3,2,1,0:T(8,128)(2,1)S(1)} collective-permute-done((bf16[2,2,72,128]{3,2,1,0:T(8,128)(2,1)S(1)}, bf16[2,2,72,128]{3,2,1,0:T(8,128)(2,1)S(1)}, u32[]{:S(2)}, u32[]{:S(2)}) %collective-permute-start.9) | collective-permute-done | bytes 73760 | tf_op jit(solution)/shard_map/ppermute | solution.py:511
  48.0 0.0 copy-start.4
  48.0 0.0 copy-start.8
  48.0 0.0 copy-start.10
  48.1 0.0 copy-start.11
  48.1 0.0 copy-start.12
  48.1 4.4 %mix.1 = (bf16[7,72,128]{2,1,0:T(8,128)(2,1)S(1)}, bf16[7,72,128]{2,1,0:T(8,128)(2,1)S(1)}) custom-call(s32[5]{0:T(128)S(1)} %stack.29.info_ref, bf16[2,2,72,128]{3,2,1,0:T(8,128)(2,1)S(1)} %get-tuple-element.20.refs_0_, bf16[2,2,72,128]{3,2,1,0:T(8,128)(2,1)S(1)} %collective-permute-done.3.refs_1_, ...), custom_call_target="tpu_custom_call" | custom-call | flops 528482304 | bytes 3833856 | tf_op jit(solution)/shard_map/mix/pallas_call | solution.py:338
  52.5 1.9 %collective-permute-start.12 = (bf16[7,72,128]{2,1,0:T(8,128)(2,1)S(1)}, bf16[7,72,128]{2,1,0:T(8,128)(2,1)S(1)}, u32[]{:S(2)}, u32[]{:S(2)}) collective-permute-start(bf16[7,72,128]{2,1,0:T(8,128)(2,1)S(1)} %get-tuple-element.28.refs_0_), channel_id=1, source_target_pairs={{0,12},{4,8},{8,4},{12,0},{1,13},{5,9},{9,5},{13,1},{2,14},{6,10},... | collective-permute-start | bytes 387080 | tf_op jit(solution)/shard_map/ppermute | solution.py:511
  54.4 2.6 %collective-permute-start.10 = (bf16[7,72,128]{2,1,0:T(8,128)(2,1)S(1)}, bf16[7,72,128]{2,1,0:T(8,128)(2,1)S(1)}, u32[]{:S(2)}, u32[]{:S(2)}) collective-permute-start(bf16[7,72,128]{2,1,0:T(8,128)(2,1)S(1)} %get-tuple-element.28.refs_0_), channel_id=1, source_target_pairs={{0,4},{4,0},{8,12},{12,8},{1,5},{5,1},{9,13},{13,9},{2,6},{6,2},{1... | collective-permute-start | bytes 387080 | tf_op jit(solution)/shard_map/ppermute | solution.py:511
  56.9 1.3 %collective-permute-start.13 = (bf16[7,72,128]{2,1,0:T(8,128)(2,1)S(1)}, bf16[7,72,128]{2,1,0:T(8,128)(2,1)S(1)}, u32[]{:S(2)}, u32[]{:S(2)}) collective-permute-start(bf16[7,72,128]{2,1,0:T(8,128)(2,1)S(1)} %get-tuple-element.28.refs_0_), channel_id=1, source_target_pairs={{0,16},{16,0},{1,17},{17,1},{2,18},{18,2},{3,19},{19,3},{4,20},{20... | collective-permute-start | bytes 387080 | tf_op jit(solution)/shard_map/ppermute | solution.py:511
  58.2 1.3 %collective-permute-done.12.refs_3_ = bf16[7,72,128]{2,1,0:T(8,128)(2,1)S(1)} collective-permute-done((bf16[7,72,128]{2,1,0:T(8,128)(2,1)S(1)}, bf16[7,72,128]{2,1,0:T(8,128)(2,1)S(1)}, u32[]{:S(2)}, u32[]{:S(2)}) %collective-permute-start.12) | collective-permute-done | bytes 129056 | tf_op jit(solution)/shard_map/ppermute | solution.py:511
  59.5 1.3 %collective-permute-start.16 = (bf16[7,72,128]{2,1,0:T(8,128)(2,1)S(1)}, bf16[7,72,128]{2,1,0:T(8,128)(2,1)S(1)}, u32[]{:S(2)}, u32[]{:S(2)}) collective-permute-start(bf16[7,72,128]{2,1,0:T(8,128)(2,1)S(1)} %collective-permute-done.12.refs_3_), channel_id=1, source_target_pairs={{0,16},{16,0},{1,17},{17,1},{2,18},{18,2},{3,19},{19,3},{4,20},{20... | collective-permute-start | bytes 387080 | tf_op jit(solution)/shard_map/ppermute | solution.py:511
  60.8 0.9 %total.1 = bf16[7,72,128]{2,1,0:T(8,128)(2,1)S(1)} custom-call(s32[5]{0:T(128)S(1)} %stack.29.info_ref, bf16[2,2,72,128]{3,2,1,0:T(8,128)(2,1)S(1)} %get-tuple-element.20.refs_0_, bf16[2,2,72,128]{3,2,1,0:T(8,128)(2,1)S(1)} %collective-permute-done.3.refs_1_, bf16[2,2,72,128]{3,2,1,0:T(8,128)(2,1)S(1)} %collective-permute-done.4.refs_2_, ...), custom_call_target="tpu_custom_call" | custom-call | tf_op jit(solution)/shard_map/total/pallas_call | solution.py:283
  61.7 2.5 %collective-permute-done.11.refs_2_ = bf16[7,72,128]{2,1,0:T(8,128)(2,1)S(1)} collective-permute-done((bf16[7,72,128]{2,1,0:T(8,128)(2,1)S(1)}, bf16[7,72,128]{2,1,0:T(8,128)(2,1)S(1)}, u32[]{:S(2)}, u32[]{:S(2)}) %collective-permute-start.11) | collective-permute-done | bytes 129056 | tf_op jit(solution)/shard_map/ppermute | solution.py:511
  64.2 0.7 collective-permute-start.15
  64.9 1.3 %collective-permute-start.14 = (bf16[7,72,128]{2,1,0:T(8,128)(2,1)S(1)}, bf16[7,72,128]{2,1,0:T(8,128)(2,1)S(1)}, u32[]{:S(2)}, u32[]{:S(2)}) collective-permute-start(bf16[7,72,128]{2,1,0:T(8,128)(2,1)S(1)} %collective-permute-done.10.refs_1_), channel_id=1, source_target_pairs={{0,16},{16,0},{1,17},{17,1},{2,18},{18,2},{3,19},{19,3},{4,20},{20... | collective-permute-start | bytes 387080 | tf_op jit(solution)/shard_map/ppermute | solution.py:511
  66.2 0.2 collective-permute-start.19
  66.4 1.5 %collective-permute-start.18 = (bf16[2,7,72,128]{3,2,1,0:T(8,128)(2,1)S(1)}, bf16[2,7,72,128]{3,2,1,0:T(8,128)(2,1)S(1)}, u32[]{:S(2)}, u32[]{:S(2)}) collective-permute-start(bf16[2,7,72,128]{3,2,1,0:T(8,128)(2,1)S(1)} %pad_maximum_fusion.refs_0_), channel_id=1, source_target_pairs={{0,2},{1,3},{2,0},{3,1},{4,6},{5,7},{6,4},{7,5},{8,10},{9,11},{10,... | collective-permute-start | bytes 774152 | tf_op jit(solution)/shard_map/ppermute | solution.py:511
  67.9 0.3 collective-permute-start.17
  68.2 2.3 %collective-permute-done.15.refs_6_ = bf16[7,72,128]{2,1,0:T(8,128)(2,1)S(1)} collective-permute-done((bf16[7,72,128]{2,1,0:T(8,128)(2,1)S(1)}, bf16[7,72,128]{2,1,0:T(8,128)(2,1)S(1)}, u32[]{:S(2)}, u32[]{:S(2)}) %collective-permute-start.15) | collective-permute-done | bytes 129056 | tf_op jit(solution)/shard_map/ppermute | solution.py:511
  70.5 1.4 %collective-permute-done.14.refs_5_ = bf16[7,72,128]{2,1,0:T(8,128)(2,1)S(1)} collective-permute-done((bf16[7,72,128]{2,1,0:T(8,128)(2,1)S(1)}, bf16[7,72,128]{2,1,0:T(8,128)(2,1)S(1)}, u32[]{:S(2)}, u32[]{:S(2)}) %collective-permute-start.14) | collective-permute-done | bytes 129056 | tf_op jit(solution)/shard_map/ppermute | solution.py:511
  71.9 0.0 copy-start.5
  72.0 8.9 %inverse.1 = bf16[32,16,16,256]{3,2,1,0:T(8,128)(2,1)} custom-call(s32[5]{0:T(128)S(1)} %stack.29.info_ref, bf16[7,72,128]{2,1,0:T(8,128)(2,1)S(1)} %get-tuple-element.28.refs_0_, bf16[7,72,128]{2,1,0:T(8,128)(2,1)S(1)} %collective-permute-done.10.refs_1_, bf16[7,72,128]{2,1,0:T(8,128)(2,1)S(1)} %collective-permute-done.11.refs_2_, ...), custom_call_target="tpu_custom_call" | custom-call | flops 2147483648 | bytes 8388608 | tf_op jit(solution)/shard_map/inverse/pallas_call | solution.py:485
  80.8 4.1 %outer.1 = f32[14,2,72,256]{3,2,1,0:T(8,128)S(1)} custom-call(s32[5]{0:T(128)S(1)} %stack.29.info_ref, bf16[2,7,72,128]{3,2,1,0:T(8,128)(2,1)S(1)} %pad_maximum_fusion.refs_0_, bf16[2,7,72,128]{3,2,1,0:T(8,128)(2,1)S(1)} %collective-permute-done.17.refs_1_, bf16[2,7,72,128]{3,2,1,0:T(8,128)(2,1)S(1)} %collective-permute-done.18.refs_2_, ...), custom_call_target="tpu_custom_call" | custom-call | flops 792723456 | bytes 4128768 | tf_op jit(solution)/shard_map/outer/pallas_call | solution.py:396
  85.0 0.1 slice_bitcast_fusion
  85.1 2.2 %copy.20 = f32[72,13,2,256]{3,2,1,0:T(2,128)} copy(f32[72,13,2,256]{3,0,2,1:T(8,128)S(1)} %slice_bitcast_fusion) | data formatting | bytes 3833856 | tf_op jit(solution)/shard_map/transpose | solution.py:601
  (39 shorter events, 0.1 us)
Async XLA Ops:
  0.8 2.2 %copy-start = (bf16[1,32,16,16,256]{4,3,2,1,0:T(8,128)(2,1)S(1)}, bf16[1,32,16,16,256]{4,3,2,1,0:T(8,128)(2,1)}, u32[]{:S(2)}) copy-start(bf16[1,32,16,16,256]{4,3,2,1,0:T(8,128)(2,1)} %param.16) | copy-start | bytes 12582916
  2.9 2.2 %copy-start.3 = (bf16[1,32,16,16,256]{4,3,2,1,0:T(8,128)(2,1)S(1)}, bf16[1,32,16,16,256]{4,3,2,1,0:T(8,128)(2,1)}, u32[]{:S(2)}) copy-start(bf16[1,32,16,16,256]{4,3,2,1,0:T(8,128)(2,1)} %param.15) | copy-start | bytes 12582916
  5.1 1.2 %copy-start.6 = (bf16[8,256,256]{2,1,0:T(8,128)(2,1)S(1)}, bf16[8,256,256]{2,1,0:T(8,128)(2,1)}, u32[]{:S(2)}) copy-start(bf16[8,256,256]{2,1,0:T(8,128)(2,1)} %constant.77.clone.refs_2_) | copy-start | bytes 3145732
  6.4 20.2 %copy-start.2 = (bf16[2,4,2,576,512]{4,3,2,1,0:T(8,128)(2,1)S(1)}, bf16[2,4,2,576,512]{4,3,2,1,0:T(8,128)(2,1)}, u32[]{:S(2)}) copy-start(bf16[2,4,2,576,512]{4,3,2,1,0:T(8,128)(2,1)} %constant.75.clone.t_ref) | copy-start | bytes 28311556
  10.1 10.2 %collective-permute-start = (bf16[2,256,256]{2,1,0:T(8,128)(2,1)S(1)}, bf16[2,256,256]{2,1,0:T(8,128)(2,1)S(1)}, u32[]{:S(2)}, u32[]{:S(2)}) collective-permute-start(bf16[2,256,256]{2,1,0:T(8,128)(2,1)S(1)} %get-tuple-element.17), channel_id=1, source_target_pairs={{0,4},{4,0},{8,12},{12,8},{16,20},{20,16},{24,28},{28,24},{1,5},{5... | collective-permute-start | bytes 786440 | tf_op jit(solution)/shard_map/ppermute | solution.py:511
  13.2 13.4 %collective-permute-start.1 = (bf16[2,256,256]{2,1,0:T(8,128)(2,1)S(1)}, bf16[2,256,256]{2,1,0:T(8,128)(2,1)S(1)}, u32[]{:S(2)}, u32[]{:S(2)}) collective-permute-start(bf16[2,256,256]{2,1,0:T(8,128)(2,1)S(1)} %get-tuple-element.18), channel_id=1, source_target_pairs={{0,16},{4,20},{8,24},{12,28},{16,0},{20,4},{24,8},{28,12},{1,17},{... | collective-permute-start | bytes 786440 | tf_op jit(solution)/shard_map/ppermute | solution.py:511
  14.7 11.9 %collective-permute-start.2 = (bf16[2,256,256]{2,1,0:T(8,128)(2,1)S(1)}, bf16[2,256,256]{2,1,0:T(8,128)(2,1)S(1)}, u32[]{:S(2)}, u32[]{:S(2)}) collective-permute-start(bf16[2,256,256]{2,1,0:T(8,128)(2,1)S(1)} %get-tuple-element.19), channel_id=1, source_target_pairs={{0,20},{4,16},{8,28},{12,24},{16,4},{20,0},{24,12},{28,8},{1,21},{... | collective-permute-start | bytes 786440 | tf_op jit(solution)/shard_map/ppermute | solution.py:511
  26.6 16.5 %copy-start.14 = (bf16[12,6,13,2,1024]{4,3,2,1,0:T(2,128)(2,1)S(1)}, bf16[12,6,13,2,1024]{4,3,2,1,0:T(2,128)(2,1)}, u32[]{:S(2)}) copy-start(bf16[12,6,13,2,1024]{4,3,2,1,0:T(2,128)(2,1)} %param.17) | copy-start | bytes 11501572
  26.6 45.3 %slice-start = ((s8[5242880]{0:T(1024)(128)(4,1)}), s8[4194304]{0:T(1024)(128)(4,1)S(1)}, s32[]{:S(2)}) async-start(s8[5242880]{0:T(1024)(128)(4,1)} %bitcast.21), calls=%async_computation | async-start | bytes 8388608
  31.0 6.2 %collective-permute-start.3 = (bf16[2,2,72,128]{3,2,1,0:T(8,128)(2,1)S(1)}, bf16[2,2,72,128]{3,2,1,0:T(8,128)(2,1)S(1)}, u32[]{:S(2)}, u32[]{:S(2)}) collective-permute-start(bf16[2,2,72,128]{3,2,1,0:T(8,128)(2,1)S(1)} %get-tuple-element.21), channel_id=1, source_target_pairs={{0,4},{4,0},{8,12},{12,8},{16,20},{20,16},{24,28},{28,24},{1,5},{5... | collective-permute-start | bytes 221192 | tf_op jit(solution)/shard_map/ppermute | solution.py:511
  32.3 8.6 %collective-permute-start.4 = (bf16[2,2,72,128]{3,2,1,0:T(8,128)(2,1)S(1)}, bf16[2,2,72,128]{3,2,1,0:T(8,128)(2,1)S(1)}, u32[]{:S(2)}, u32[]{:S(2)}) collective-permute-start(bf16[2,2,72,128]{3,2,1,0:T(8,128)(2,1)S(1)} %get-tuple-element.22), channel_id=1, source_target_pairs={{0,8},{4,12},{8,0},{12,4},{16,24},{20,28},{24,16},{28,20},{1,9},{5... | collective-permute-start | bytes 221192 | tf_op jit(solution)/shard_map/ppermute | solution.py:511
  34.9 9.5 %collective-permute-start.5 = (bf16[2,2,72,128]{3,2,1,0:T(8,128)(2,1)S(1)}, bf16[2,2,72,128]{3,2,1,0:T(8,128)(2,1)S(1)}, u32[]{:S(2)}, u32[]{:S(2)}) collective-permute-start(bf16[2,2,72,128]{3,2,1,0:T(8,128)(2,1)S(1)} %get-tuple-element.23), channel_id=1, source_target_pairs={{0,12},{4,8},{8,4},{12,0},{16,28},{20,24},{24,20},{28,16},{1,13},{... | collective-permute-start | bytes 221192 | tf_op jit(solution)/shard_map/ppermute | solution.py:511
  35.5 8.9 %collective-permute-start.6 = (bf16[2,2,72,128]{3,2,1,0:T(8,128)(2,1)S(1)}, bf16[2,2,72,128]{3,2,1,0:T(8,128)(2,1)S(1)}, u32[]{:S(2)}, u32[]{:S(2)}) collective-permute-start(bf16[2,2,72,128]{3,2,1,0:T(8,128)(2,1)S(1)} %get-tuple-element.24), channel_id=1, source_target_pairs={{0,16},{4,20},{8,24},{12,28},{16,0},{20,4},{24,8},{28,12},{1,17},{... | collective-permute-start | bytes 221192 | tf_op jit(solution)/shard_map/ppermute | solution.py:511
  37.0 7.4 %collective-permute-start.7 = (bf16[2,2,72,128]{3,2,1,0:T(8,128)(2,1)S(1)}, bf16[2,2,72,128]{3,2,1,0:T(8,128)(2,1)S(1)}, u32[]{:S(2)}, u32[]{:S(2)}) collective-permute-start(bf16[2,2,72,128]{3,2,1,0:T(8,128)(2,1)S(1)} %get-tuple-element.25), channel_id=1, source_target_pairs={{0,20},{4,16},{8,28},{12,24},{16,4},{20,0},{24,12},{28,8},{1,21},{... | collective-permute-start | bytes 221192 | tf_op jit(solution)/shard_map/ppermute | solution.py:511
  37.3 9.1 %collective-permute-start.8 = (bf16[2,2,72,128]{3,2,1,0:T(8,128)(2,1)S(1)}, bf16[2,2,72,128]{3,2,1,0:T(8,128)(2,1)S(1)}, u32[]{:S(2)}, u32[]{:S(2)}) collective-permute-start(bf16[2,2,72,128]{3,2,1,0:T(8,128)(2,1)S(1)} %get-tuple-element.26), channel_id=1, source_target_pairs={{0,24},{4,28},{8,16},{12,20},{16,8},{20,12},{24,0},{28,4},{1,25},{... | collective-permute-start | bytes 221192 | tf_op jit(solution)/shard_map/ppermute | solution.py:511
  40.9 7.1 %collective-permute-start.9 = (bf16[2,2,72,128]{3,2,1,0:T(8,128)(2,1)S(1)}, bf16[2,2,72,128]{3,2,1,0:T(8,128)(2,1)S(1)}, u32[]{:S(2)}, u32[]{:S(2)}) collective-permute-start(bf16[2,2,72,128]{3,2,1,0:T(8,128)(2,1)S(1)} %get-tuple-element.27), channel_id=1, source_target_pairs={{0,28},{4,24},{8,20},{12,16},{16,12},{20,8},{24,4},{28,0},{1,29},{... | collective-permute-start | bytes 221192 | tf_op jit(solution)/shard_map/ppermute | solution.py:511
  43.1 4.9 %copy-start.7 = (bf16[128,512]{1,0:T(8,128)(2,1)S(1)}, bf16[128,512]{1,0:T(8,128)(2,1)}, u32[]{:S(2)}) copy-start(bf16[128,512]{1,0:T(8,128)(2,1)} %constant.80.clone.refs_11_.refs_4_) | copy-start | bytes 393220
  43.1 4.9 %copy-start.9 = (bf16[1024,128]{1,0:T(8,128)(2,1)S(1)}, bf16[1024,128]{1,0:T(8,128)(2,1)}, u32[]{:S(2)}) copy-start(bf16[1024,128]{1,0:T(8,128)(2,1)} %constant.81.clone.refs_12_) | copy-start | bytes 786436
  43.1 4.9 %copy-start.13 = (f32[7,1,128]{2,1,0:T(1,128)S(1)}, f32[7,1,128]{2,1,0:T(1,128)}, u32[]{:S(2)}) copy-start(f32[7,1,128]{2,1,0:T(1,128)} %constant.85.clone.refs_8_) | copy-start | bytes 10756
  43.1 28.8 %slice-start.1 = ((s8[5242880]{0:T(1024)(128)(4,1)}), s8[1048576]{0:T(1024)(128)(4,1)S(1)}, s32[]{:S(2)}) async-start(s8[5242880]{0:T(1024)(128)(4,1)} %bitcast.21), calls=%async_computation.1 | async-start | bytes 2097152
  48.0 23.9 %copy-start.1 = (bf16[1,32,16,16,256]{4,3,2,1,0:T(8,128)(2,1)S(1)}, bf16[1,32,16,16,256]{4,3,2,1,0:T(8,128)(2,1)}, u32[]{:S(2)}) copy-start(bf16[1,32,16,16,256]{4,3,2,1,0:T(8,128)(2,1)} %param.16) | copy-start | bytes 12582916
  48.0 23.9 %copy-start.4 = (bf16[896,1024]{1,0:T(8,128)(2,1)S(1)}, bf16[896,1024]{1,0:T(8,128)(2,1)}, u32[]{:S(2)}) copy-start(bf16[896,1024]{1,0:T(8,128)(2,1)} %constant.79.clone.refs_9_) | copy-start | bytes 5505028
  48.0 23.9 %copy-start.8 = (bf16[256,1024]{1,0:T(8,128)(2,1)S(1)}, bf16[256,1024]{1,0:T(8,128)(2,1)}, u32[]{:S(2)}) copy-start(bf16[256,1024]{1,0:T(8,128)(2,1)} %constant.78.clone.refs_10_) | copy-start | bytes 1572868
  48.0 23.9 %copy-start.10 = (bf16[512,32]{1,0:T(8,128)(2,1)S(1)}, bf16[512,32]{1,0:T(8,128)(2,1)}, u32[]{:S(2)}) copy-start(bf16[512,32]{1,0:T(8,128)(2,1)} %constant.83.clone.refs_12_) | copy-start | bytes 98308
  48.1 23.9 %copy-start.11 = (bf16[32,512]{1,0:T(8,128)(2,1)S(1)}, bf16[32,512]{1,0:T(8,128)(2,1)}, u32[]{:S(2)}) copy-start(bf16[32,512]{1,0:T(8,128)(2,1)} %constant.84.clone.refs_13_) | copy-start | bytes 98308
  48.1 23.9 %copy-start.12 = (bf16[32,32]{1,0:T(8,128)(2,1)S(1)}, bf16[32,32]{1,0:T(8,128)(2,1)}, u32[]{:S(2)}) copy-start(bf16[32,32]{1,0:T(8,128)(2,1)} %refs_11_.2) | copy-start | bytes 6148
  52.5 7.0 %collective-permute-start.12 = (bf16[7,72,128]{2,1,0:T(8,128)(2,1)S(1)}, bf16[7,72,128]{2,1,0:T(8,128)(2,1)S(1)}, u32[]{:S(2)}, u32[]{:S(2)}) collective-permute-start(bf16[7,72,128]{2,1,0:T(8,128)(2,1)S(1)} %get-tuple-element.28.refs_0_), channel_id=1, source_target_pairs={{0,12},{4,8},{8,4},{12,0},{1,13},{5,9},{9,5},{13,1},{2,14},{6,10},... | collective-permute-start | bytes 387080 | tf_op jit(solution)/shard_map/ppermute | solution.py:511
  54.3 9.8 %collective-permute-start.11 = (bf16[7,72,128]{2,1,0:T(8,128)(2,1)S(1)}, bf16[7,72,128]{2,1,0:T(8,128)(2,1)S(1)}, u32[]{:S(2)}, u32[]{:S(2)}) collective-permute-start(bf16[7,72,128]{2,1,0:T(8,128)(2,1)S(1)} %get-tuple-element.28.refs_0_), channel_id=1, source_target_pairs={{0,8},{4,12},{8,0},{12,4},{1,9},{5,13},{9,1},{13,5},{2,10},{6,14},... | collective-permute-start | bytes 387080 | tf_op jit(solution)/shard_map/ppermute | solution.py:511
  54.4 10.6 %collective-permute-start.10 = (bf16[7,72,128]{2,1,0:T(8,128)(2,1)S(1)}, bf16[7,72,128]{2,1,0:T(8,128)(2,1)S(1)}, u32[]{:S(2)}, u32[]{:S(2)}) collective-permute-start(bf16[7,72,128]{2,1,0:T(8,128)(2,1)S(1)} %get-tuple-element.28.refs_0_), channel_id=1, source_target_pairs={{0,4},{4,0},{8,12},{12,8},{1,5},{5,1},{9,13},{13,9},{2,6},{6,2},{1... | collective-permute-start | bytes 387080 | tf_op jit(solution)/shard_map/ppermute | solution.py:511
  56.9 9.5 %collective-permute-start.13 = (bf16[7,72,128]{2,1,0:T(8,128)(2,1)S(1)}, bf16[7,72,128]{2,1,0:T(8,128)(2,1)S(1)}, u32[]{:S(2)}, u32[]{:S(2)}) collective-permute-start(bf16[7,72,128]{2,1,0:T(8,128)(2,1)S(1)} %get-tuple-element.28.refs_0_), channel_id=1, source_target_pairs={{0,16},{16,0},{1,17},{17,1},{2,18},{18,2},{3,19},{19,3},{4,20},{20... | collective-permute-start | bytes 387080 | tf_op jit(solution)/shard_map/ppermute | solution.py:511
  59.5 8.4 %collective-permute-start.16 = (bf16[7,72,128]{2,1,0:T(8,128)(2,1)S(1)}, bf16[7,72,128]{2,1,0:T(8,128)(2,1)S(1)}, u32[]{:S(2)}, u32[]{:S(2)}) collective-permute-start(bf16[7,72,128]{2,1,0:T(8,128)(2,1)S(1)} %collective-permute-done.12.refs_3_), channel_id=1, source_target_pairs={{0,16},{16,0},{1,17},{17,1},{2,18},{18,2},{3,19},{19,3},{4,20},{20... | collective-permute-start | bytes 387080 | tf_op jit(solution)/shard_map/ppermute | solution.py:511
  64.2 6.3 %collective-permute-start.15 = (bf16[7,72,128]{2,1,0:T(8,128)(2,1)S(1)}, bf16[7,72,128]{2,1,0:T(8,128)(2,1)S(1)}, u32[]{:S(2)}, u32[]{:S(2)}) collective-permute-start(bf16[7,72,128]{2,1,0:T(8,128)(2,1)S(1)} %collective-permute-done.11.refs_2_), channel_id=1, source_target_pairs={{0,16},{16,0},{1,17},{17,1},{2,18},{18,2},{3,19},{19,3},{4,20},{20... | collective-permute-start | bytes 387080 | tf_op jit(solution)/shard_map/ppermute | solution.py:511
  64.9 7.0 %collective-permute-start.14 = (bf16[7,72,128]{2,1,0:T(8,128)(2,1)S(1)}, bf16[7,72,128]{2,1,0:T(8,128)(2,1)S(1)}, u32[]{:S(2)}, u32[]{:S(2)}) collective-permute-start(bf16[7,72,128]{2,1,0:T(8,128)(2,1)S(1)} %collective-permute-done.10.refs_1_), channel_id=1, source_target_pairs={{0,16},{16,0},{1,17},{17,1},{2,18},{18,2},{3,19},{19,3},{4,20},{20... | collective-permute-start | bytes 387080 | tf_op jit(solution)/shard_map/ppermute | solution.py:511
  66.2 14.6 %collective-permute-start.19 = (bf16[2,7,72,128]{3,2,1,0:T(8,128)(2,1)S(1)}, bf16[2,7,72,128]{3,2,1,0:T(8,128)(2,1)S(1)}, u32[]{:S(2)}, u32[]{:S(2)}) collective-permute-start(bf16[2,7,72,128]{3,2,1,0:T(8,128)(2,1)S(1)} %pad_maximum_fusion.refs_0_), channel_id=1, source_target_pairs={{0,3},{1,2},{2,1},{3,0},{4,7},{5,6},{6,5},{7,4},{8,11},{9,10},{10,... | collective-permute-start | bytes 774152 | tf_op jit(solution)/shard_map/ppermute | solution.py:511
  66.4 14.4 %collective-permute-start.18 = (bf16[2,7,72,128]{3,2,1,0:T(8,128)(2,1)S(1)}, bf16[2,7,72,128]{3,2,1,0:T(8,128)(2,1)S(1)}, u32[]{:S(2)}, u32[]{:S(2)}) collective-permute-start(bf16[2,7,72,128]{3,2,1,0:T(8,128)(2,1)S(1)} %pad_maximum_fusion.refs_0_), channel_id=1, source_target_pairs={{0,2},{1,3},{2,0},{3,1},{4,6},{5,7},{6,4},{7,5},{8,10},{9,11},{10,... | collective-permute-start | bytes 774152 | tf_op jit(solution)/shard_map/ppermute | solution.py:511
  67.9 12.9 %collective-permute-start.17 = (bf16[2,7,72,128]{3,2,1,0:T(8,128)(2,1)S(1)}, bf16[2,7,72,128]{3,2,1,0:T(8,128)(2,1)S(1)}, u32[]{:S(2)}, u32[]{:S(2)}) collective-permute-start(bf16[2,7,72,128]{3,2,1,0:T(8,128)(2,1)S(1)} %pad_maximum_fusion.refs_0_), channel_id=1, source_target_pairs={{0,1},{1,0},{2,3},{3,2},{4,5},{5,4},{6,7},{7,6},{8,9},{9,8},{10,11... | collective-permute-start | bytes 774152 | tf_op jit(solution)/shard_map/ppermute | solution.py:511
  71.9 8.9 %copy-start.5 = (bf16[4,128,1024]{2,1,0:T(8,128)(2,1)S(1)}, bf16[4,128,1024]{2,1,0:T(8,128)(2,1)}, u32[]{:S(2)}) copy-start(bf16[4,128,1024]{2,1,0:T(8,128)(2,1)} %constant.82.clone.refs_5_) | copy-start | bytes 3145732

commit v2 on v0

v2 whole, which is shorter than its diff:
```python
import functools
import math

import jax
import jax.numpy as jnp
import ml_dtypes
import numpy as np
from jax import lax
from jax.experimental import pallas as pl
from jax.experimental.pallas import tpu as pltpu
from jax.sharding import PartitionSpec as P

MX = 24
MY = 24
MZ = 13
LANES = 128
NT = (((1,), (1,)), ((), ()))
BF16 = ml_dtypes.bfloat16


def angles(xp, index, modes, positions, length):
    freq = xp.where(index < modes // 2, index, index - modes)
    turns = (freq[..., None] * positions) % length
    return turns.astype(np.float32) * np.float32(2.0 * math.pi / length)


def mode_angles(xp, rows, sizes, local_x, local_y):
    groups, groups_y, modes_xd, modes_yd, total_x, total_y = sizes
    owner = xp.repeat(xp.arange(groups, dtype=np.int32), rows)
    within = xp.tile(xp.arange(rows, dtype=np.int32), groups)
    kx = owner // groups_y * modes_xd + xp.minimum(within // modes_yd, modes_xd - 1)
    ky = owner % groups_y * modes_yd + within % modes_yd
    angle_x = angles(xp, kx, MX, local_x, total_x)
    angle_y = angles(xp, ky, MY, local_y, total_y)
    theta = (angle_x[:, :, None] + angle_y[:, None, :]).reshape(owner.shape[0], -1)
    return theta, (within < modes_xd * modes_yd)[:, None]


def device_cells(xp, me, groups_y, cells_x, cells_y):
    local_x = me // groups_y * cells_x + xp.arange(cells_x, dtype=np.int32)
    local_y = me % groups_y * cells_y + xp.arange(cells_y, dtype=np.int32)
    return local_x, local_y


def forward_table(rows, sizes, cells_x, cells_y):
    groups, groups_y = sizes[:2]
    theta, real = mode_angles(
        np, rows, sizes, *device_cells(np, np.int32(0), groups_y, cells_x, cells_y)
    )
    base = np.where(real, np.concatenate([np.cos(theta), np.sin(theta)], 1), np.float32(0))
    turns = []
    for x in range(0, groups // groups_y, 2):
        for y in range(0, groups_y, 2):
            turn = np.zeros((groups * rows, LANES), np.float32)
            for t in range(4):
                device = np.int32(x * groups_y + y + quad_offset(t, groups_y))
                local_x, local_y = device_cells(np, device, groups_y, cells_x, cells_y)
                angle, _ = mode_angles(np, rows, sizes, local_x[:1], local_y[:1])
                turn[:, 2 * t] = np.cos(angle[:, 0])
                turn[:, 2 * t + 1] = np.sin(angle[:, 0])
            turns.append(turn)
    return base, np.stack(turns)


def inverse_table(xp, me, rows, sizes, cells_x, cells_y):
    theta, real = mode_angles(
        xp, rows, sizes, *device_cells(xp, me, sizes[1], cells_x, cells_y)
    )
    cosine = xp.where(real, xp.cos(theta), np.float32(0))
    sine = xp.where(real, xp.sin(theta), np.float32(0))
    return xp.concatenate([cosine.T, sine.T], 0).astype(BF16)


def quad_offset(t, groups_y):
    return t // 2 * groups_y + t % 2


def quad_of(r, groups_y):
    return r // groups_y % 2 * 2 + r % groups_y % 2


def z_angles(length):
    return angles(np, np.arange(MZ, dtype=np.int32), 2 * MZ, np.arange(length, dtype=np.int32), length)


def forward_z_table(length):
    theta = z_angles(length)
    parts = np.stack([np.cos(theta), -np.sin(theta)], 1).reshape(2 * MZ, length)
    table = np.zeros((-(-2 * MZ // 16) * 16, length), np.float32)
    table[: 2 * MZ] = parts
    return table.astype(BF16)


def split16(values):
    high = values.astype(BF16)
    low = (values - high.astype(np.float32)).astype(BF16)
    return high, low


def inverse_z_table(length, per_tile, slot, norm):
    theta = z_angles(length)
    parts = np.stack([np.cos(theta), -np.sin(theta)], 0) * np.float32(norm)
    table = np.zeros((per_tile, 2, slot, per_tile, length), np.float32)
    for c in range(per_tile):
        table[c, :, :MZ, c] = parts
    high, low = split16(table.reshape(LANES, per_tile * length))
    return np.concatenate([high, low], 0)


def order_table(channels, kz_pad, per_tile, slot):
    table = np.zeros((kz_pad, 2, channels, channels // per_tile, per_tile, 2, slot), np.float32)
    for kz in range(MZ):
        for part in range(2):
            for c in range(channels):
                table[kz, part, c, c // per_tile, c % per_tile, part, kz] = 1
    return table.reshape(kz_pad * 2 * channels, -1).astype(BF16)


def spread_table(channels, half, copies):
    table = np.zeros((half, 2, channels, half, 2, copies.shape[0]), np.float32)
    for h in range(half):
        for part in range(2):
            table[h, part, copies, h, part, np.arange(copies.shape[0])] = 1
    return table.reshape(half * 2 * channels, -1).astype(BF16)


def gather_table(channels, copies):
    table = np.zeros((channels, channels, copies, channels), np.float32)
    for i in range(channels):
        table[i, :, :, i] = 1
    return table.reshape(channels * channels, -1).astype(BF16)


def cell_tables(channels, per_tile, cells_y):
    rows = np.zeros((per_tile, channels // per_tile, cells_y, channels), np.float32)
    for c in range(channels):
        rows[c % per_tile, c // per_tile, :, c] = 1
    columns = np.repeat(np.eye(channels, dtype=np.float32), cells_y, 1)
    return rows.reshape(-1, channels).astype(BF16), columns.astype(BF16)


def regroup_table(channels, block, half):
    groups = channels // block
    kz_tile = LANES // (2 * block)
    table = np.zeros((groups, kz_tile, 2, block, kz_tile // half, half, 2, groups, block), np.float32)
    for g in range(groups):
        for kz in range(kz_tile):
            for part in range(2):
                for c in range(block):
                    table[g, kz, part, c, kz // half, kz % half, part, g, c] = 1
    return table.reshape(groups * LANES, -1).astype(BF16)


def params(mib):
    return pltpu.CompilerParams(vmem_limit_bytes=mib * 1024 * 1024)


IN_VMEM = pl.BlockSpec(memory_space=pltpu.VMEM)
IN_SMEM = pl.BlockSpec(memory_space=pltpu.SMEM)
IN_HBM = pl.BlockSpec(memory_space=pl.ANY)


def resident(*arrays):
    return [pltpu.with_memory_space_constraint(a, pltpu.VMEM) for a in arrays]


def along_z_kernel(info_ref, z_ref, x_ref, *rest):
    outs, table = rest[:4], rest[4]
    block, span, _ = table.shape
    shape = (span, z_ref.shape[0])
    row = lax.broadcasted_iota(jnp.int32, shape, 0) // block
    repeat = (row == lax.broadcasted_iota(jnp.int32, shape, 1)).astype(jnp.bfloat16)
    rows = jnp.dot(repeat, z_ref[...], preferred_element_type=jnp.float32)
    channel = lax.broadcasted_iota(jnp.int32, rows.shape, 0) % block
    for c in range(block):
        table[c] = jnp.where(channel == c, rows, 0.0).astype(jnp.bfloat16)
    for t in range(4):
        first = jnp.bitwise_xor(info_ref[1], t) * block
        total = None
        for c in range(block):
            term = lax.dot_general(
                table[c], x_ref[first + c], NT, preferred_element_type=jnp.float32
            )
            total = term if total is None else total + term
        outs[t][...] = total.astype(jnp.bfloat16)


def along_z(info, field, z_table, block):
    channels, cells, length = field.shape
    span = 2 * MZ * block
    return pl.pallas_call(
        along_z_kernel,
        out_shape=[jax.ShapeDtypeStruct((span, cells), jnp.bfloat16)] * 4,
        in_specs=[IN_SMEM] + [IN_VMEM] * 2,
        out_specs=[IN_VMEM] * 4,
        scratch_shapes=[pltpu.VMEM((block, span, length), jnp.bfloat16)],
        compiler_params=params(12),
        cost_estimate=pl.CostEstimate(
            flops=2 * span * cells * length * channels,
            bytes_accessed=2 * field.size,
            transcendentals=0,
        ),
        name="along_z",
    )(info, *resident(z_table, field))


def place_cells(info_ref, sources, block, data):
    span, cells = sources[0].shape
    for t in range(4):
        place = jnp.bitwise_xor(info_ref[1], t)
        value = sources[t][...].astype(jnp.float32)
        turned = []
        for k in range(0, span, 2 * block):
            turned += [value[k + block : k + 2 * block], -value[k : k + block]]
        data[place, :, :cells] = sources[t][...]
        data[place, :, cells:] = jnp.concatenate(turned, 0).astype(jnp.bfloat16)


def sum_plane(table, data):
    total = None
    for device in range(4):
        for part in range(2):
            term = lax.dot_general(
                table[device, part], data[device], NT, preferred_element_type=jnp.float32
            )
            total = term if total is None else total + term
    return total


def first_plane_kernel(block, info_ref, base_ref, turn_ref, *refs):
    sources, (out_ref, table, data) = refs[:4], refs[4:]
    cells = sources[0].shape[1]
    place_cells(info_ref, sources, block, data)
    turns = turn_ref[info_ref[2]]
    cosine, sine = base_ref[:, :cells], base_ref[:, cells:]
    for device in range(4):
        turn_cos = turns[:, 2 * device : 2 * device + 1]
        turn_sin = turns[:, 2 * device + 1 : 2 * device + 2]
        both = (cosine * turn_cos - sine * turn_sin, sine * turn_cos + cosine * turn_sin)
        for k, values in enumerate(both):
            high = values.astype(jnp.bfloat16)
            table[device, 0, :, k * cells : (k + 1) * cells] = high
            low = (values - high.astype(jnp.float32)).astype(jnp.bfloat16)
            table[device, 1, :, k * cells : (k + 1) * cells] = low
    out_ref[...] = sum_plane(table, data)


def first_plane(info, sources, base, turns, block):
    span, cells = sources[0].shape
    modes = base.shape[0]
    return pl.pallas_call(
        functools.partial(first_plane_kernel, block),
        out_shape=[
            jax.ShapeDtypeStruct((modes, span), jnp.float32),
            jax.ShapeDtypeStruct((4, 2, modes, 2 * cells), jnp.bfloat16),
        ],
        in_specs=[IN_SMEM] + [IN_VMEM] * 6,
        out_specs=[IN_VMEM] * 2,
        scratch_shapes=[pltpu.VMEM((4, span, 2 * cells), jnp.bfloat16)],
        compiler_params=params(24),
        cost_estimate=pl.CostEstimate(
            flops=32 * cells * span * modes, bytes_accessed=4 * base.size, transcendentals=0
        ),
        name="first_plane",
    )(info, *resident(base, turns), *sources)


def tail_parts(rows):
    return next(k for k in (3, 2, 1) if rows % (8 * k) == 0)


def second_plane_kernel(groups, rows, block, info_ref, table_ref, other_ref, *refs):
    sources, outs, (sums, data) = refs[:4], refs[4 : 4 + groups], refs[4 + groups :]
    place_cells(info_ref, sources, block, data)
    sums[...] = sum_plane(table_ref, data)
    over = sums.shape[1] - LANES
    room = LANES - over
    parts = tail_parts(rows)
    step = rows // parts
    for r in range(groups):
        owner = jnp.bitwise_xor(info_ref[0], r)
        own = pl.ds(pl.multiple_of(owner * rows, 8), rows)
        first, second = other_ref[own], sums[own]
        mixed = jnp.concatenate([first[:, LANES:], second[:, LANES : LANES + room]], 1)
        tail = second[:, LANES + room :]
        tail = [tail[k * step : (k + 1) * step] for k in range(parts)]
        rest = LANES - parts * (over - room)
        tail = jnp.concatenate(tail + [jnp.zeros((step, rest), jnp.float32)], 1)
        whole = jnp.concatenate([first[:, :LANES], second[:, :LANES], mixed, tail], 0)
        outs[r][...] = whole.astype(jnp.bfloat16)


def second_plane(info, sources, table, other, groups, rows, block):
    span, cells = sources[0].shape
    modes = table.shape[2]
    chunk = jax.ShapeDtypeStruct((3 * rows + rows // tail_parts(rows), LANES), jnp.bfloat16)
    return pl.pallas_call(
        functools.partial(second_plane_kernel, groups, rows, block),
        out_shape=[chunk] * groups,
        in_specs=[IN_SMEM] + [IN_VMEM] * 6,
        out_specs=[IN_VMEM] * groups,
        scratch_shapes=[
            pltpu.VMEM((modes, span), jnp.float32),
            pltpu.VMEM((4, span, 2 * cells), jnp.bfloat16),
        ],
        compiler_params=params(24),
        cost_estimate=pl.CostEstimate(
            flops=32 * cells * span * modes, bytes_accessed=2 * table.size, transcendentals=0
        ),
        name="second_plane",
    )(info, *resident(table), other, *sources)


def total_kernel(groups, groups_y, over, scale, info_ref, scale_ref, regroup_ref, *refs):
    chunks, outs, held = refs[:groups], refs[groups:-1], refs[-1]
    rows = held.shape[2]
    parts = tail_parts(rows)
    room = LANES - over
    left = over - room
    for t in range(4):
        place = jnp.bitwise_xor(info_ref[1], t)
        mine = [c for r, c in enumerate(chunks) if quad_of(r, groups_y) == t]
        total = mine[0][...].astype(jnp.float32)
        for ref in mine[1:]:
            total = total + ref[...].astype(jnp.float32)
        mixed, tail = total[2 * rows : 3 * rows], total[3 * rows :]
        tail = jnp.concatenate([tail[:, k * left : (k + 1) * left] for k in range(parts)], 0)
        zeros = jnp.zeros((rows, room), jnp.float32)
        held[place, 0] = total[:rows]
        held[place, 1] = jnp.concatenate([mixed[:, :over], zeros], 1)
        held[place, 2] = total[rows : 2 * rows]
        held[place, 3] = jnp.concatenate([mixed[:, over:], tail, zeros], 1)
    tiles = outs[0].shape[0] - 2
    for j in range(2):
        values = jnp.concatenate([held[g, j] for g in range(4)], 1) * scale_ref[j : j + 1]
        sums = jnp.dot(
            values.astype(jnp.bfloat16), regroup_ref[...], preferred_element_type=jnp.float32
        ).astype(jnp.bfloat16)
        for k in range(4):
            if j * 4 + k < tiles:
                for out in outs:
                    out[j * 4 + k] = sums[:, k * LANES : (k + 1) * LANES]
    for r, out in enumerate(outs):
        for j in range(2):
            value = held[jnp.bitwise_xor(info_ref[4], r), 2 + j] * scale
            out[tiles + j] = value.astype(jnp.bfloat16)


def total(info, chunks, scale, norm, regroup, tiles, rows, over, scenes, groups_y):
    out = jax.ShapeDtypeStruct((tiles + 2, rows, LANES), jnp.bfloat16)
    return pl.pallas_call(
        functools.partial(total_kernel, len(chunks), groups_y, over, norm),
        out_shape=[out] * scenes,
        in_specs=[IN_SMEM] + [IN_VMEM] * (2 + len(chunks)),
        out_specs=[IN_VMEM] * scenes,
        scratch_shapes=[pltpu.VMEM((4, 4, rows, LANES), jnp.float32)],
        compiler_params=params(12),
        cost_estimate=pl.CostEstimate(
            flops=4 * rows * regroup.size,
            bytes_accessed=2 * len(chunks) * chunks[0].size,
            transcendentals=0,
        ),
        name="total",
    )(info, *resident(scale, regroup), *chunks)


def mix_kernel(spread_ref, gather_ref, w_ref, s_ref, out_ref):
    tiles, rows, _ = out_ref.shape
    last, _, _, width = w_ref.shape
    half = spread_ref.shape[1] // (2 * LANES)
    for tile in range(tiles):
        wide = jnp.dot(s_ref[tile], spread_ref[...], preferred_element_type=jnp.float32)
        products = []
        for h in range(half):
            kz = tile * half + h
            if kz >= last:
                continue
            out_re = wide[:, (2 * h) * LANES : (2 * h + 1) * LANES]
            out_im = wide[:, (2 * h + 1) * LANES : (2 * h + 2) * LANES]
            real, imag = [], []
            for k in range(width // LANES):
                lane = slice(k * LANES, (k + 1) * LANES)
                w_re = w_ref[kz, 0, :, lane].astype(jnp.float32)
                w_im = w_ref[kz, 1, :, lane].astype(jnp.float32)
                real.append((w_re * out_re + w_im * out_im).astype(jnp.bfloat16))
                imag.append((w_re * out_im - w_im * out_re).astype(jnp.bfloat16))
            products += [jnp.concatenate(real, 1), jnp.concatenate(imag, 1)]
        sums = jnp.dot(
            jnp.concatenate(products, 0), gather_ref[...], preferred_element_type=jnp.float32
        )
        which = lax.broadcasted_iota(jnp.int32, (rows, LANES), 1) // (LANES // (2 * half))
        out = sums[:rows]
        for k in range(1, len(products)):
            out = jnp.where(which == k, sums[k * rows : (k + 1) * rows], out)
        out_ref[tile] = jnp.where(which < len(products), out, 0.0).astype(jnp.bfloat16)


def mix(spectra, weight, spread, gather):
    tiles, rows = spectra.shape[0] - 2, spectra.shape[1]
    return pl.pallas_call(
        mix_kernel,
        out_shape=jax.ShapeDtypeStruct((tiles, rows, LANES), jnp.bfloat16),
        in_specs=[IN_VMEM] * 4,
        out_specs=IN_VMEM,
        compiler_params=params(16),
        cost_estimate=pl.CostEstimate(
            flops=8 * tiles * rows * gather.size, bytes_accessed=2 * weight.size, transcendentals=0
        ),
        name="mix",
    )(*resident(spread, gather, weight), spectra)


def outer_kernel(scenes, spread_ref, pick_ref, *refs):
    spectra, out_ref = refs[:scenes], refs[scenes]
    last, _, rows, wide = out_ref.shape
    half = spread_ref.shape[1] // (2 * LANES)
    per_tile = pick_ref.shape[0]
    tiles = spectra[0].shape[0] - 2
    for kz in range(last):
        if kz % half == 0:
            grads = jnp.dot(
                jnp.concatenate([ref[kz // half] for ref in spectra], 0),
                spread_ref[...],
                preferred_element_type=jnp.float32,
            )
        if kz % per_tile == 0:
            field = jnp.concatenate([ref[tiles + kz // per_tile] for ref in spectra], 0)
        hats = jnp.dot(field, pick_ref[kz % per_tile], preferred_element_type=jnp.float32)
        lane = 2 * (kz % half) * LANES
        for k in range(wide // LANES):
            real, imag = 0.0, 0.0
            for s in range(scenes):
                here = slice(s * rows, (s + 1) * rows)
                hat_re = hats[here, k * LANES : (k + 1) * LANES]
                hat_im = hats[here, wide + k * LANES : wide + (k + 1) * LANES]
                out_re = grads[here, lane : lane + LANES]
                out_im = grads[here, lane + LANES : lane + 2 * LANES]
                real += out_re * hat_re + out_im * hat_im
                imag += out_im * hat_re - out_re * hat_im
            out_ref[kz, 0, :, k * LANES : (k + 1) * LANES] = real
            out_ref[kz, 1, :, k * LANES : (k + 1) * LANES] = imag


def outer(spectra, spread, pick):
    tiles, rows, _ = spectra[0].shape
    wide = pick.shape[2] // 2
    return pl.pallas_call(
        functools.partial(outer_kernel, len(spectra)),
        out_shape=jax.ShapeDtypeStruct((MZ, 2, rows, wide), jnp.float32),
        in_specs=[IN_VMEM] * (2 + len(spectra)),
        out_specs=IN_VMEM,
        compiler_params=params(16),
        cost_estimate=pl.CostEstimate(
            flops=2 * tiles * rows * 4 * LANES * 12 * LANES,
            bytes_accessed=16 * tiles * rows * wide + 8 * tiles * rows * LANES * len(spectra),
            transcendentals=0,
        ),
        name="outer",
    )(*resident(spread, pick), *spectra)


def local_kernel(row_ref, column_ref, point_ref, grad_ref, out_ref, mixing):
    channels, cells_x, cells_y, length = grad_ref.shape
    picked = lax.dot_general(row_ref[...], point_ref[...], NT, preferred_element_type=jnp.float32)
    spread = jnp.dot(
        picked.astype(jnp.bfloat16), column_ref[...], preferred_element_type=jnp.float32
    )
    row = lax.broadcasted_iota(jnp.int32, spread.shape, 0) % cells_y
    column = lax.broadcasted_iota(jnp.int32, spread.shape, 1) % cells_y
    mixing[...] = jnp.where(row == column, spread, 0.0).astype(jnp.bfloat16)

    @pl.loop(0, cells_x)
    def _(x):
        out_ref[x] = jnp.dot(
            mixing[...],
            grad_ref[:, x].reshape(channels * cells_y, length),
            preferred_element_type=jnp.float32,
        ).astype(out_ref.dtype)


def local(cell_rows, cell_columns, point, grad):
    channels, cells_x, cells_y, length = grad.shape
    width = channels * cells_y
    return pl.pallas_call(
        local_kernel,
        out_shape=jax.ShapeDtypeStruct((cells_x, width, length), jnp.bfloat16),
        in_specs=[IN_VMEM] * 4,
        out_specs=IN_VMEM,
        scratch_shapes=[pltpu.VMEM((width, width), jnp.bfloat16)],
        compiler_params=params(16),
        cost_estimate=pl.CostEstimate(
            flops=2 * grad.size * width, bytes_accessed=4 * grad.size, transcendentals=0
        ),
        name="local",
    )(*resident(cell_rows, cell_columns, point, grad))


def inverse_kernel(groups, per_tile, here, info_ref, t_ref, order_ref, z_ref, local_ref, *refs):
    chunks, (out_ref, modes, held, built, sems) = refs[:groups], refs[groups:]
    channels, cells_x, cells_y, length = built.shape
    rows = chunks[0].shape[1]
    tiles = channels // per_tile
    for r in range(groups):
        own = pl.ds(pl.multiple_of(jnp.bitwise_xor(info_ref[0], r) * rows, 8), rows)
        for j in range(chunks[r].shape[0]):
            modes[own, j * LANES : (j + 1) * LANES] = chunks[r][j].astype(jnp.float32)
    sums = jnp.dot(
        t_ref[info_ref[3]], modes[...].astype(jnp.bfloat16), preferred_element_type=jnp.float32
    )
    cells = sums.shape[0] // 2
    cosine, sine = sums[:cells], sums[cells:]
    wide = sine.shape[1]
    lane = lax.broadcasted_iota(jnp.int32, sine.shape, 1)
    first = lane % (2 * channels) < channels
    turned = jnp.where(
        first, -pltpu.roll(sine, wide - channels, 1), pltpu.roll(sine, channels, 1)
    )
    back = (cosine + turned).astype(jnp.bfloat16)
    ordered = jnp.dot(back, order_ref[...], preferred_element_type=jnp.float32)
    held[...] = ordered.astype(jnp.bfloat16).reshape(held.shape)

    span = tiles * cells_y
    copies = []
    for start in range(0, cells_x, here):
        stack = []
        for x in range(start, start + here):
            back = held[x]
            stack += [back[:, k * LANES : (k + 1) * LANES] for k in range(tiles)]
        stack = jnp.concatenate(stack, 0)
        spectral = jnp.dot(
            jnp.concatenate([stack, stack], 1), z_ref[...], preferred_element_type=jnp.float32
        )
        for x in range(here):
            for j in range(per_tile):
                both = (
                    spectral[x * span : (x + 1) * span, j * length : (j + 1) * length]
                    + local_ref[start + x, j * span : (j + 1) * span].astype(jnp.float32)
                ).astype(jnp.bfloat16)
                for k in range(tiles):
                    built[k * per_tile + j, start + x] = both[k * cells_y : (k + 1) * cells_y]
        copies.append(
            pltpu.make_async_copy(
                built.at[:, pl.ds(start, here)],
                out_ref.at[:, pl.ds(start, here)],
                sems.at[start // here],
            )
        )
        copies[-1].start()
    for copy in copies:
        copy.wait()


def inverse(info, chunks, table, order, z_table, local_part, shape, per_tile, here):
    channels, cells_x, cells_y, length = shape
    return pl.pallas_call(
        functools.partial(inverse_kernel, len(chunks), per_tile, here),
        out_shape=jax.ShapeDtypeStruct(shape, jnp.bfloat16),
        in_specs=[IN_SMEM] + [IN_VMEM] * (4 + len(chunks)),
        out_specs=IN_HBM,
        scratch_shapes=[
            pltpu.VMEM((table.shape[2], order.shape[0]), jnp.float32),
            pltpu.VMEM((cells_x, cells_y, order.shape[1]), jnp.bfloat16),
            pltpu.VMEM(shape, jnp.bfloat16),
            pltpu.SemaphoreType.DMA((cells_x // here,)),
        ],
        compiler_params=params(28),
        cost_estimate=pl.CostEstimate(
            flops=2 * local_part.size * LANES, bytes_accessed=4 * local_part.size, transcendentals=0
        ),
        name="inverse",
    )(info, *resident(table, order, z_table, local_part), *chunks)


def flip(value, axes, size, r):
    return lax.ppermute(value, axes, [(i, i ^ r) for i in range(size)])


def body(field_in, grad_pre, spec_weight, point_weight):
    _, channels, cells_x, cells_y, cells_z = field_in.shape
    groups_x, groups_y = lax.axis_size("gx"), lax.axis_size("gy")
    groups, scenes = groups_x * groups_y, lax.axis_size("scene")
    group_axes = ("gx", "gy")
    total_x, total_y = cells_x * groups_x, cells_y * groups_y
    cells = cells_x * cells_y
    norm = float(total_x * total_y * cells_z) ** -0.5
    modes_xd, modes_yd = spec_weight.shape[:2]
    modes = modes_xd * modes_yd
    rows = -(-modes // 8) * 8
    half = LANES // (2 * channels)
    tiles = -(-MZ // half)
    block = channels // 4
    slot = 16
    per_tile = LANES // (2 * slot)
    sizes = (groups, groups_y, modes_xd, modes_yd, total_x, total_y)

    me = lax.axis_index(group_axes)
    at_x, at_y = lax.axis_index("gx"), lax.axis_index("gy")
    quad = at_x % 2 * 2 + at_y % 2
    base, turns = (jnp.asarray(t) for t in forward_table(rows, sizes, cells_x, cells_y))
    if groups * groups * rows * 2 * cells <= 1 << 24:
        inverse_t = jnp.asarray(
            np.stack([inverse_table(np, i, rows, sizes, cells_x, cells_y) for i in range(groups)])
        )
        inverse_at = me
    else:
        inverse_t = inverse_table(jnp, me, rows, sizes, cells_x, cells_y)[None]
        inverse_at = 0 * me
    forward_at = at_x // 2 * (groups_y // 2) + at_y // 2
    info = jnp.stack([me, quad, forward_at, inverse_at, lax.axis_index("scene")])

    z_table = jnp.asarray(forward_z_table(cells_z))
    regroup = jnp.asarray(regroup_table(channels, block, half))
    inverse_z = jnp.asarray(inverse_z_table(cells_z, per_tile, slot, norm))
    order = jnp.asarray(order_table(channels, tiles * half, per_tile, slot))
    lane = np.arange(LANES)
    spread = jnp.asarray(spread_table(channels, half, lane % channels))
    gather = jnp.asarray(gather_table(channels, LANES // channels))
    here = channels // scenes
    pair = np.arange(here * channels)
    kz_tile = LANES // (2 * block)
    pick = spread_table(here, kz_tile, pair // channels).reshape(LANES, kz_tile, -1)
    pick = jnp.asarray(pick.transpose(1, 0, 2))
    cell_rows, cell_columns = (jnp.asarray(t) for t in cell_tables(channels, per_tile, cells_y))
    scale = np.full((2, 4, kz_tile, 2 * block), 2.0 * norm, np.float32)
    scale[0, :, 0] = norm
    scale = jnp.asarray(scale.reshape(2, 4 * LANES))

    def cells_of(field):
        mine = along_z(info, field.reshape(channels, cells, cells_z), z_table, block)
        return [mine[0]] + [
            flip(mine[t], group_axes, groups, quad_offset(t, groups_y)) for t in range(1, 4)
        ]

    grad_cells = cells_of(grad_pre)
    field, _ = lax.optimization_barrier((field_in, grad_cells[0]))
    field_cells = cells_of(field)
    grad_sums, table = first_plane(info, grad_cells, base, turns, block)
    sums = second_plane(info, field_cells, table, grad_sums, groups, rows, block)
    got = [sums[0]] + [flip(sums[r], group_axes, groups, r) for r in range(1, groups)]
    weight = spec_weight.reshape(modes, MZ, 2, channels * channels)
    weight = jnp.pad(weight.transpose(1, 2, 0, 3), ((0, 0), (0, 0), (0, rows - modes), (0, 0)))
    local_part = local(
        cell_rows,
        cell_columns,
        point_weight,
        grad_pre.reshape(channels, cells_x, cells_y, cells_z),
    )
    got, weight, local_part = lax.optimization_barrier((got, weight, local_part))
    over = 2 * MZ * block - LANES
    spectra = total(
        info, got, scale, norm, regroup, tiles, rows, over, scenes, groups_y
    )
    mode_grad = mix(spectra[0], weight, spread, gather)

    along_y = {0: mode_grad}
    apart = groups_y // 2
    while apart:
        along_y.update({r ^ apart: flip(v, "gy", groups_y, apart) for r, v in along_y.items()})
        apart //= 2
    gathered = [along_y[r] for r in range(groups_y)]
    for r in range(1, groups_x):
        gathered += [flip(m, "gx", groups_x, r) for m in gathered[:groups_y]]

    others, _ = lax.optimization_barrier((spectra[1:], mode_grad))
    spectra = [spectra[0]] + [flip(others[r - 1], "scene", scenes, r) for r in range(1, scenes)]
    grads = outer(spectra, spread, pick)
    grad_spec = grads[:, :, :modes].transpose(2, 0, 1, 3)
    grad_spec = grad_spec.reshape(modes_xd, modes_yd, MZ, 2, here * channels)

    gathered, grad_spec = lax.optimization_barrier((gathered, grad_spec))
    grad_field = inverse(
        info,
        gathered,
        inverse_t,
        order,
        inverse_z,
        local_part,
        (channels, cells_x, cells_y, cells_z),
        per_tile,
        2,
    )
    return grad_field[None], grad_spec


def solution(mesh):
    return jax.shard_map(
        body,
        mesh=mesh,
        in_specs=(
            P("scene", None, "gx", "gy", None),
            P("scene", None, "gx", "gy", None),
            P("gx", "gy", None, None, None),
            P(),
        ),
        out_specs=(P("scene", None, "gx", "gy", None), P("gx", "gy", None, None, "scene")),
        check_vma=False,
    )
```

time: 369 us -> 73.6 us (0.20); the launches traced: 364 us -> 73.3 us
  local copies, waits for them, and re-layouts: 104 us -> 6.57 us
  matrix products: 93.8 us -> 0 us
  waiting for transfers between devices: 84.7 us -> 12.3 us
  blocking collectives: 37.2 us -> 0 us
  starting transfers between devices: 0.34 us -> 29.6 us
  other arithmetic: 28.9 us -> 0.01 us
  Pallas kernels: 0 us -> 23.7 us
  between operations: 14.6 us -> 1.12 us
    dot_general x10 -> x0, matrix products: 93.8 us -> none  [the longest x1 23.3 us: body(): jnp.einsum('abkio,absok->absik', weight_im, out_im, precision=highest)]
    unnamed x3 -> x0, waiting for transfers between devices: 84.7 us -> none
    another operation x14 -> x1, local copies, waits for them, and re-layouts: 47.6 us -> 0.09 us  [body(): jnp.stack([me, quad, forward_at, inverse_at, lax.axis_index('scene')])]
    all_gather x1 -> x0, blocking collectives: 37.2 us -> none  [body(): gathered = lax.all_gather(mode_flat, ('gx', 'gy'), axis=0, tiled=True)]
    ppermute x0 -> x23, starting transfers between devices: none -> 29.6 us  [flip(): return lax.ppermute(value, axes, [(i, i ^ r) for i in range(size)])]
    reshape x4 -> x1, local copies, waits for them, and re-layouts: 27.6 us -> 1.25 us  [body(): weight = spec_weight.reshape(modes, MZ, 2, channels * channels)]
    pallas_call x0 -> x9, Pallas kernels: none -> 23.7 us  [the longest x1 5.28 us: local(): pl.pallas_call(local_kernel, out_shape=jax.ShapeDtypeStruct((cells_x, wid...]
    add x3 -> x0, other arithmetic: 12.4 us -> none  [the longest x1 12.4 us: body(): jnp.einsum('absok,absik->abkio', out_re, hat_re, precision=highest)]
  transfers between devices with their start and end apart: 2 -> 23, of which waited for: 1 -> 7; matrix products, arithmetic and copies ran while one was open for 32% -> 5% of each run, Pallas kernels for 0% -> 16%
where the time goes in v2:
time: 73.6 us; the launch traced here: 73.3 us
  starting transfers between devices  29.6 us (40%)
  Pallas kernels  23.7 us (32%)
  waiting for transfers between devices  12.3 us (17%)
  local copies, waits for them, and re-layouts  6.57 us (9%)
  between operations  1.12 us (2%)
    ppermute x23, starting transfers between devices, flip(): return lax.ppermute(value, axes, [(i, i ^ r) for i in range(size)])  29.6 us
    ppermute x23, waiting for transfers between devices, flip(): return lax.ppermute(value, axes, [(i, i ^ r) for i in range(size)])  12.3 us
    pallas_call x1, Pallas kernels, local(): pl.pallas_call(local_kernel, out_shape=jax.ShapeDtypeStruct((cells_x, wid...  5.28 us
    pallas_call x1, Pallas kernels, inverse(): pl.pallas_call(functools.partial(inverse_kernel, len(chunks), per_tile, h...  4.64 us
    pallas_call x2, Pallas kernels, along_z(): pl.pallas_call(along_z_kernel, out_shape=[jax.ShapeDtypeStruct((span, cel...  4.08 us
    unnamed x38, local copies, waits for them, and re-layouts  3 us
    pallas_call x1, Pallas kernels, first_plane(): pl.pallas_call(functools.partial(first_plane_kernel, block), out_shape=[j...  2.55 us
    transpose x1, local copies, waits for them, and re-layouts, body(): grad_spec = grads[:, :, :modes].transpose(2, 0, 1, 3)  2.24 us
  transfers between devices with their start and end apart: 23, of which 7 were waited for; matrix products, arithmetic and copies ran while one was open for 5% of the time, Pallas kernels for 16%

profile of v2, /device:TPU:0, one launch (start us, length us, event | category | flops | bytes accessed | tf_op | source)
XLA Modules:
  0.0 73.3 jit_solution(13974967446455164455)
XLA Ops:
  0.7 0.1 stack.20.info_ref
  0.8 2.2 %copy-done = bf16[1,32,16,16,256]{4,3,2,1,0:T(8,128)(2,1)S(1)} copy-done((bf16[1,32,16,16,256]{4,3,2,1,0:T(8,128)(2,1)S(1)}, bf16[1,32,16,16,256]{4,3,2,1,0:T(8,128)(2,1)}, u32[]{:S(2)}) %copy-start) | copy-done | bytes 4194328
  2.9 0.7 copy-done.9
  3.7 2.0 %along_z.2 = (bf16[208,256]{1,0:T(8,128)(2,1)S(1)}, bf16[208,256]{1,0:T(8,128)(2,1)S(1)}, bf16[208,256]{1,0:T(8,128)(2,1)S(1)}, bf16[208,256]{1,0:T(8,128)(2,1)S(1)}) custom-call(s32[5]{0:T(128)S(1)} %stack.20.info_ref, bf16[32,256]{1,0:T(8,128)(2,1)S(1)} %copy-done.9, bf16[32,256,256]{2,1,0:T(8,128)(2,1)S(1)} %bitcast.14), custom_call_target="tpu_custom_call" | custom-call | flops 872415232 | bytes 4194304 | tf_op jit(solution)/shard_map/along_z/pallas_call | solution.py:191
  5.7 3.1 %collective-permute-start = (bf16[208,256]{1,0:T(8,128)(2,1)S(1)}, bf16[208,256]{1,0:T(8,128)(2,1)S(1)}, u32[]{:S(2)}, u32[]{:S(2)}) collective-permute-start(bf16[208,256]{1,0:T(8,128)(2,1)S(1)} %get-tuple-element.48), channel_id=1, source_target_pairs={{0,4},{4,0},{8,12},{12,8},{16,20},{20,16},{24,28},{28,24},{1,5},{5... | collective-permute-start | bytes 319496 | tf_op jit(solution)/shard_map/ppermute | solution.py:575
  8.8 1.5 %collective-permute-start.1 = (bf16[208,256]{1,0:T(8,128)(2,1)S(1)}, bf16[208,256]{1,0:T(8,128)(2,1)S(1)}, u32[]{:S(2)}, u32[]{:S(2)}) collective-permute-start(bf16[208,256]{1,0:T(8,128)(2,1)S(1)} %get-tuple-element.49), channel_id=1, source_target_pairs={{0,16},{4,20},{8,24},{12,28},{16,0},{20,4},{24,8},{28,12},{1,17},{... | collective-permute-start | bytes 319496 | tf_op jit(solution)/shard_map/ppermute | solution.py:575
  10.3 0.0 collective-permute-start.2
  10.3 2.0 %along_z.3 = (bf16[208,256]{1,0:T(8,128)(2,1)S(1)}, bf16[208,256]{1,0:T(8,128)(2,1)S(1)}, bf16[208,256]{1,0:T(8,128)(2,1)S(1)}, bf16[208,256]{1,0:T(8,128)(2,1)S(1)}) custom-call(s32[5]{0:T(128)S(1)} %stack.20.info_ref, bf16[32,256]{1,0:T(8,128)(2,1)S(1)} %copy-done.9, bf16[32,256,256]{2,1,0:T(8,128)(2,1)S(1)} %bitcast.19), custom_call_target="tpu_custom_call" | custom-call | flops 872415232 | bytes 4194304 | tf_op jit(solution)/shard_map/along_z/pallas_call | solution.py:191
  12.4 2.0 %collective-permute-start.3 = (bf16[208,256]{1,0:T(8,128)(2,1)S(1)}, bf16[208,256]{1,0:T(8,128)(2,1)S(1)}, u32[]{:S(2)}, u32[]{:S(2)}) collective-permute-start(bf16[208,256]{1,0:T(8,128)(2,1)S(1)} %get-tuple-element.55), channel_id=1, source_target_pairs={{0,4},{4,0},{8,12},{12,8},{16,20},{20,16},{24,28},{28,24},{1,5},{5... | collective-permute-start | bytes 319496 | tf_op jit(solution)/shard_map/ppermute | solution.py:575
  14.4 1.5 %collective-permute-start.4 = (bf16[208,256]{1,0:T(8,128)(2,1)S(1)}, bf16[208,256]{1,0:T(8,128)(2,1)S(1)}, u32[]{:S(2)}, u32[]{:S(2)}) collective-permute-start(bf16[208,256]{1,0:T(8,128)(2,1)S(1)} %get-tuple-element.56), channel_id=1, source_target_pairs={{0,16},{4,20},{8,24},{12,28},{16,0},{20,4},{24,8},{28,12},{1,17},{... | collective-permute-start | bytes 319496 | tf_op jit(solution)/shard_map/ppermute | solution.py:575
  15.9 0.1 collective-permute-start.5
  16.0 0.5 collective-permute-done.2.refs_3_
  16.5 2.5 %first_plane.1 = (f32[576,208]{1,0:T(8,128)S(1)}, bf16[4,2,576,512]{3,2,1,0:T(8,128)(2,1)S(1)}) custom-call(s32[5]{0:T(128)S(1)} %stack.20.info_ref, f32[576,512]{1,0:T(8,128)S(1)} %copy-done.13, f32[2,576,128]{2,1,0:T(8,128)S(1)} %copy-done.15, bf16[208,256]{1,0:T(8,128)(2,1)S(1)} %get-tuple-element.47.refs_0_, ...), custom_call_target="tpu_custom_call" | custom-call | flops 981467136 | bytes 1179648 | tf_op jit(solution)/shard_map/first_plane/pallas_call | solution.py:251
  19.1 1.1 %collective-permute-done.4.refs_2_ = bf16[208,256]{1,0:T(8,128)(2,1)S(1)} collective-permute-done((bf16[208,256]{1,0:T(8,128)(2,1)S(1)}, bf16[208,256]{1,0:T(8,128)(2,1)S(1)}, u32[]{:S(2)}, u32[]{:S(2)}) %collective-permute-start.4) | collective-permute-done | bytes 106528 | tf_op jit(solution)/shard_map/ppermute | solution.py:575
  20.2 1.4 %collective-permute-done.5.refs_3_ = bf16[208,256]{1,0:T(8,128)(2,1)S(1)} collective-permute-done((bf16[208,256]{1,0:T(8,128)(2,1)S(1)}, bf16[208,256]{1,0:T(8,128)(2,1)S(1)}, u32[]{:S(2)}, u32[]{:S(2)}) %collective-permute-start.5) | collective-permute-done | bytes 106528 | tf_op jit(solution)/shard_map/ppermute | solution.py:575
  21.6 2.2 %second_plane.1 = (bf16[240,128]{1,0:T(8,128)(2,1)S(1)}, bf16[240,128]{1,0:T(8,128)(2,1)S(1)}, bf16[240,128]{1,0:T(8,128)(2,1)S(1)}, bf16[240,128]{1,0:T(8,128)(...) custom-call(s32[5]{0:T(128)S(1)} %stack.20.info_ref, ...), custom_call_target="tpu_custom_call" | custom-call | flops 981467136 | bytes 4718592 | tf_op jit(solution)/shard_map/second_plane/pallas_call | solution.py:297
  23.8 0.4 collective-permute-start.10
  24.2 3.6 %collective-permute-start.11 = (bf16[240,128]{1,0:T(8,128)(2,1)S(1)}, bf16[240,128]{1,0:T(8,128)(2,1)S(1)}, u32[]{:S(2)}, u32[]{:S(2)}) collective-permute-start(bf16[240,128]{1,0:T(8,128)(2,1)S(1)} %get-tuple-element.64), channel_id=1, source_target_pairs={{0,24},{4,28},{8,16},{12,20},{16,8},{20,12},{24,0},{28,4},{1,25},{... | collective-permute-start | bytes 184328 | tf_op jit(solution)/shard_map/ppermute | solution.py:575
  27.8 1.3 %collective-permute-start.12 = (bf16[240,128]{1,0:T(8,128)(2,1)S(1)}, bf16[240,128]{1,0:T(8,128)(2,1)S(1)}, u32[]{:S(2)}, u32[]{:S(2)}) collective-permute-start(bf16[240,128]{1,0:T(8,128)(2,1)S(1)} %get-tuple-element.65), channel_id=1, source_target_pairs={{0,28},{4,24},{8,20},{12,16},{16,12},{20,8},{24,4},{28,0},{1,29},{... | collective-permute-start | bytes 184328 | tf_op jit(solution)/shard_map/ppermute | solution.py:575
  29.1 0.3 collective-permute-start.6
  29.3 2.8 %collective-permute-start.7 = (bf16[240,128]{1,0:T(8,128)(2,1)S(1)}, bf16[240,128]{1,0:T(8,128)(2,1)S(1)}, u32[]{:S(2)}, u32[]{:S(2)}) collective-permute-start(bf16[240,128]{1,0:T(8,128)(2,1)S(1)} %get-tuple-element.60), channel_id=1, source_target_pairs={{0,8},{4,12},{8,0},{12,4},{16,24},{20,28},{24,16},{28,20},{1,9},{5... | collective-permute-start | bytes 184328 | tf_op jit(solution)/shard_map/ppermute | solution.py:575
  32.1 1.3 %collective-permute-start.8 = (bf16[240,128]{1,0:T(8,128)(2,1)S(1)}, bf16[240,128]{1,0:T(8,128)(2,1)S(1)}, u32[]{:S(2)}, u32[]{:S(2)}) collective-permute-start(bf16[240,128]{1,0:T(8,128)(2,1)S(1)} %get-tuple-element.61), channel_id=1, source_target_pairs={{0,12},{4,8},{8,4},{12,0},{16,28},{20,24},{24,20},{28,16},{1,13},{... | collective-permute-start | bytes 184328 | tf_op jit(solution)/shard_map/ppermute | solution.py:575
  33.5 1.5 %collective-permute-start.9 = (bf16[240,128]{1,0:T(8,128)(2,1)S(1)}, bf16[240,128]{1,0:T(8,128)(2,1)S(1)}, u32[]{:S(2)}, u32[]{:S(2)}) collective-permute-start(bf16[240,128]{1,0:T(8,128)(2,1)S(1)} %get-tuple-element.62), channel_id=1, source_target_pairs={{0,16},{4,20},{8,24},{12,28},{16,0},{20,4},{24,8},{28,12},{1,17},{... | collective-permute-start | bytes 184328 | tf_op jit(solution)/shard_map/ppermute | solution.py:575
  35.0 5.3 %local.1.local_ref = bf16[16,512,256]{2,1,0:T(8,128)(2,1)S(1)} custom-call(bf16[512,32]{1,0:T(8,128)(2,1)S(1)} %copy-done.7, bf16[32,512]{1,0:T(8,128)(2,1)S(1)} %copy-done.10, bf16[32,32]{1,0:T(8,128)(2,1)S(1)} %copy-done.11, bf16[32,16,16,256]{3,2,1,0:T(8,128)(2,1)S(1)} %bitcast.15), custom_call_target="tpu_custom_call" | custom-call | flops 2147483648 | bytes 8388608 | tf_op jit(solution)/shard_map/local/pallas_call | solution.py:484
  40.3 0.0 copy-start.5
  40.3 0.0 copy-start.12
  40.3 0.0 copy-start.6
  40.4 1.2 %copy.24 = bf16[72,13,2,1024]{3,0,2,1:T(8,128)(2,1)S(1)} copy(bf16[72,13,2,1024]{3,2,1,0:T(2,128)(2,1)S(1)} %bitcast.22) | data formatting | bytes 7667712 | tf_op jit(solution)/shard_map/reshape | solution.py:640
  41.6 0.0 copy-start.14
  41.7 1.0 %total.1 = (bf16[9,72,128]{2,1,0:T(8,128)(2,1)S(1)}, bf16[9,72,128]{2,1,0:T(8,128)(2,1)S(1)}, bf16[9,72,128]{2,1,0:T(8,128)(2,1)S(1)}, bf16[9,72,128]{2,1,0:T(8,128)(2,1)S(1)}) custom-call(s32[5]{0:T(128)S(1)} %stack.20.info_ref, f32[2,512]{1,0:T(2,128)S(1)} %copy-done.12, bf16[512,512]{1,0:T(8,128)(2,1)S(1)} %copy-done.5, ...), custom_call_target="tpu_custom_call" | custom-call | flops 75497472 | bytes 491520 | tf_op jit(solution)/shard_map/total/pallas_call | solution.py:351
  42.7 0.0 slice-start
  42.7 2.2 %mix.1.refs_0_ = bf16[7,72,128]{2,1,0:T(8,128)(2,1)S(1)} custom-call(bf16[128,512]{1,0:T(8,128)(2,1)S(1)} %copy-done.8, bf16[1024,128]{1,0:T(8,128)(2,1)S(1)} %copy-done.6, bf16[13,2,72,1024]{3,2,1,0:T(8,128)(2,1)S(1)} %bitcast.16, bf16[9,72,128]{2,1,0:T(8,128)(2,1)S(1)} %get-tuple-element.76.s_ref.refs_0_), custom_call_target="tpu_custom_call" | custom-call | flops 528482304 | bytes 3833856 | tf_op jit(solution)/shard_map/mix/pallas_call | solution.py:400
  44.9 0.0 copy-start.3
  45.0 0.9 %collective-permute-start.14 = (bf16[7,72,128]{2,1,0:T(8,128)(2,1)S(1)}, bf16[7,72,128]{2,1,0:T(8,128)(2,1)S(1)}, u32[]{:S(2)}, u32[]{:S(2)}) collective-permute-start(bf16[7,72,128]{2,1,0:T(8,128)(2,1)S(1)} %mix.1.refs_0_), channel_id=1, source_target_pairs={{0,8},{4,12},{8,0},{12,4},{1,9},{5,13},{9,1},{13,5},{2,10},{6,14},... | collective-permute-start | bytes 387080 | tf_op jit(solution)/shard_map/ppermute | solution.py:575
  45.8 1.5 %collective-permute-start.21 = (bf16[9,72,128]{2,1,0:T(8,128)(2,1)S(1)}, bf16[9,72,128]{2,1,0:T(8,128)(2,1)S(1)}, u32[]{:S(2)}, u32[]{:S(2)}) collective-permute-start(bf16[9,72,128]{2,1,0:T(8,128)(2,1)S(1)} %get-tuple-element.81), channel_id=1, source_target_pairs={{0,2},{1,3},{2,0},{3,1},{4,6},{5,7},{6,4},{7,5},{8,10},{9,11},{10,... | collective-permute-start | bytes 497672 | tf_op jit(solution)/shard_map/ppermute | solution.py:575
  47.3 0.3 collective-permute-start.22
  47.7 3.4 %collective-permute-start.13 = (bf16[7,72,128]{2,1,0:T(8,128)(2,1)S(1)}, bf16[7,72,128]{2,1,0:T(8,128)(2,1)S(1)}, u32[]{:S(2)}, u32[]{:S(2)}) collective-permute-start(bf16[7,72,128]{2,1,0:T(8,128)(2,1)S(1)} %mix.1.refs_0_), channel_id=1, source_target_pairs={{0,4},{4,0},{8,12},{12,8},{1,5},{5,1},{9,13},{13,9},{2,6},{6,2},{1... | collective-permute-start | bytes 387080 | tf_op jit(solution)/shard_map/ppermute | solution.py:575
  51.1 1.2 %collective-permute-done.14.refs_2_ = bf16[7,72,128]{2,1,0:T(8,128)(2,1)S(1)} collective-permute-done((bf16[7,72,128]{2,1,0:T(8,128)(2,1)S(1)}, bf16[7,72,128]{2,1,0:T(8,128)(2,1)S(1)}, u32[]{:S(2)}, u32[]{:S(2)}) %collective-permute-start.14) | collective-permute-done | bytes 129056 | tf_op jit(solution)/shard_map/ppermute | solution.py:575
  52.3 3.0 %collective-permute-done.13.refs_1_ = bf16[7,72,128]{2,1,0:T(8,128)(2,1)S(1)} collective-permute-done((bf16[7,72,128]{2,1,0:T(8,128)(2,1)S(1)}, bf16[7,72,128]{2,1,0:T(8,128)(2,1)S(1)}, u32[]{:S(2)}, u32[]{:S(2)}) %collective-permute-start.13) | collective-permute-done | bytes 129056 | tf_op jit(solution)/shard_map/ppermute | solution.py:575
  55.3 0.7 collective-permute-start.16
  56.0 1.3 %collective-permute-start.18 = (bf16[7,72,128]{2,1,0:T(8,128)(2,1)S(1)}, bf16[7,72,128]{2,1,0:T(8,128)(2,1)S(1)}, u32[]{:S(2)}, u32[]{:S(2)}) collective-permute-start(bf16[7,72,128]{2,1,0:T(8,128)(2,1)S(1)} %collective-permute-done.14.refs_2_), channel_id=1, source_target_pairs={{0,16},{16,0},{1,17},{17,1},{2,18},{18,2},{3,19},{19,3},{4,20},{20... | collective-permute-start | bytes 387080 | tf_op jit(solution)/shard_map/ppermute | solution.py:575
  57.3 0.7 collective-permute-start.17
  58.0 1.3 %collective-permute-start.19 = (bf16[7,72,128]{2,1,0:T(8,128)(2,1)S(1)}, bf16[7,72,128]{2,1,0:T(8,128)(2,1)S(1)}, u32[]{:S(2)}, u32[]{:S(2)}) collective-permute-start(bf16[7,72,128]{2,1,0:T(8,128)(2,1)S(1)} %collective-permute-done.15.refs_3_), channel_id=1, source_target_pairs={{0,16},{16,0},{1,17},{17,1},{2,18},{18,2},{3,19},{19,3},{4,20},{20... | collective-permute-start | bytes 387080 | tf_op jit(solution)/shard_map/ppermute | solution.py:575
  59.3 1.8 %outer.1 = f32[13,2,72,256]{3,2,1,0:T(8,128)S(1)} custom-call(bf16[128,512]{1,0:T(8,128)(2,1)S(1)} %copy-done.8, bf16[8,128,512]{2,1,0:T(8,128)(2,1)S(1)} %copy-done.14, bf16[9,72,128]{2,1,0:T(8,128)(2,1)S(1)} %get-tuple-element.76.s_ref.refs_0_, bf16[9,72,128]{2,1,0:T(8,128)(2,1)S(1)} %collective-permute-done.20.refs_1_, ...), custom_call_target="tpu_custom_call" | custom-call | flops 1019215872 | bytes 5308416 | tf_op jit(solution)/shard_map/outer/pallas_call | solution.py:447
  61.2 2.2 %copy.22 = f32[72,13,2,256]{3,2,1,0:T(2,128)} copy(f32[72,13,2,256]{3,0,2,1:T(8,128)S(1)} %bitcast.20) | data formatting | bytes 3833856 | tf_op jit(solution)/shard_map/transpose | solution.py:667
  63.4 3.7 %collective-permute-done.17.refs_5_ = bf16[7,72,128]{2,1,0:T(8,128)(2,1)S(1)} collective-permute-done((bf16[7,72,128]{2,1,0:T(8,128)(2,1)S(1)}, bf16[7,72,128]{2,1,0:T(8,128)(2,1)S(1)}, u32[]{:S(2)}, u32[]{:S(2)}) %collective-permute-start.17) | collective-permute-done | bytes 129056 | tf_op jit(solution)/shard_map/ppermute | solution.py:575
  67.1 1.4 %collective-permute-done.19.refs_7_ = bf16[7,72,128]{2,1,0:T(8,128)(2,1)S(1)} collective-permute-done((bf16[7,72,128]{2,1,0:T(8,128)(2,1)S(1)}, bf16[7,72,128]{2,1,0:T(8,128)(2,1)S(1)}, u32[]{:S(2)}, u32[]{:S(2)}) %collective-permute-start.19) | collective-permute-done | bytes 129056 | tf_op jit(solution)/shard_map/ppermute | solution.py:575
  68.5 4.6 %inverse.1 = bf16[32,16,16,256]{3,2,1,0:T(8,128)(2,1)} custom-call(s32[5]{0:T(128)S(1)} %stack.20.info_ref, bf16[8,512,576]{2,1,0:T(8,128)(2,1)S(1)} %bitcast.18, bf16[896,1024]{1,0:T(8,128)(2,1)S(1)} %copy-done.3, bf16[256,1024]{1,0:T(8,128)(2,1)S(1)} %copy-done.4, bf16[16,512,256]{2,1,0:T(8,128)(2,1)S(1)} %local.1.local_ref, ...), custom_call_target="tpu_custom_call" | custom-call | flops 536870912 | bytes 8388608 | tf_op jit(solution)/shard_map/inverse/pallas_call | solution.py:555
  (49 shorter events, 0.1 us)
Async XLA Ops:
  0.8 2.2 %copy-start = (bf16[1,32,16,16,256]{4,3,2,1,0:T(8,128)(2,1)S(1)}, bf16[1,32,16,16,256]{4,3,2,1,0:T(8,128)(2,1)}, u32[]{:S(2)}) copy-start(bf16[1,32,16,16,256]{4,3,2,1,0:T(8,128)(2,1)} %param.18) | copy-start | bytes 12582916
  2.9 0.7 copy-start.9
  3.7 6.7 %copy-start.2 = (bf16[1,32,16,16,256]{4,3,2,1,0:T(8,128)(2,1)S(1)}, bf16[1,32,16,16,256]{4,3,2,1,0:T(8,128)(2,1)}, u32[]{:S(2)}) copy-start(bf16[1,32,16,16,256]{4,3,2,1,0:T(8,128)(2,1)} %param.17) | copy-start | bytes 12582916
  3.7 12.9 %copy-start.13 = (f32[576,512]{1,0:T(8,128)S(1)}, f32[576,512]{1,0:T(8,128)}, u32[]{:S(2)}) copy-start(f32[576,512]{1,0:T(8,128)} %constant.77.clone.base_ref) | copy-start | bytes 3538948
  3.7 12.9 %copy-start.15 = (f32[2,576,128]{2,1,0:T(8,128)S(1)}, f32[2,576,128]{2,1,0:T(8,128)}, u32[]{:S(2)}) copy-start(f32[2,576,128]{2,1,0:T(8,128)} %constant.78.clone.turn_ref) | copy-start | bytes 1769476
  5.7 10.2 %collective-permute-start = (bf16[208,256]{1,0:T(8,128)(2,1)S(1)}, bf16[208,256]{1,0:T(8,128)(2,1)S(1)}, u32[]{:S(2)}, u32[]{:S(2)}) collective-permute-start(bf16[208,256]{1,0:T(8,128)(2,1)S(1)} %get-tuple-element.48), channel_id=1, source_target_pairs={{0,4},{4,0},{8,12},{12,8},{16,20},{20,16},{24,28},{28,24},{1,5},{5... | collective-permute-start | bytes 319496 | tf_op jit(solution)/shard_map/ppermute | solution.py:575
  8.8 7.2 %collective-permute-start.1 = (bf16[208,256]{1,0:T(8,128)(2,1)S(1)}, bf16[208,256]{1,0:T(8,128)(2,1)S(1)}, u32[]{:S(2)}, u32[]{:S(2)}) collective-permute-start(bf16[208,256]{1,0:T(8,128)(2,1)S(1)} %get-tuple-element.49), channel_id=1, source_target_pairs={{0,16},{4,20},{8,24},{12,28},{16,0},{20,4},{24,8},{28,12},{1,17},{... | collective-permute-start | bytes 319496 | tf_op jit(solution)/shard_map/ppermute | solution.py:575
  10.3 6.2 %collective-permute-start.2 = (bf16[208,256]{1,0:T(8,128)(2,1)S(1)}, bf16[208,256]{1,0:T(8,128)(2,1)S(1)}, u32[]{:S(2)}, u32[]{:S(2)}) collective-permute-start(bf16[208,256]{1,0:T(8,128)(2,1)S(1)} %get-tuple-element.50), channel_id=1, source_target_pairs={{0,20},{4,16},{8,28},{12,24},{16,4},{20,0},{24,12},{28,8},{1,21},{... | collective-permute-start | bytes 319496 | tf_op jit(solution)/shard_map/ppermute | solution.py:575
  12.4 6.7 %collective-permute-start.3 = (bf16[208,256]{1,0:T(8,128)(2,1)S(1)}, bf16[208,256]{1,0:T(8,128)(2,1)S(1)}, u32[]{:S(2)}, u32[]{:S(2)}) collective-permute-start(bf16[208,256]{1,0:T(8,128)(2,1)S(1)} %get-tuple-element.55), channel_id=1, source_target_pairs={{0,4},{4,0},{8,12},{12,8},{16,20},{20,16},{24,28},{28,24},{1,5},{5... | collective-permute-start | bytes 319496 | tf_op jit(solution)/shard_map/ppermute | solution.py:575
  14.4 5.8 %collective-permute-start.4 = (bf16[208,256]{1,0:T(8,128)(2,1)S(1)}, bf16[208,256]{1,0:T(8,128)(2,1)S(1)}, u32[]{:S(2)}, u32[]{:S(2)}) collective-permute-start(bf16[208,256]{1,0:T(8,128)(2,1)S(1)} %get-tuple-element.56), channel_id=1, source_target_pairs={{0,16},{4,20},{8,24},{12,28},{16,0},{20,4},{24,8},{28,12},{1,17},{... | collective-permute-start | bytes 319496 | tf_op jit(solution)/shard_map/ppermute | solution.py:575
  15.9 19.1 %copy-start.1 = (bf16[1,32,16,16,256]{4,3,2,1,0:T(8,128)(2,1)S(1)}, bf16[1,32,16,16,256]{4,3,2,1,0:T(8,128)(2,1)}, u32[]{:S(2)}) copy-start(bf16[1,32,16,16,256]{4,3,2,1,0:T(8,128)(2,1)} %param.18) | copy-start | bytes 12582916
  15.9 19.1 %copy-start.7 = (bf16[512,32]{1,0:T(8,128)(2,1)S(1)}, bf16[512,32]{1,0:T(8,128)(2,1)}, u32[]{:S(2)}) copy-start(bf16[512,32]{1,0:T(8,128)(2,1)} %constant.87.clone.row_ref) | copy-start | bytes 98308
  15.9 19.1 %copy-start.10 = (bf16[32,512]{1,0:T(8,128)(2,1)S(1)}, bf16[32,512]{1,0:T(8,128)(2,1)}, u32[]{:S(2)}) copy-start(bf16[32,512]{1,0:T(8,128)(2,1)} %constant.88.clone.column_ref) | copy-start | bytes 98308
  15.9 19.1 %copy-start.11 = (bf16[32,32]{1,0:T(8,128)(2,1)S(1)}, bf16[32,32]{1,0:T(8,128)(2,1)}, u32[]{:S(2)}) copy-start(bf16[32,32]{1,0:T(8,128)(2,1)} %point_ref.1) | copy-start | bytes 6148
  15.9 5.7 %collective-permute-start.5 = (bf16[208,256]{1,0:T(8,128)(2,1)S(1)}, bf16[208,256]{1,0:T(8,128)(2,1)S(1)}, u32[]{:S(2)}, u32[]{:S(2)}) collective-permute-start(bf16[208,256]{1,0:T(8,128)(2,1)S(1)} %get-tuple-element.57), channel_id=1, source_target_pairs={{0,20},{4,16},{8,28},{12,24},{16,4},{20,0},{24,12},{28,8},{1,21},{... | collective-permute-start | bytes 319496 | tf_op jit(solution)/shard_map/ppermute | solution.py:575
  23.8 8.4 %collective-permute-start.10 = (bf16[240,128]{1,0:T(8,128)(2,1)S(1)}, bf16[240,128]{1,0:T(8,128)(2,1)S(1)}, u32[]{:S(2)}, u32[]{:S(2)}) collective-permute-start(bf16[240,128]{1,0:T(8,128)(2,1)S(1)} %get-tuple-element.63), channel_id=1, source_target_pairs={{0,20},{4,16},{8,28},{12,24},{16,4},{20,0},{24,12},{28,8},{1,21},{... | collective-permute-start | bytes 184328 | tf_op jit(solution)/shard_map/ppermute | solution.py:575
  24.2 9.3 %collective-permute-start.11 = (bf16[240,128]{1,0:T(8,128)(2,1)S(1)}, bf16[240,128]{1,0:T(8,128)(2,1)S(1)}, u32[]{:S(2)}, u32[]{:S(2)}) collective-permute-start(bf16[240,128]{1,0:T(8,128)(2,1)S(1)} %get-tuple-element.64), channel_id=1, source_target_pairs={{0,24},{4,28},{8,16},{12,20},{16,8},{20,12},{24,0},{28,4},{1,25},{... | collective-permute-start | bytes 184328 | tf_op jit(solution)/shard_map/ppermute | solution.py:575
  27.8 13.9 %collective-permute-start.12 = (bf16[240,128]{1,0:T(8,128)(2,1)S(1)}, bf16[240,128]{1,0:T(8,128)(2,1)S(1)}, u32[]{:S(2)}, u32[]{:S(2)}) collective-permute-start(bf16[240,128]{1,0:T(8,128)(2,1)S(1)} %get-tuple-element.65), channel_id=1, source_target_pairs={{0,28},{4,24},{8,20},{12,16},{16,12},{20,8},{24,4},{28,0},{1,29},{... | collective-permute-start | bytes 184328 | tf_op jit(solution)/shard_map/ppermute | solution.py:575
  29.1 12.5 %collective-permute-start.6 = (bf16[240,128]{1,0:T(8,128)(2,1)S(1)}, bf16[240,128]{1,0:T(8,128)(2,1)S(1)}, u32[]{:S(2)}, u32[]{:S(2)}) collective-permute-start(bf16[240,128]{1,0:T(8,128)(2,1)S(1)} %get-tuple-element.59), channel_id=1, source_target_pairs={{0,4},{4,0},{8,12},{12,8},{16,20},{20,16},{24,28},{28,24},{1,5},{5... | collective-permute-start | bytes 184328 | tf_op jit(solution)/shard_map/ppermute | solution.py:575
  29.3 12.3 %collective-permute-start.7 = (bf16[240,128]{1,0:T(8,128)(2,1)S(1)}, bf16[240,128]{1,0:T(8,128)(2,1)S(1)}, u32[]{:S(2)}, u32[]{:S(2)}) collective-permute-start(bf16[240,128]{1,0:T(8,128)(2,1)S(1)} %get-tuple-element.60), channel_id=1, source_target_pairs={{0,8},{4,12},{8,0},{12,4},{16,24},{20,28},{24,16},{28,20},{1,9},{5... | collective-permute-start | bytes 184328 | tf_op jit(solution)/shard_map/ppermute | solution.py:575
  32.1 9.5 %collective-permute-start.8 = (bf16[240,128]{1,0:T(8,128)(2,1)S(1)}, bf16[240,128]{1,0:T(8,128)(2,1)S(1)}, u32[]{:S(2)}, u32[]{:S(2)}) collective-permute-start(bf16[240,128]{1,0:T(8,128)(2,1)S(1)} %get-tuple-element.61), channel_id=1, source_target_pairs={{0,12},{4,8},{8,4},{12,0},{16,28},{20,24},{24,20},{28,16},{1,13},{... | collective-permute-start | bytes 184328 | tf_op jit(solution)/shard_map/ppermute | solution.py:575
  33.5 8.2 %collective-permute-start.9 = (bf16[240,128]{1,0:T(8,128)(2,1)S(1)}, bf16[240,128]{1,0:T(8,128)(2,1)S(1)}, u32[]{:S(2)}, u32[]{:S(2)}) collective-permute-start(bf16[240,128]{1,0:T(8,128)(2,1)S(1)} %get-tuple-element.62), channel_id=1, source_target_pairs={{0,16},{4,20},{8,24},{12,28},{16,0},{20,4},{24,8},{28,12},{1,17},{... | collective-permute-start | bytes 184328 | tf_op jit(solution)/shard_map/ppermute | solution.py:575
  35.0 5.3 %copy-start.16 = (bf16[12,6,13,2,1024]{4,3,2,1,0:T(2,128)(2,1)S(1)}, bf16[12,6,13,2,1024]{4,3,2,1,0:T(2,128)(2,1)}, u32[]{:S(2)}) copy-start(bf16[12,6,13,2,1024]{4,3,2,1,0:T(2,128)(2,1)} %param.19) | copy-start | bytes 11501572
  40.3 1.4 %copy-start.5 = (bf16[512,512]{1,0:T(8,128)(2,1)S(1)}, bf16[512,512]{1,0:T(8,128)(2,1)}, u32[]{:S(2)}) copy-start(bf16[512,512]{1,0:T(8,128)(2,1)} %constant.81.clone.regroup_ref) | copy-start | bytes 1572868
  40.3 1.4 %copy-start.12 = (f32[2,512]{1,0:T(2,128)S(1)}, f32[2,512]{1,0:T(2,128)}, u32[]{:S(2)}) copy-start(f32[2,512]{1,0:T(2,128)} %constant.89.clone.scale_ref) | copy-start | bytes 12292
  40.3 2.4 %copy-start.6 = (bf16[1024,128]{1,0:T(8,128)(2,1)S(1)}, bf16[1024,128]{1,0:T(8,128)(2,1)}, u32[]{:S(2)}) copy-start(bf16[1024,128]{1,0:T(8,128)(2,1)} %constant.85.clone.gather_ref) | copy-start | bytes 786436
  40.3 2.4 %copy-start.8 = (bf16[128,512]{1,0:T(8,128)(2,1)S(1)}, bf16[128,512]{1,0:T(8,128)(2,1)}, u32[]{:S(2)}) copy-start(bf16[128,512]{1,0:T(8,128)(2,1)} %constant.84.clone.spread_ref) | copy-start | bytes 393220
  41.6 17.7 %copy-start.14 = (bf16[8,128,512]{2,1,0:T(8,128)(2,1)S(1)}, bf16[8,128,512]{2,1,0:T(8,128)(2,1)}, u32[]{:S(2)}) copy-start(bf16[8,128,512]{2,1,0:T(8,128)(2,1)} %constant.86.clone.pick_ref) | copy-start | bytes 3145732
  42.7 25.8 %slice-start = ((s8[5242880]{0:T(1024)(128)(4,1)}), s8[1048576]{0:T(1024)(128)(4,1)S(1)}, s32[]{:S(2)}) async-start(s8[5242880]{0:T(1024)(128)(4,1)} %bitcast.17), calls=%async_computation | async-start | bytes 2097152
  44.9 23.6 %copy-start.3 = (bf16[896,1024]{1,0:T(8,128)(2,1)S(1)}, bf16[896,1024]{1,0:T(8,128)(2,1)}, u32[]{:S(2)}) copy-start(bf16[896,1024]{1,0:T(8,128)(2,1)} %constant.83.clone.order_ref) | copy-start | bytes 5505028
  44.9 23.6 %copy-start.4 = (bf16[256,1024]{1,0:T(8,128)(2,1)S(1)}, bf16[256,1024]{1,0:T(8,128)(2,1)}, u32[]{:S(2)}) copy-start(bf16[256,1024]{1,0:T(8,128)(2,1)} %constant.82.clone.z_ref) | copy-start | bytes 1572868
  45.0 7.3 %collective-permute-start.14 = (bf16[7,72,128]{2,1,0:T(8,128)(2,1)S(1)}, bf16[7,72,128]{2,1,0:T(8,128)(2,1)S(1)}, u32[]{:S(2)}, u32[]{:S(2)}) collective-permute-start(bf16[7,72,128]{2,1,0:T(8,128)(2,1)S(1)} %mix.1.refs_0_), channel_id=1, source_target_pairs={{0,8},{4,12},{8,0},{12,4},{1,9},{5,13},{9,1},{13,5},{2,10},{6,14},... | collective-permute-start | bytes 387080 | tf_op jit(solution)/shard_map/ppermute | solution.py:575
  45.8 22.7 %slice-start.1 = ((s8[5242880]{0:T(1024)(128)(4,1)}), s8[4194304]{0:T(1024)(128)(4,1)S(1)}, s32[]{:S(2)}) async-start(s8[5242880]{0:T(1024)(128)(4,1)} %bitcast.17), calls=%async_computation.1 | async-start | bytes 8388608
  45.8 10.1 %collective-permute-start.20 = (bf16[9,72,128]{2,1,0:T(8,128)(2,1)S(1)}, bf16[9,72,128]{2,1,0:T(8,128)(2,1)S(1)}, u32[]{:S(2)}, u32[]{:S(2)}) collective-permute-start(bf16[9,72,128]{2,1,0:T(8,128)(2,1)S(1)} %get-tuple-element.80), channel_id=1, source_target_pairs={{0,1},{1,0},{2,3},{3,2},{4,5},{5,4},{6,7},{7,6},{8,9},{9,8},{10,11... | collective-permute-start | bytes 497672 | tf_op jit(solution)/shard_map/ppermute | solution.py:575
  45.8 11.5 %collective-permute-start.21 = (bf16[9,72,128]{2,1,0:T(8,128)(2,1)S(1)}, bf16[9,72,128]{2,1,0:T(8,128)(2,1)S(1)}, u32[]{:S(2)}, u32[]{:S(2)}) collective-permute-start(bf16[9,72,128]{2,1,0:T(8,128)(2,1)S(1)} %get-tuple-element.81), channel_id=1, source_target_pairs={{0,2},{1,3},{2,0},{3,1},{4,6},{5,7},{6,4},{7,5},{8,10},{9,11},{10,... | collective-permute-start | bytes 497672 | tf_op jit(solution)/shard_map/ppermute | solution.py:575
  47.3 12.0 %collective-permute-start.22 = (bf16[9,72,128]{2,1,0:T(8,128)(2,1)S(1)}, bf16[9,72,128]{2,1,0:T(8,128)(2,1)S(1)}, u32[]{:S(2)}, u32[]{:S(2)}) collective-permute-start(bf16[9,72,128]{2,1,0:T(8,128)(2,1)S(1)} %get-tuple-element.82), channel_id=1, source_target_pairs={{0,3},{1,2},{2,1},{3,0},{4,7},{5,6},{6,5},{7,4},{8,11},{9,10},{10,... | collective-permute-start | bytes 497672 | tf_op jit(solution)/shard_map/ppermute | solution.py:575
  47.7 7.6 %collective-permute-start.13 = (bf16[7,72,128]{2,1,0:T(8,128)(2,1)S(1)}, bf16[7,72,128]{2,1,0:T(8,128)(2,1)S(1)}, u32[]{:S(2)}, u32[]{:S(2)}) collective-permute-start(bf16[7,72,128]{2,1,0:T(8,128)(2,1)S(1)} %mix.1.refs_0_), channel_id=1, source_target_pairs={{0,4},{4,0},{8,12},{12,8},{1,5},{5,1},{9,13},{13,9},{2,6},{6,2},{1... | collective-permute-start | bytes 387080 | tf_op jit(solution)/shard_map/ppermute | solution.py:575
  52.2 5.8 %collective-permute-start.15 = (bf16[7,72,128]{2,1,0:T(8,128)(2,1)S(1)}, bf16[7,72,128]{2,1,0:T(8,128)(2,1)S(1)}, u32[]{:S(2)}, u32[]{:S(2)}) collective-permute-start(bf16[7,72,128]{2,1,0:T(8,128)(2,1)S(1)} %collective-permute-done.14.refs_2_), channel_id=1, source_target_pairs={{0,4},{4,0},{8,12},{12,8},{1,5},{5,1},{9,13},{13,9},{2,6},{6,2},{1... | collective-permute-start | bytes 387080 | tf_op jit(solution)/shard_map/ppermute | solution.py:575
  55.3 8.1 %collective-permute-start.16 = (bf16[7,72,128]{2,1,0:T(8,128)(2,1)S(1)}, bf16[7,72,128]{2,1,0:T(8,128)(2,1)S(1)}, u32[]{:S(2)}, u32[]{:S(2)}) collective-permute-start(bf16[7,72,128]{2,1,0:T(8,128)(2,1)S(1)} %mix.1.refs_0_), channel_id=1, source_target_pairs={{0,16},{16,0},{1,17},{17,1},{2,18},{18,2},{3,19},{19,3},{4,20},{20... | collective-permute-start | bytes 387080 | tf_op jit(solution)/shard_map/ppermute | solution.py:575
  56.0 11.2 %collective-permute-start.18 = (bf16[7,72,128]{2,1,0:T(8,128)(2,1)S(1)}, bf16[7,72,128]{2,1,0:T(8,128)(2,1)S(1)}, u32[]{:S(2)}, u32[]{:S(2)}) collective-permute-start(bf16[7,72,128]{2,1,0:T(8,128)(2,1)S(1)} %collective-permute-done.14.refs_2_), channel_id=1, source_target_pairs={{0,16},{16,0},{1,17},{17,1},{2,18},{18,2},{3,19},{19,3},{4,20},{20... | collective-permute-start | bytes 387080 | tf_op jit(solution)/shard_map/ppermute | solution.py:575
  57.3 9.8 %collective-permute-start.17 = (bf16[7,72,128]{2,1,0:T(8,128)(2,1)S(1)}, bf16[7,72,128]{2,1,0:T(8,128)(2,1)S(1)}, u32[]{:S(2)}, u32[]{:S(2)}) collective-permute-start(bf16[7,72,128]{2,1,0:T(8,128)(2,1)S(1)} %collective-permute-done.13.refs_1_), channel_id=1, source_target_pairs={{0,16},{16,0},{1,17},{17,1},{2,18},{18,2},{3,19},{19,3},{4,20},{20... | collective-permute-start | bytes 387080 | tf_op jit(solution)/shard_map/ppermute | solution.py:575
  58.0 10.5 %collective-permute-start.19 = (bf16[7,72,128]{2,1,0:T(8,128)(2,1)S(1)}, bf16[7,72,128]{2,1,0:T(8,128)(2,1)S(1)}, u32[]{:S(2)}, u32[]{:S(2)}) collective-permute-start(bf16[7,72,128]{2,1,0:T(8,128)(2,1)S(1)} %collective-permute-done.15.refs_3_), channel_id=1, source_target_pairs={{0,16},{16,0},{1,17},{17,1},{2,18},{18,2},{3,19},{19,3},{4,20},{20... | collective-permute-start | bytes 387080 | tf_op jit(solution)/shard_map/ppermute | solution.py:575

commit v3 on v2

--- a/solution.py
+++ b/solution.py
@@ -79,18 +79,6 @@
     return r // groups_y % 2 * 2 + r % groups_y % 2
 
 
-def z_angles(length):
-    return angles(np, np.arange(MZ, dtype=np.int32), 2 * MZ, np.arange(length, dtype=np.int32), length)
-
-
-def forward_z_table(length):
-    theta = z_angles(length)
-    parts = np.stack([np.cos(theta), -np.sin(theta)], 1).reshape(2 * MZ, length)
-    table = np.zeros((-(-2 * MZ // 16) * 16, length), np.float32)
-    table[: 2 * MZ] = parts
-    return table.astype(BF16)
-
-
 def split16(values):
     high = values.astype(BF16)
     low = (values - high.astype(np.float32)).astype(BF16)
@@ -98,7 +86,8 @@
 
 
 def inverse_z_table(length, per_tile, slot, norm):
-    theta = z_angles(length)
+    modes, cells = np.arange(MZ, dtype=np.int32), np.arange(length, dtype=np.int32)
+    theta = angles(np, modes, 2 * MZ, cells, length)
     parts = np.stack([np.cos(theta), -np.sin(theta)], 0) * np.float32(norm)
     table = np.zeros((per_tile, 2, slot, per_tile, length), np.float32)
     for c in range(per_tile):
@@ -164,13 +153,17 @@
     return [pltpu.with_memory_space_constraint(a, pltpu.VMEM) for a in arrays]
 
 
-def along_z_kernel(info_ref, z_ref, x_ref, *rest):
+def along_z_kernel(info_ref, x_ref, *rest):
     outs, table = rest[:4], rest[4]
-    block, span, _ = table.shape
-    shape = (span, z_ref.shape[0])
-    row = lax.broadcasted_iota(jnp.int32, shape, 0) // block
-    repeat = (row == lax.broadcasted_iota(jnp.int32, shape, 1)).astype(jnp.bfloat16)
-    rows = jnp.dot(repeat, z_ref[...], preferred_element_type=jnp.float32)
+    block, span, length = table.shape
+    padded = -(-2 * MZ // 16) * 16
+    row = lax.broadcasted_iota(jnp.int32, (padded, length), 0)
+    cell = lax.broadcasted_iota(jnp.int32, (padded, length), 1)
+    theta = ((row // 2 * cell) % length).astype(jnp.float32) * (2.0 * math.pi / length)
+    parts = jnp.where(row % 2 == 0, jnp.cos(theta), -jnp.sin(theta))
+    row = lax.broadcasted_iota(jnp.int32, (span, padded), 0) // block
+    repeat = (row == lax.broadcasted_iota(jnp.int32, (span, padded), 1)).astype(jnp.bfloat16)
+    rows = jnp.dot(repeat, parts.astype(jnp.bfloat16), preferred_element_type=jnp.float32)
     channel = lax.broadcasted_iota(jnp.int32, rows.shape, 0) % block
     for c in range(block):
         table[c] = jnp.where(channel == c, rows, 0.0).astype(jnp.bfloat16)
@@ -185,13 +178,13 @@
         outs[t][...] = total.astype(jnp.bfloat16)
 
 
-def along_z(info, field, z_table, block):
+def along_z(info, field, block):
     channels, cells, length = field.shape
     span = 2 * MZ * block
     return pl.pallas_call(
         along_z_kernel,
         out_shape=[jax.ShapeDtypeStruct((span, cells), jnp.bfloat16)] * 4,
-        in_specs=[IN_SMEM] + [IN_VMEM] * 2,
+        in_specs=[IN_SMEM, IN_VMEM],
         out_specs=[IN_VMEM] * 4,
         scratch_shapes=[pltpu.VMEM((block, span, length), jnp.bfloat16)],
         compiler_params=params(12),
@@ -201,7 +194,7 @@
             transcendentals=0,
         ),
         name="along_z",
-    )(info, *resident(z_table, field))
+    )(info, *resident(field))
 
 
 def place_cells(info_ref, sources, block, data):
@@ -311,8 +304,9 @@
     )(info, *resident(table), other, *sources)
 
 
-def total_kernel(groups, groups_y, over, scale, info_ref, scale_ref, regroup_ref, *refs):
-    chunks, outs, held = refs[:groups], refs[groups:-1], refs[-1]
+def mix_kernel(groups, groups_y, over, scale, info_ref, *refs):
+    (scale_ref, regroup_ref), consts, refs = refs[:2], refs[2:5], refs[5:]
+    chunks, mode_ref, outs, held = refs[:groups], refs[groups], refs[groups + 1 : -1], refs[-1]
     rows = held.shape[2]
     parts = tail_parts(rows)
     room = LANES - over
@@ -344,28 +338,16 @@
         for j in range(2):
             value = held[jnp.bitwise_xor(info_ref[4], r), 2 + j] * scale
             out[tiles + j] = value.astype(jnp.bfloat16)
-
-
-def total(info, chunks, scale, norm, regroup, tiles, rows, over, scenes, groups_y):
-    out = jax.ShapeDtypeStruct((tiles + 2, rows, LANES), jnp.bfloat16)
-    return pl.pallas_call(
-        functools.partial(total_kernel, len(chunks), groups_y, over, norm),
-        out_shape=[out] * scenes,
-        in_specs=[IN_SMEM] + [IN_VMEM] * (2 + len(chunks)),
-        out_specs=[IN_VMEM] * scenes,
-        scratch_shapes=[pltpu.VMEM((4, 4, rows, LANES), jnp.float32)],
-        compiler_params=params(12),
-        cost_estimate=pl.CostEstimate(
-            flops=4 * rows * regroup.size,
-            bytes_accessed=2 * len(chunks) * chunks[0].size,
-            transcendentals=0,
-        ),
-        name="total",
-    )(info, *resident(scale, regroup), *chunks)
-
-
-def mix_kernel(spread_ref, gather_ref, w_ref, s_ref, out_ref):
-    tiles, rows, _ = out_ref.shape
+    mode_gradients(*consts, outs[0], mode_ref)
+
+
+def packed_rows(tiles, rows, used):
+    top = -(-rows // 16) * 8 if 2 * used <= LANES else rows
+    return top, (tiles - 1) * rows + top
+
+
+def mode_gradients(spread_ref, gather_ref, w_ref, s_ref, out_ref):
+    tiles, rows = s_ref.shape[0] - 2, s_ref.shape[1]
     last, _, _, width = w_ref.shape
     half = spread_ref.shape[1] // (2 * LANES)
     for tile in range(tiles):
@@ -392,27 +374,44 @@
         out = sums[:rows]
         for k in range(1, len(products)):
             out = jnp.where(which == k, sums[k * rows : (k + 1) * rows], out)
-        out_ref[tile] = jnp.where(which < len(products), out, 0.0).astype(jnp.bfloat16)
-
-
-def mix(spectra, weight, spread, gather):
-    tiles, rows = spectra.shape[0] - 2, spectra.shape[1]
-    return pl.pallas_call(
-        mix_kernel,
-        out_shape=jax.ShapeDtypeStruct((tiles, rows, LANES), jnp.bfloat16),
-        in_specs=[IN_VMEM] * 4,
-        out_specs=IN_VMEM,
-        compiler_params=params(16),
+        out = jnp.where(which < len(products), out, 0.0)
+        top = out_ref.shape[0] - (tiles - 1) * rows
+        if tile == tiles - 1 and top < rows:
+            lower = out[top:]
+            if 2 * top > rows:
+                zeros = jnp.zeros((2 * top - rows, LANES), jnp.float32)
+                lower = jnp.concatenate([lower, zeros], 0)
+            out = jnp.concatenate([out[:top, : LANES // 2], lower[:, : LANES // 2]], 1)
+        out_ref[tile * rows : tile * rows + out.shape[0]] = out.astype(jnp.bfloat16)
+
+
+def mix(info, chunks, scale, norm, regroup, spread, gather, weight, sizes):
+    tiles, rows, over, scenes, groups_y = sizes
+    half = spread.shape[1] // (2 * LANES)
+    used = (MZ - (tiles - 1) * half) * spread.shape[0] // half
+    out = jax.ShapeDtypeStruct((tiles + 2, rows, LANES), jnp.bfloat16)
+    modes = jax.ShapeDtypeStruct((packed_rows(tiles, rows, used)[1], LANES), jnp.bfloat16)
+    results = pl.pallas_call(
+        functools.partial(mix_kernel, len(chunks), groups_y, over, norm),
+        out_shape=[modes] + [out] * scenes,
+        in_specs=[IN_SMEM] + [IN_VMEM] * (5 + len(chunks)),
+        out_specs=[IN_VMEM] * (1 + scenes),
+        scratch_shapes=[pltpu.VMEM((4, 4, rows, LANES), jnp.float32)],
+        compiler_params=params(24),
         cost_estimate=pl.CostEstimate(
             flops=8 * tiles * rows * gather.size, bytes_accessed=2 * weight.size, transcendentals=0
         ),
         name="mix",
-    )(*resident(spread, gather, weight), spectra)
+    )(info, *resident(scale, regroup, spread, gather, weight), *chunks)
+    return results[0], results[1:]
 
 
 def outer_kernel(scenes, spread_ref, pick_ref, *refs):
     spectra, out_ref = refs[:scenes], refs[scenes]
-    last, _, rows, wide = out_ref.shape
+    rows = spectra[0].shape[1]
+    copies = pick_ref.shape[2] // (2 * LANES)
+    last = out_ref.shape[0] // (2 * copies * rows)
+    wide = copies * LANES
     half = spread_ref.shape[1] // (2 * LANES)
     per_tile = pick_ref.shape[0]
     tiles = spectra[0].shape[0] - 2
@@ -437,8 +436,9 @@
                 out_im = grads[here, lane + LANES : lane + 2 * LANES]
                 real += out_re * hat_re + out_im * hat_im
                 imag += out_im * hat_re - out_re * hat_im
-            out_ref[kz, 0, :, k * LANES : (k + 1) * LANES] = real
-            out_ref[kz, 1, :, k * LANES : (k + 1) * LANES] = imag
+            for part, value in enumerate((real, imag)):
+                first = (kz * copies + k) * 2 + part
+                out_ref[pl.ds(first, rows, stride=2 * copies * last), :] = value
 
 
 def outer(spectra, spread, pick):
@@ -446,7 +446,7 @@
     wide = pick.shape[2] // 2
     return pl.pallas_call(
         functools.partial(outer_kernel, len(spectra)),
-        out_shape=jax.ShapeDtypeStruct((MZ, 2, rows, wide), jnp.float32),
+        out_shape=jax.ShapeDtypeStruct((rows * MZ * wide // LANES * 2, LANES), jnp.float32),
         in_specs=[IN_VMEM] * (2 + len(spectra)),
         out_specs=IN_VMEM,
         compiler_params=params(16),
@@ -469,13 +469,14 @@
     column = lax.broadcasted_iota(jnp.int32, spread.shape, 1) % cells_y
     mixing[...] = jnp.where(row == column, spread, 0.0).astype(jnp.bfloat16)
 
-    @pl.loop(0, cells_x)
-    def _(x):
-        out_ref[x] = jnp.dot(
-            mixing[...],
-            grad_ref[:, x].reshape(channels * cells_y, length),
-            preferred_element_type=jnp.float32,
-        ).astype(out_ref.dtype)
+    @pl.loop(0, cells_x, step=4)
+    def _(start):
+        for x in range(4):
+            out_ref[start + x] = jnp.dot(
+                mixing[...],
+                grad_ref[:, start + x].reshape(channels * cells_y, length),
+                preferred_element_type=jnp.float32,
+            ).astype(out_ref.dtype)
 
 
 def local(cell_rows, cell_columns, point, grad):
@@ -498,12 +499,21 @@
 def inverse_kernel(groups, per_tile, here, info_ref, t_ref, order_ref, z_ref, local_ref, *refs):
     chunks, (out_ref, modes, held, built, sems) = refs[:groups], refs[groups:]
     channels, cells_x, cells_y, length = built.shape
-    rows = chunks[0].shape[1]
+    rows = modes.shape[0] // groups
     tiles = channels // per_tile
+    last = modes.shape[1] // LANES - 1
+    top = chunks[0].shape[0] - last * rows
     for r in range(groups):
         own = pl.ds(pl.multiple_of(jnp.bitwise_xor(info_ref[0], r) * rows, 8), rows)
-        for j in range(chunks[r].shape[0]):
-            modes[own, j * LANES : (j + 1) * LANES] = chunks[r][j].astype(jnp.float32)
+        for j in range(last):
+            value = chunks[r][j * rows : (j + 1) * rows]
+            modes[own, j * LANES : (j + 1) * LANES] = value.astype(jnp.float32)
+        value = chunks[r][last * rows :].astype(jnp.float32)
+        if top < rows:
+            middle = LANES // 2
+            value = jnp.concatenate([value[:, :middle], value[: rows - top, middle:]], 0)
+            value = jnp.concatenate([value, jnp.zeros_like(value)], 1)
+        modes[own, last * LANES :] = value
     sums = jnp.dot(
         t_ref[info_ref[3]], modes[...].astype(jnp.bfloat16), preferred_element_type=jnp.float32
     )
@@ -608,7 +618,6 @@
     forward_at = at_x // 2 * (groups_y // 2) + at_y // 2
     info = jnp.stack([me, quad, forward_at, inverse_at, lax.axis_index("scene")])
 
-    z_table = jnp.asarray(forward_z_table(cells_z))
     regroup = jnp.asarray(regroup_table(channels, block, half))
     inverse_z = jnp.asarray(inverse_z_table(cells_z, per_tile, slot, norm))
     order = jnp.asarray(order_table(channels, tiles * half, per_tile, slot))
@@ -626,7 +635,7 @@
     scale = jnp.asarray(scale.reshape(2, 4 * LANES))
 
     def cells_of(field):
-        mine = along_z(info, field.reshape(channels, cells, cells_z), z_table, block)
+        mine = along_z(info, field.reshape(channels, cells, cells_z), block)
         return [mine[0]] + [
             flip(mine[t], group_axes, groups, quad_offset(t, groups_y)) for t in range(1, 4)
         ]
@@ -636,7 +645,15 @@
     field_cells = cells_of(field)
     grad_sums, table = first_plane(info, grad_cells, base, turns, block)
     sums = second_plane(info, field_cells, table, grad_sums, groups, rows, block)
-    got = [sums[0]] + [flip(sums[r], group_axes, groups, r) for r in range(1, groups)]
+    got = {0: sums[0], 1: flip(sums[1], group_axes, groups, 1)}
+    far = [r for r in range(groups - 1, 1, -1) if r % groups_y >= groups_y // 2]
+    for r in far:
+        got[r] = flip(sums[r], group_axes, groups, r)
+    near = [r for r in range(2, groups) if r not in far]
+    waiting, _ = lax.optimization_barrier(([sums[r] for r in near], got[1]))
+    for r, value in zip(near, waiting):
+        got[r] = flip(value, group_axes, groups, r)
+    got = [got[r] for r in range(groups)]
     weight = spec_weight.reshape(modes, MZ, 2, channels * channels)
     weight = jnp.pad(weight.transpose(1, 2, 0, 3), ((0, 0), (0, 0), (0, rows - modes), (0, 0)))
     local_part = local(
@@ -647,27 +664,30 @@
     )
     got, weight, local_part = lax.optimization_barrier((got, weight, local_part))
     over = 2 * MZ * block - LANES
-    spectra = total(
-        info, got, scale, norm, regroup, tiles, rows, over, scenes, groups_y
-    )
-    mode_grad = mix(spectra[0], weight, spread, gather)
-
-    along_y = {0: mode_grad}
-    apart = groups_y // 2
-    while apart:
-        along_y.update({r ^ apart: flip(v, "gy", groups_y, apart) for r, v in along_y.items()})
-        apart //= 2
-    gathered = [along_y[r] for r in range(groups_y)]
+    mode_grad, spectra = mix(
+        info,
+        got,
+        scale,
+        norm,
+        regroup,
+        spread,
+        gather,
+        weight,
+        (tiles, rows, over, scenes, groups_y),
+    )
+
+    along_y = [mode_grad] + [None] * (groups_y - 1)
+    for r in range(groups_y - 1, 0, -1):
+        along_y[r] = flip(mode_grad, "gy", groups_y, r)
+    gathered = list(along_y)
     for r in range(1, groups_x):
-        gathered += [flip(m, "gx", groups_x, r) for m in gathered[:groups_y]]
-
-    others, _ = lax.optimization_barrier((spectra[1:], mode_grad))
-    spectra = [spectra[0]] + [flip(others[r - 1], "scene", scenes, r) for r in range(1, scenes)]
-    grads = outer(spectra, spread, pick)
-    grad_spec = grads[:, :, :modes].transpose(2, 0, 1, 3)
-    grad_spec = grad_spec.reshape(modes_xd, modes_yd, MZ, 2, here * channels)
-
-    gathered, grad_spec = lax.optimization_barrier((gathered, grad_spec))
+        gathered += [flip(value, "gx", groups_x, r) for value in along_y]
+
+    got, before = [spectra[0]], ()
+    for r in range(1, scenes):
+        value, before = lax.optimization_barrier((spectra[r], along_y[-1]))
+        got.append(flip(value, "scene", scenes, r))
+    spectra = got
     grad_field = inverse(
         info,
         gathered,
@@ -679,6 +699,13 @@
         per_tile,
         2,
     )
+    spectra, grad_field = lax.optimization_barrier((spectra, grad_field))
+    grads = outer(spectra, spread, pick)
+    grads = grads.reshape(rows, MZ, here * channels // LANES, 2, LANES)[:modes]
+    grad_spec = grads.transpose(0, 1, 3, 2, 4).reshape(
+        modes_xd, modes_yd, MZ, 2, here * channels
+    )
+
     return grad_field[None], grad_spec
 
 

time: 73.6 us -> 66.6 us (0.905)
  waiting for transfers between devices: 12.3 us -> 9.27 us
  local copies, waits for them, and re-layouts: 6.57 us -> 3.63 us
    ppermute x23, waiting for transfers between devices: 12.3 us -> 9.27 us  [flip(): return lax.ppermute(value, axes, [(i, i ^ r) for i in range(size)])]
    transpose x1 -> x0, local copies, waits for them, and re-layouts: 2.24 us -> none  [body(): grad_spec = grads[:, :, :modes].transpose(2, 0, 1, 3)]
    pallas_call x1, Pallas kernels: 5.28 us -> 3.41 us  [local(): pl.pallas_call(local_kernel, out_shape=jax.ShapeDtypeStruct((cells_x, wid...]
    pallas_call x1, Pallas kernels: 1.8 us -> 3.15 us  [outer(): pl.pallas_call(functools.partial(outer_kernel, len(spectra)), out_shape=j...]
    unnamed x38 -> x36, local copies, waits for them, and re-layouts: 3 us -> 2.28 us
    pallas_call x2 -> x1, Pallas kernels: 3.19 us -> 3.13 us  [mix(): pl.pallas_call(functools.partial(mix_kernel, len(chunks), groups_y, over,...]
  transfers between devices with their start and end apart: 23 -> 23, of which waited for: 7 -> 8; matrix products, arithmetic and copies ran while one was open for 5% -> 2% of each run, Pallas kernels for 16% -> 19%
where the time goes in v3:
time: 66.6 us; the launch traced here: 66.5 us
  starting transfers between devices  29.2 us (44%)
  Pallas kernels  23.5 us (35%)
  waiting for transfers between devices  9.27 us (14%)
  local copies, waits for them, and re-layouts  3.63 us (5%)
  between operations  0.96 us (1%)
    ppermute x23, starting transfers between devices, flip(): return lax.ppermute(value, axes, [(i, i ^ r) for i in range(size)])  29.2 us
    ppermute x23, waiting for transfers between devices, flip(): return lax.ppermute(value, axes, [(i, i ^ r) for i in range(size)])  9.27 us
    pallas_call x1, Pallas kernels, inverse(): pl.pallas_call(functools.partial(inverse_kernel, len(chunks), per_tile, h...  4.69 us
    pallas_call x2, Pallas kernels, along_z(): pl.pallas_call(along_z_kernel, out_shape=[jax.ShapeDtypeStruct((span, cel...  4.37 us
    pallas_call x1, Pallas kernels, local(): pl.pallas_call(local_kernel, out_shape=jax.ShapeDtypeStruct((cells_x, wid...  3.41 us
    pallas_call x1, Pallas kernels, outer(): pl.pallas_call(functools.partial(outer_kernel, len(spectra)), out_shape=j...  3.15 us
    pallas_call x1, Pallas kernels, mix(): pl.pallas_call(functools.partial(mix_kernel, len(chunks), groups_y, over,...  3.13 us
    pallas_call x1, Pallas kernels, first_plane(): pl.pallas_call(functools.partial(first_plane_kernel, block), out_shape=[j...  2.55 us
  transfers between devices with their start and end apart: 23, of which 8 were waited for; matrix products, arithmetic and copies ran while one was open for 2% of the time, Pallas kernels for 19%

profile of v3, /device:TPU:0, one launch (start us, length us, event | category | flops | bytes accessed | tf_op | source)
XLA Modules:
  0.0 66.5 jit_solution(6696532201963821362)
XLA Ops:
  0.7 0.1 stack.20.info_ref
  0.8 2.2 %copy-done = bf16[1,32,16,16,256]{4,3,2,1,0:T(8,128)(2,1)S(1)} copy-done((bf16[1,32,16,16,256]{4,3,2,1,0:T(8,128)(2,1)S(1)}, bf16[1,32,16,16,256]{4,3,2,1,0:T(8,128)(2,1)}, u32[]{:S(2)}) %copy-start) | copy-done | bytes 4194328
  2.9 2.2 %along_z.2 = (bf16[208,256]{1,0:T(8,128)(2,1)S(1)}, bf16[208,256]{1,0:T(8,128)(2,1)S(1)}, bf16[208,256]{1,0:T(8,128)(2,1)S(1)}, bf16[208,256]{1,0:T(8,128)(2,1)S(1)}) custom-call(s32[5]{0:T(128)S(1)} %stack.20.info_ref, bf16[32,256,256]{2,1,0:T(8,128)(2,1)S(1)} %bitcast.17), custom_call_target="tpu_custom_call" | custom-call | flops 872415232 | bytes 4194304 | tf_op jit(solution)/shard_map/along_z/pallas_call | solution.py:184
  5.1 3.1 %collective-permute-start = (bf16[208,256]{1,0:T(8,128)(2,1)S(1)}, bf16[208,256]{1,0:T(8,128)(2,1)S(1)}, u32[]{:S(2)}, u32[]{:S(2)}) collective-permute-start(bf16[208,256]{1,0:T(8,128)(2,1)S(1)} %get-tuple-element.47), channel_id=1, source_target_pairs={{0,4},{4,0},{8,12},{12,8},{16,20},{20,16},{24,28},{28,24},{1,5},{5... | collective-permute-start | bytes 319496 | tf_op jit(solution)/shard_map/ppermute | solution.py:585
  8.2 1.5 %collective-permute-start.1 = (bf16[208,256]{1,0:T(8,128)(2,1)S(1)}, bf16[208,256]{1,0:T(8,128)(2,1)S(1)}, u32[]{:S(2)}, u32[]{:S(2)}) collective-permute-start(bf16[208,256]{1,0:T(8,128)(2,1)S(1)} %get-tuple-element.48), channel_id=1, source_target_pairs={{0,16},{4,20},{8,24},{12,28},{16,0},{20,4},{24,8},{28,12},{1,17},{... | collective-permute-start | bytes 319496 | tf_op jit(solution)/shard_map/ppermute | solution.py:585
  9.7 0.1 collective-permute-start.2
  9.8 2.2 %along_z.3 = (bf16[208,256]{1,0:T(8,128)(2,1)S(1)}, bf16[208,256]{1,0:T(8,128)(2,1)S(1)}, bf16[208,256]{1,0:T(8,128)(2,1)S(1)}, bf16[208,256]{1,0:T(8,128)(2,1)S(1)}) custom-call(s32[5]{0:T(128)S(1)} %stack.20.info_ref, bf16[32,256,256]{2,1,0:T(8,128)(2,1)S(1)} %bitcast.22), custom_call_target="tpu_custom_call" | custom-call | flops 872415232 | bytes 4194304 | tf_op jit(solution)/shard_map/along_z/pallas_call | solution.py:184
  12.0 2.0 %collective-permute-start.3 = (bf16[208,256]{1,0:T(8,128)(2,1)S(1)}, bf16[208,256]{1,0:T(8,128)(2,1)S(1)}, u32[]{:S(2)}, u32[]{:S(2)}) collective-permute-start(bf16[208,256]{1,0:T(8,128)(2,1)S(1)} %get-tuple-element.54), channel_id=1, source_target_pairs={{0,4},{4,0},{8,12},{12,8},{16,20},{20,16},{24,28},{28,24},{1,5},{5... | collective-permute-start | bytes 319496 | tf_op jit(solution)/shard_map/ppermute | solution.py:585
  14.0 1.5 %collective-permute-start.4 = (bf16[208,256]{1,0:T(8,128)(2,1)S(1)}, bf16[208,256]{1,0:T(8,128)(2,1)S(1)}, u32[]{:S(2)}, u32[]{:S(2)}) collective-permute-start(bf16[208,256]{1,0:T(8,128)(2,1)S(1)} %get-tuple-element.55), channel_id=1, source_target_pairs={{0,16},{4,20},{8,24},{12,28},{16,0},{20,4},{24,8},{28,12},{1,17},{... | collective-permute-start | bytes 319496 | tf_op jit(solution)/shard_map/ppermute | solution.py:585
  15.5 0.1 collective-permute-start.5
  15.6 0.1 collective-permute-done.2.refs_3_
  15.8 2.5 %first_plane.1 = (f32[576,208]{1,0:T(8,128)S(1)}, bf16[4,2,576,512]{3,2,1,0:T(8,128)(2,1)S(1)}) custom-call(s32[5]{0:T(128)S(1)} %stack.20.info_ref, f32[576,512]{1,0:T(8,128)S(1)} %copy-done.12, f32[2,576,128]{2,1,0:T(8,128)S(1)} %copy-done.14, bf16[208,256]{1,0:T(8,128)(2,1)S(1)} %get-tuple-element.46.refs_0_, ...), custom_call_target="tpu_custom_call" | custom-call | flops 981467136 | bytes 1179648 | tf_op jit(solution)/shard_map/first_plane/pallas_call | solution.py:244
  18.3 1.5 %collective-permute-done.4.refs_2_ = bf16[208,256]{1,0:T(8,128)(2,1)S(1)} collective-permute-done((bf16[208,256]{1,0:T(8,128)(2,1)S(1)}, bf16[208,256]{1,0:T(8,128)(2,1)S(1)}, u32[]{:S(2)}, u32[]{:S(2)}) %collective-permute-start.4) | collective-permute-done | bytes 106528 | tf_op jit(solution)/shard_map/ppermute | solution.py:585
  19.8 1.4 %collective-permute-done.5.refs_3_ = bf16[208,256]{1,0:T(8,128)(2,1)S(1)} collective-permute-done((bf16[208,256]{1,0:T(8,128)(2,1)S(1)}, bf16[208,256]{1,0:T(8,128)(2,1)S(1)}, u32[]{:S(2)}, u32[]{:S(2)}) %collective-permute-start.5) | collective-permute-done | bytes 106528 | tf_op jit(solution)/shard_map/ppermute | solution.py:585
  21.2 2.2 %second_plane.1 = (bf16[240,128]{1,0:T(8,128)(2,1)S(1)}, bf16[240,128]{1,0:T(8,128)(2,1)S(1)}, bf16[240,128]{1,0:T(8,128)(2,1)S(1)}, bf16[240,128]{1,0:T(8,128)(...) custom-call(s32[5]{0:T(128)S(1)} %stack.20.info_ref, ...), custom_call_target="tpu_custom_call" | custom-call | flops 981467136 | bytes 4718592 | tf_op jit(solution)/shard_map/second_plane/pallas_call | solution.py:290
  23.3 0.5 collective-permute-start.6
  23.9 2.6 %collective-permute-start.7 = (bf16[240,128]{1,0:T(8,128)(2,1)S(1)}, bf16[240,128]{1,0:T(8,128)(2,1)S(1)}, u32[]{:S(2)}, u32[]{:S(2)}) collective-permute-start(bf16[240,128]{1,0:T(8,128)(2,1)S(1)} %get-tuple-element.59), channel_id=1, source_target_pairs={{0,8},{4,12},{8,0},{12,4},{16,24},{20,28},{24,16},{28,20},{1,9},{5... | collective-permute-start | bytes 184328 | tf_op jit(solution)/shard_map/ppermute | solution.py:585
  26.5 1.3 %collective-permute-start.8 = (bf16[240,128]{1,0:T(8,128)(2,1)S(1)}, bf16[240,128]{1,0:T(8,128)(2,1)S(1)}, u32[]{:S(2)}, u32[]{:S(2)}) collective-permute-start(bf16[240,128]{1,0:T(8,128)(2,1)S(1)} %get-tuple-element.60), channel_id=1, source_target_pairs={{0,12},{4,8},{8,4},{12,0},{16,28},{20,24},{24,20},{28,16},{1,13},{... | collective-permute-start | bytes 184328 | tf_op jit(solution)/shard_map/ppermute | solution.py:585
  27.8 1.9 %collective-permute-start.11 = (bf16[240,128]{1,0:T(8,128)(2,1)S(1)}, bf16[240,128]{1,0:T(8,128)(2,1)S(1)}, u32[]{:S(2)}, u32[]{:S(2)}) collective-permute-start(bf16[240,128]{1,0:T(8,128)(2,1)S(1)} %get-tuple-element.65), channel_id=1, source_target_pairs={{0,24},{4,28},{8,16},{12,20},{16,8},{20,12},{24,0},{28,4},{1,25},{... | collective-permute-start | bytes 184328 | tf_op jit(solution)/shard_map/ppermute | solution.py:585
  29.7 1.6 %collective-permute-start.12 = (bf16[240,128]{1,0:T(8,128)(2,1)S(1)}, bf16[240,128]{1,0:T(8,128)(2,1)S(1)}, u32[]{:S(2)}, u32[]{:S(2)}) collective-permute-start(bf16[240,128]{1,0:T(8,128)(2,1)S(1)} %get-tuple-element.66), channel_id=1, source_target_pairs={{0,28},{4,24},{8,20},{12,16},{16,12},{20,8},{24,4},{28,0},{1,29},{... | collective-permute-start | bytes 184328 | tf_op jit(solution)/shard_map/ppermute | solution.py:585
  31.3 0.8 %collective-permute-start.9 = (bf16[240,128]{1,0:T(8,128)(2,1)S(1)}, bf16[240,128]{1,0:T(8,128)(2,1)S(1)}, u32[]{:S(2)}, u32[]{:S(2)}) collective-permute-start(bf16[240,128]{1,0:T(8,128)(2,1)S(1)} %get-tuple-element.63), channel_id=1, source_target_pairs={{0,16},{4,20},{8,24},{12,28},{16,0},{20,4},{24,8},{28,12},{1,17},{... | collective-permute-start | bytes 184328 | tf_op jit(solution)/shard_map/ppermute | solution.py:585
  32.1 1.6 %collective-permute-start.10 = (bf16[240,128]{1,0:T(8,128)(2,1)S(1)}, bf16[240,128]{1,0:T(8,128)(2,1)S(1)}, u32[]{:S(2)}, u32[]{:S(2)}) collective-permute-start(bf16[240,128]{1,0:T(8,128)(2,1)S(1)} %get-tuple-element.64), channel_id=1, source_target_pairs={{0,20},{4,16},{8,28},{12,24},{16,4},{20,0},{24,12},{28,8},{1,21},{... | collective-permute-start | bytes 184328 | tf_op jit(solution)/shard_map/ppermute | solution.py:585
  33.7 3.4 %local.1.local_ref = bf16[16,512,256]{2,1,0:T(8,128)(2,1)S(1)} custom-call(bf16[512,32]{1,0:T(8,128)(2,1)S(1)} %copy-done.7, bf16[32,512]{1,0:T(8,128)(2,1)S(1)} %copy-done.9, bf16[32,32]{1,0:T(8,128)(2,1)S(1)} %copy-done.10, bf16[32,16,16,256]{3,2,1,0:T(8,128)(2,1)S(1)} %bitcast.18), custom_call_target="tpu_custom_call" | custom-call | flops 2147483648 | bytes 8388608 | tf_op jit(solution)/shard_map/local/pallas_call | solution.py:485
  37.1 0.0 copy-start.6
  37.1 0.0 copy-start.8
  37.1 0.0 copy-start.11
  37.1 0.0 slice-start
  37.2 0.0 slice-start.1
  37.2 1.3 %copy.23 = bf16[72,13,2,1024]{3,0,2,1:T(8,128)(2,1)S(1)} copy(bf16[72,13,2,1024]{3,2,1,0:T(2,128)(2,1)S(1)} %bitcast.24) | data formatting | bytes 7667712 | tf_op jit(solution)/shard_map/reshape | solution.py:657
  38.4 0.0 copy-start.3
  38.5 0.0 copy-start.4
  38.6 3.1 %mix.1 = (bf16[472,128]{1,0:T(8,128)(2,1)S(1)}, bf16[9,72,128]{2,1,0:T(8,128)(2,1)S(1)}, bf16[9,72,128]{2,1,0:T(8,128)(2,1)S(1)}, bf16[9,72,128]{2,1,0:T(8,128)(2,1)S(1)}, bf16[9,72,128]{2,1,0:T(8,128)(2,1)S(1)}) custom-call(s32[5]{0:T(128)S(1)} %stack.20.info_ref, f32[2,512]{1,0:T(2,128)S(1)} %copy-done.11, bf16[512,512]{1,0:T(8,128)(2,1)S(1)} %copy-done.5, ...), custom_call_target="tpu_custom_call" | custom-call | flops 528482304 | bytes 3833856 | tf_op jit(solution)/shard_map/mix/pallas_call | solution.py:394
  41.7 1.1 %collective-permute-start.17 = (bf16[472,128]{1,0:T(8,128)(2,1)S(1)}, bf16[472,128]{1,0:T(8,128)(2,1)S(1)}, u32[]{:S(2)}, u32[]{:S(2)}) collective-permute-start(bf16[472,128]{1,0:T(8,128)(2,1)S(1)} %get-tuple-element.78.refs_0_), channel_id=1, source_target_pairs={{0,4},{4,0},{8,12},{12,8},{1,5},{5,1},{9,13},{13,9},{2,6},{6,2},{1... | collective-permute-start | bytes 362504 | tf_op jit(solution)/shard_map/ppermute | solution.py:585
  42.8 2.4 %collective-permute-start.18 = (bf16[472,128]{1,0:T(8,128)(2,1)S(1)}, bf16[472,128]{1,0:T(8,128)(2,1)S(1)}, u32[]{:S(2)}, u32[]{:S(2)}) collective-permute-start(bf16[472,128]{1,0:T(8,128)(2,1)S(1)} %get-tuple-element.78.refs_0_), channel_id=1, source_target_pairs={{0,8},{4,12},{8,0},{12,4},{1,9},{5,13},{9,1},{13,5},{2,10},{6,14},... | collective-permute-start | bytes 362504 | tf_op jit(solution)/shard_map/ppermute | solution.py:585
  45.2 1.4 %collective-permute-start.13 = (bf16[472,128]{1,0:T(8,128)(2,1)S(1)}, bf16[472,128]{1,0:T(8,128)(2,1)S(1)}, u32[]{:S(2)}, u32[]{:S(2)}) collective-permute-start(bf16[472,128]{1,0:T(8,128)(2,1)S(1)} %get-tuple-element.78.refs_0_), channel_id=1, source_target_pairs={{0,12},{4,8},{8,4},{12,0},{1,13},{5,9},{9,5},{13,1},{2,14},{6,10},... | collective-permute-start | bytes 362504 | tf_op jit(solution)/shard_map/ppermute | solution.py:585
  46.6 0.8 %collective-permute-start.19 = (bf16[472,128]{1,0:T(8,128)(2,1)S(1)}, bf16[472,128]{1,0:T(8,128)(2,1)S(1)}, u32[]{:S(2)}, u32[]{:S(2)}) collective-permute-start(bf16[472,128]{1,0:T(8,128)(2,1)S(1)} %get-tuple-element.78.refs_0_), channel_id=1, source_target_pairs={{0,16},{16,0},{1,17},{17,1},{2,18},{18,2},{3,19},{19,3},{4,20},{20... | collective-permute-start | bytes 362504 | tf_op jit(solution)/shard_map/ppermute | solution.py:585
  47.4 0.5 collective-permute-done.17.refs_1_
  47.9 0.8 %collective-permute-start.20 = (bf16[472,128]{1,0:T(8,128)(2,1)S(1)}, bf16[472,128]{1,0:T(8,128)(2,1)S(1)}, u32[]{:S(2)}, u32[]{:S(2)}) collective-permute-start(bf16[472,128]{1,0:T(8,128)(2,1)S(1)} %collective-permute-done.17.refs_1_), channel_id=1, source_target_pairs={{0,16},{16,0},{1,17},{17,1},{2,18},{18,2},{3,19},{19,3},{4,20},{20... | collective-permute-start | bytes 362504 | tf_op jit(solution)/shard_map/ppermute | solution.py:585
  48.7 0.3 collective-permute-done.18.refs_2_
  49.0 0.9 %collective-permute-start.21 = (bf16[472,128]{1,0:T(8,128)(2,1)S(1)}, bf16[472,128]{1,0:T(8,128)(2,1)S(1)}, u32[]{:S(2)}, u32[]{:S(2)}) collective-permute-start(bf16[472,128]{1,0:T(8,128)(2,1)S(1)} %collective-permute-done.18.refs_2_), channel_id=1, source_target_pairs={{0,16},{16,0},{1,17},{17,1},{2,18},{18,2},{3,19},{19,3},{4,20},{20... | collective-permute-start | bytes 362504 | tf_op jit(solution)/shard_map/ppermute | solution.py:585
  49.9 2.2 %collective-permute-done.13.refs_3_ = bf16[472,128]{1,0:T(8,128)(2,1)S(1)} collective-permute-done((bf16[472,128]{1,0:T(8,128)(2,1)S(1)}, bf16[472,128]{1,0:T(8,128)(2,1)S(1)}, u32[]{:S(2)}, u32[]{:S(2)}) %collective-permute-start.13) | collective-permute-done | bytes 120864 | tf_op jit(solution)/shard_map/ppermute | solution.py:585
  52.1 0.8 %collective-permute-start.22 = (bf16[472,128]{1,0:T(8,128)(2,1)S(1)}, bf16[472,128]{1,0:T(8,128)(2,1)S(1)}, u32[]{:S(2)}, u32[]{:S(2)}) collective-permute-start(bf16[472,128]{1,0:T(8,128)(2,1)S(1)} %collective-permute-done.13.refs_3_), channel_id=1, source_target_pairs={{0,16},{16,0},{1,17},{17,1},{2,18},{18,2},{3,19},{19,3},{4,20},{20... | collective-permute-start | bytes 362504 | tf_op jit(solution)/shard_map/ppermute | solution.py:585
  52.9 2.3 %collective-permute-start.15 = (bf16[9,72,128]{2,1,0:T(8,128)(2,1)S(1)}, bf16[9,72,128]{2,1,0:T(8,128)(2,1)S(1)}, u32[]{:S(2)}, u32[]{:S(2)}) collective-permute-start(bf16[9,72,128]{2,1,0:T(8,128)(2,1)S(1)} %get-tuple-element.81), channel_id=1, source_target_pairs={{0,2},{1,3},{2,0},{3,1},{4,6},{5,7},{6,4},{7,5},{8,10},{9,11},{10,... | collective-permute-start | bytes 497672 | tf_op jit(solution)/shard_map/ppermute | solution.py:585
  55.2 0.1 collective-permute-start.16
  55.3 1.6 %collective-permute-done.22.refs_7_ = bf16[472,128]{1,0:T(8,128)(2,1)S(1)} collective-permute-done((bf16[472,128]{1,0:T(8,128)(2,1)S(1)}, bf16[472,128]{1,0:T(8,128)(2,1)S(1)}, u32[]{:S(2)}, u32[]{:S(2)}) %collective-permute-start.22) | collective-permute-done | bytes 120864 | tf_op jit(solution)/shard_map/ppermute | solution.py:585
  57.0 4.7 %inverse.1 = bf16[32,16,16,256]{3,2,1,0:T(8,128)(2,1)} custom-call(s32[5]{0:T(128)S(1)} %stack.20.info_ref, bf16[8,512,576]{2,1,0:T(8,128)(2,1)S(1)} %bitcast.21, bf16[896,1024]{1,0:T(8,128)(2,1)S(1)} %copy-done.3, bf16[256,1024]{1,0:T(8,128)(2,1)S(1)} %copy-done.4, bf16[16,512,256]{2,1,0:T(8,128)(2,1)S(1)} %local.1.local_ref, ...), custom_call_target="tpu_custom_call" | custom-call | flops 536870912 | bytes 8388608 | tf_op jit(solution)/shard_map/inverse/pallas_call | solution.py:565
  61.7 1.6 %collective-permute-done.16.refs_3_ = bf16[9,72,128]{2,1,0:T(8,128)(2,1)S(1)} collective-permute-done((bf16[9,72,128]{2,1,0:T(8,128)(2,1)S(1)}, bf16[9,72,128]{2,1,0:T(8,128)(2,1)S(1)}, u32[]{:S(2)}, u32[]{:S(2)}) %collective-permute-start.16) | collective-permute-done | bytes 165920 | tf_op jit(solution)/shard_map/ppermute | solution.py:585
  63.3 3.2 %outer.1 = f32[3744,128]{1,0:T(8,128)} custom-call(bf16[128,512]{1,0:T(8,128)(2,1)S(1)} %copy-done.8, bf16[8,128,512]{2,1,0:T(8,128)(2,1)S(1)} %copy-done.13, bf16[9,72,128]{2,1,0:T(8,128)(2,1)S(1)} %get-tuple-element.86.refs_0_, bf16[9,72,128]{2,1,0:T(8,128)(2,1)S(1)} %collective-permute-done.14.refs_1_, ...), custom_call_target="tpu_custom_call" | custom-call | flops 1019215872 | bytes 5308416 | tf_op jit(solution)/shard_map/outer/pallas_call | solution.py:447
  (45 shorter events, 0.1 us)
Async XLA Ops:
  0.8 2.2 %copy-start = (bf16[1,32,16,16,256]{4,3,2,1,0:T(8,128)(2,1)S(1)}, bf16[1,32,16,16,256]{4,3,2,1,0:T(8,128)(2,1)}, u32[]{:S(2)}) copy-start(bf16[1,32,16,16,256]{4,3,2,1,0:T(8,128)(2,1)} %param.17) | copy-start | bytes 12582916
  2.9 6.8 %copy-start.2 = (bf16[1,32,16,16,256]{4,3,2,1,0:T(8,128)(2,1)S(1)}, bf16[1,32,16,16,256]{4,3,2,1,0:T(8,128)(2,1)}, u32[]{:S(2)}) copy-start(bf16[1,32,16,16,256]{4,3,2,1,0:T(8,128)(2,1)} %param.16) | copy-start | bytes 12582916
  2.9 12.8 %copy-start.12 = (f32[576,512]{1,0:T(8,128)S(1)}, f32[576,512]{1,0:T(8,128)}, u32[]{:S(2)}) copy-start(f32[576,512]{1,0:T(8,128)} %constant.75.clone.base_ref) | copy-start | bytes 3538948
  2.9 12.8 %copy-start.14 = (f32[2,576,128]{2,1,0:T(8,128)S(1)}, f32[2,576,128]{2,1,0:T(8,128)}, u32[]{:S(2)}) copy-start(f32[2,576,128]{2,1,0:T(8,128)} %constant.76.clone.turn_ref) | copy-start | bytes 1769476
  5.1 10.3 %collective-permute-start = (bf16[208,256]{1,0:T(8,128)(2,1)S(1)}, bf16[208,256]{1,0:T(8,128)(2,1)S(1)}, u32[]{:S(2)}, u32[]{:S(2)}) collective-permute-start(bf16[208,256]{1,0:T(8,128)(2,1)S(1)} %get-tuple-element.47), channel_id=1, source_target_pairs={{0,4},{4,0},{8,12},{12,8},{16,20},{20,16},{24,28},{28,24},{1,5},{5... | collective-permute-start | bytes 319496 | tf_op jit(solution)/shard_map/ppermute | solution.py:585
  8.2 7.4 %collective-permute-start.1 = (bf16[208,256]{1,0:T(8,128)(2,1)S(1)}, bf16[208,256]{1,0:T(8,128)(2,1)S(1)}, u32[]{:S(2)}, u32[]{:S(2)}) collective-permute-start(bf16[208,256]{1,0:T(8,128)(2,1)S(1)} %get-tuple-element.48), channel_id=1, source_target_pairs={{0,16},{4,20},{8,24},{12,28},{16,0},{20,4},{24,8},{28,12},{1,17},{... | collective-permute-start | bytes 319496 | tf_op jit(solution)/shard_map/ppermute | solution.py:585
  9.7 6.0 %collective-permute-start.2 = (bf16[208,256]{1,0:T(8,128)(2,1)S(1)}, bf16[208,256]{1,0:T(8,128)(2,1)S(1)}, u32[]{:S(2)}, u32[]{:S(2)}) collective-permute-start(bf16[208,256]{1,0:T(8,128)(2,1)S(1)} %get-tuple-element.49), channel_id=1, source_target_pairs={{0,20},{4,16},{8,28},{12,24},{16,4},{20,0},{24,12},{28,8},{1,21},{... | collective-permute-start | bytes 319496 | tf_op jit(solution)/shard_map/ppermute | solution.py:585
  12.0 6.3 %collective-permute-start.3 = (bf16[208,256]{1,0:T(8,128)(2,1)S(1)}, bf16[208,256]{1,0:T(8,128)(2,1)S(1)}, u32[]{:S(2)}, u32[]{:S(2)}) collective-permute-start(bf16[208,256]{1,0:T(8,128)(2,1)S(1)} %get-tuple-element.54), channel_id=1, source_target_pairs={{0,4},{4,0},{8,12},{12,8},{16,20},{20,16},{24,28},{28,24},{1,5},{5... | collective-permute-start | bytes 319496 | tf_op jit(solution)/shard_map/ppermute | solution.py:585
  14.0 5.8 %collective-permute-start.4 = (bf16[208,256]{1,0:T(8,128)(2,1)S(1)}, bf16[208,256]{1,0:T(8,128)(2,1)S(1)}, u32[]{:S(2)}, u32[]{:S(2)}) collective-permute-start(bf16[208,256]{1,0:T(8,128)(2,1)S(1)} %get-tuple-element.55), channel_id=1, source_target_pairs={{0,16},{4,20},{8,24},{12,28},{16,0},{20,4},{24,8},{28,12},{1,17},{... | collective-permute-start | bytes 319496 | tf_op jit(solution)/shard_map/ppermute | solution.py:585
  15.5 18.2 %copy-start.1 = (bf16[1,32,16,16,256]{4,3,2,1,0:T(8,128)(2,1)S(1)}, bf16[1,32,16,16,256]{4,3,2,1,0:T(8,128)(2,1)}, u32[]{:S(2)}) copy-start(bf16[1,32,16,16,256]{4,3,2,1,0:T(8,128)(2,1)} %param.17) | copy-start | bytes 12582916
  15.5 18.2 %copy-start.7 = (bf16[512,32]{1,0:T(8,128)(2,1)S(1)}, bf16[512,32]{1,0:T(8,128)(2,1)}, u32[]{:S(2)}) copy-start(bf16[512,32]{1,0:T(8,128)(2,1)} %constant.84.clone.row_ref) | copy-start | bytes 98308
  15.5 18.2 %copy-start.9 = (bf16[32,512]{1,0:T(8,128)(2,1)S(1)}, bf16[32,512]{1,0:T(8,128)(2,1)}, u32[]{:S(2)}) copy-start(bf16[32,512]{1,0:T(8,128)(2,1)} %constant.85.clone.column_ref) | copy-start | bytes 98308
  15.5 18.2 %copy-start.10 = (bf16[32,32]{1,0:T(8,128)(2,1)S(1)}, bf16[32,32]{1,0:T(8,128)(2,1)}, u32[]{:S(2)}) copy-start(bf16[32,32]{1,0:T(8,128)(2,1)} %point_ref.1) | copy-start | bytes 6148
  15.5 5.7 %collective-permute-start.5 = (bf16[208,256]{1,0:T(8,128)(2,1)S(1)}, bf16[208,256]{1,0:T(8,128)(2,1)S(1)}, u32[]{:S(2)}, u32[]{:S(2)}) collective-permute-start(bf16[208,256]{1,0:T(8,128)(2,1)S(1)} %get-tuple-element.56), channel_id=1, source_target_pairs={{0,20},{4,16},{8,28},{12,24},{16,4},{20,0},{24,12},{28,8},{1,21},{... | collective-permute-start | bytes 319496 | tf_op jit(solution)/shard_map/ppermute | solution.py:585
  23.3 8.0 %collective-permute-start.6 = (bf16[240,128]{1,0:T(8,128)(2,1)S(1)}, bf16[240,128]{1,0:T(8,128)(2,1)S(1)}, u32[]{:S(2)}, u32[]{:S(2)}) collective-permute-start(bf16[240,128]{1,0:T(8,128)(2,1)S(1)} %get-tuple-element.58), channel_id=1, source_target_pairs={{0,4},{4,0},{8,12},{12,8},{16,20},{20,16},{24,28},{28,24},{1,5},{5... | collective-permute-start | bytes 184328 | tf_op jit(solution)/shard_map/ppermute | solution.py:585
  23.9 8.2 %collective-permute-start.7 = (bf16[240,128]{1,0:T(8,128)(2,1)S(1)}, bf16[240,128]{1,0:T(8,128)(2,1)S(1)}, u32[]{:S(2)}, u32[]{:S(2)}) collective-permute-start(bf16[240,128]{1,0:T(8,128)(2,1)S(1)} %get-tuple-element.59), channel_id=1, source_target_pairs={{0,8},{4,12},{8,0},{12,4},{16,24},{20,28},{24,16},{28,20},{1,9},{5... | collective-permute-start | bytes 184328 | tf_op jit(solution)/shard_map/ppermute | solution.py:585
  26.5 12.0 %collective-permute-start.8 = (bf16[240,128]{1,0:T(8,128)(2,1)S(1)}, bf16[240,128]{1,0:T(8,128)(2,1)S(1)}, u32[]{:S(2)}, u32[]{:S(2)}) collective-permute-start(bf16[240,128]{1,0:T(8,128)(2,1)S(1)} %get-tuple-element.60), channel_id=1, source_target_pairs={{0,12},{4,8},{8,4},{12,0},{16,28},{20,24},{24,20},{28,16},{1,13},{... | collective-permute-start | bytes 184328 | tf_op jit(solution)/shard_map/ppermute | solution.py:585
  27.8 10.7 %collective-permute-start.11 = (bf16[240,128]{1,0:T(8,128)(2,1)S(1)}, bf16[240,128]{1,0:T(8,128)(2,1)S(1)}, u32[]{:S(2)}, u32[]{:S(2)}) collective-permute-start(bf16[240,128]{1,0:T(8,128)(2,1)S(1)} %get-tuple-element.65), channel_id=1, source_target_pairs={{0,24},{4,28},{8,16},{12,20},{16,8},{20,12},{24,0},{28,4},{1,25},{... | collective-permute-start | bytes 184328 | tf_op jit(solution)/shard_map/ppermute | solution.py:585
  29.7 8.8 %collective-permute-start.12 = (bf16[240,128]{1,0:T(8,128)(2,1)S(1)}, bf16[240,128]{1,0:T(8,128)(2,1)S(1)}, u32[]{:S(2)}, u32[]{:S(2)}) collective-permute-start(bf16[240,128]{1,0:T(8,128)(2,1)S(1)} %get-tuple-element.66), channel_id=1, source_target_pairs={{0,28},{4,24},{8,20},{12,16},{16,12},{20,8},{24,4},{28,0},{1,29},{... | collective-permute-start | bytes 184328 | tf_op jit(solution)/shard_map/ppermute | solution.py:585
  31.3 7.2 %collective-permute-start.9 = (bf16[240,128]{1,0:T(8,128)(2,1)S(1)}, bf16[240,128]{1,0:T(8,128)(2,1)S(1)}, u32[]{:S(2)}, u32[]{:S(2)}) collective-permute-start(bf16[240,128]{1,0:T(8,128)(2,1)S(1)} %get-tuple-element.63), channel_id=1, source_target_pairs={{0,16},{4,20},{8,24},{12,28},{16,0},{20,4},{24,8},{28,12},{1,17},{... | collective-permute-start | bytes 184328 | tf_op jit(solution)/shard_map/ppermute | solution.py:585
  32.1 6.5 %collective-permute-start.10 = (bf16[240,128]{1,0:T(8,128)(2,1)S(1)}, bf16[240,128]{1,0:T(8,128)(2,1)S(1)}, u32[]{:S(2)}, u32[]{:S(2)}) collective-permute-start(bf16[240,128]{1,0:T(8,128)(2,1)S(1)} %get-tuple-element.64), channel_id=1, source_target_pairs={{0,20},{4,16},{8,28},{12,24},{16,4},{20,0},{24,12},{28,8},{1,21},{... | collective-permute-start | bytes 184328 | tf_op jit(solution)/shard_map/ppermute | solution.py:585
  33.7 3.5 %copy-start.15 = (bf16[12,6,13,2,1024]{4,3,2,1,0:T(2,128)(2,1)S(1)}, bf16[12,6,13,2,1024]{4,3,2,1,0:T(2,128)(2,1)}, u32[]{:S(2)}) copy-start(bf16[12,6,13,2,1024]{4,3,2,1,0:T(2,128)(2,1)} %param.18) | copy-start | bytes 11501572
  37.1 1.4 %copy-start.5 = (bf16[512,512]{1,0:T(8,128)(2,1)S(1)}, bf16[512,512]{1,0:T(8,128)(2,1)}, u32[]{:S(2)}) copy-start(bf16[512,512]{1,0:T(8,128)(2,1)} %constant.78.clone.refs_1_) | copy-start | bytes 1572868
  37.1 1.4 %copy-start.6 = (bf16[1024,128]{1,0:T(8,128)(2,1)S(1)}, bf16[1024,128]{1,0:T(8,128)(2,1)}, u32[]{:S(2)}) copy-start(bf16[1024,128]{1,0:T(8,128)(2,1)} %constant.82.clone.refs_3_) | copy-start | bytes 786436
  37.1 1.4 %copy-start.8 = (bf16[128,512]{1,0:T(8,128)(2,1)S(1)}, bf16[128,512]{1,0:T(8,128)(2,1)}, u32[]{:S(2)}) copy-start(bf16[128,512]{1,0:T(8,128)(2,1)} %constant.81.clone.refs_2_.spread_ref) | copy-start | bytes 393220
  37.1 1.4 %copy-start.11 = (f32[2,512]{1,0:T(2,128)S(1)}, f32[2,512]{1,0:T(2,128)}, u32[]{:S(2)}) copy-start(f32[2,512]{1,0:T(2,128)} %constant.86.clone.refs_0_) | copy-start | bytes 12292
  37.1 19.8 %slice-start = ((s8[5242880]{0:T(1024)(128)(4,1)}), s8[4194304]{0:T(1024)(128)(4,1)S(1)}, s32[]{:S(2)}) async-start(s8[5242880]{0:T(1024)(128)(4,1)} %bitcast.20), calls=%async_computation | async-start | bytes 8388608
  37.2 19.8 %slice-start.1 = ((s8[5242880]{0:T(1024)(128)(4,1)}), s8[1048576]{0:T(1024)(128)(4,1)S(1)}, s32[]{:S(2)}) async-start(s8[5242880]{0:T(1024)(128)(4,1)} %bitcast.20), calls=%async_computation.1 | async-start | bytes 2097152
  38.4 18.5 %copy-start.3 = (bf16[896,1024]{1,0:T(8,128)(2,1)S(1)}, bf16[896,1024]{1,0:T(8,128)(2,1)}, u32[]{:S(2)}) copy-start(bf16[896,1024]{1,0:T(8,128)(2,1)} %constant.80.clone.order_ref) | copy-start | bytes 5505028
  38.5 18.5 %copy-start.4 = (bf16[256,1024]{1,0:T(8,128)(2,1)S(1)}, bf16[256,1024]{1,0:T(8,128)(2,1)}, u32[]{:S(2)}) copy-start(bf16[256,1024]{1,0:T(8,128)(2,1)} %constant.79.clone.z_ref) | copy-start | bytes 1572868
  41.7 6.2 %collective-permute-start.17 = (bf16[472,128]{1,0:T(8,128)(2,1)S(1)}, bf16[472,128]{1,0:T(8,128)(2,1)S(1)}, u32[]{:S(2)}, u32[]{:S(2)}) collective-permute-start(bf16[472,128]{1,0:T(8,128)(2,1)S(1)} %get-tuple-element.78.refs_0_), channel_id=1, source_target_pairs={{0,4},{4,0},{8,12},{12,8},{1,5},{5,1},{9,13},{13,9},{2,6},{6,2},{1... | collective-permute-start | bytes 362504 | tf_op jit(solution)/shard_map/ppermute | solution.py:585
  42.8 6.1 %collective-permute-start.18 = (bf16[472,128]{1,0:T(8,128)(2,1)S(1)}, bf16[472,128]{1,0:T(8,128)(2,1)S(1)}, u32[]{:S(2)}, u32[]{:S(2)}) collective-permute-start(bf16[472,128]{1,0:T(8,128)(2,1)S(1)} %get-tuple-element.78.refs_0_), channel_id=1, source_target_pairs={{0,8},{4,12},{8,0},{12,4},{1,9},{5,13},{9,1},{13,5},{2,10},{6,14},... | collective-permute-start | bytes 362504 | tf_op jit(solution)/shard_map/ppermute | solution.py:585
  45.2 6.9 %collective-permute-start.13 = (bf16[472,128]{1,0:T(8,128)(2,1)S(1)}, bf16[472,128]{1,0:T(8,128)(2,1)S(1)}, u32[]{:S(2)}, u32[]{:S(2)}) collective-permute-start(bf16[472,128]{1,0:T(8,128)(2,1)S(1)} %get-tuple-element.78.refs_0_), channel_id=1, source_target_pairs={{0,12},{4,8},{8,4},{12,0},{1,13},{5,9},{9,5},{13,1},{2,14},{6,10},... | collective-permute-start | bytes 362504 | tf_op jit(solution)/shard_map/ppermute | solution.py:585
  46.6 6.3 %collective-permute-start.19 = (bf16[472,128]{1,0:T(8,128)(2,1)S(1)}, bf16[472,128]{1,0:T(8,128)(2,1)S(1)}, u32[]{:S(2)}, u32[]{:S(2)}) collective-permute-start(bf16[472,128]{1,0:T(8,128)(2,1)S(1)} %get-tuple-element.78.refs_0_), channel_id=1, source_target_pairs={{0,16},{16,0},{1,17},{17,1},{2,18},{18,2},{3,19},{19,3},{4,20},{20... | collective-permute-start | bytes 362504 | tf_op jit(solution)/shard_map/ppermute | solution.py:585
  47.9 7.3 %collective-permute-start.20 = (bf16[472,128]{1,0:T(8,128)(2,1)S(1)}, bf16[472,128]{1,0:T(8,128)(2,1)S(1)}, u32[]{:S(2)}, u32[]{:S(2)}) collective-permute-start(bf16[472,128]{1,0:T(8,128)(2,1)S(1)} %collective-permute-done.17.refs_1_), channel_id=1, source_target_pairs={{0,16},{16,0},{1,17},{17,1},{2,18},{18,2},{3,19},{19,3},{4,20},{20... | collective-permute-start | bytes 362504 | tf_op jit(solution)/shard_map/ppermute | solution.py:585
  49.0 6.4 %collective-permute-start.21 = (bf16[472,128]{1,0:T(8,128)(2,1)S(1)}, bf16[472,128]{1,0:T(8,128)(2,1)S(1)}, u32[]{:S(2)}, u32[]{:S(2)}) collective-permute-start(bf16[472,128]{1,0:T(8,128)(2,1)S(1)} %collective-permute-done.18.refs_2_), channel_id=1, source_target_pairs={{0,16},{16,0},{1,17},{17,1},{2,18},{18,2},{3,19},{19,3},{4,20},{20... | collective-permute-start | bytes 362504 | tf_op jit(solution)/shard_map/ppermute | solution.py:585
  52.1 4.9 %collective-permute-start.22 = (bf16[472,128]{1,0:T(8,128)(2,1)S(1)}, bf16[472,128]{1,0:T(8,128)(2,1)S(1)}, u32[]{:S(2)}, u32[]{:S(2)}) collective-permute-start(bf16[472,128]{1,0:T(8,128)(2,1)S(1)} %collective-permute-done.13.refs_3_), channel_id=1, source_target_pairs={{0,16},{16,0},{1,17},{17,1},{2,18},{18,2},{3,19},{19,3},{4,20},{20... | collective-permute-start | bytes 362504 | tf_op jit(solution)/shard_map/ppermute | solution.py:585
  52.9 8.8 %collective-permute-start.14 = (bf16[9,72,128]{2,1,0:T(8,128)(2,1)S(1)}, bf16[9,72,128]{2,1,0:T(8,128)(2,1)S(1)}, u32[]{:S(2)}, u32[]{:S(2)}) collective-permute-start(bf16[9,72,128]{2,1,0:T(8,128)(2,1)S(1)} %get-tuple-element.79), channel_id=1, source_target_pairs={{0,1},{1,0},{2,3},{3,2},{4,5},{5,4},{6,7},{7,6},{8,9},{9,8},{10,11... | collective-permute-start | bytes 497672 | tf_op jit(solution)/shard_map/ppermute | solution.py:585
  52.9 10.4 %copy-start.13 = (bf16[8,128,512]{2,1,0:T(8,128)(2,1)S(1)}, bf16[8,128,512]{2,1,0:T(8,128)(2,1)}, u32[]{:S(2)}) copy-start(bf16[8,128,512]{2,1,0:T(8,128)(2,1)} %constant.83.clone.pick_ref) | copy-start | bytes 3145732
  52.9 8.8 %collective-permute-start.15 = (bf16[9,72,128]{2,1,0:T(8,128)(2,1)S(1)}, bf16[9,72,128]{2,1,0:T(8,128)(2,1)S(1)}, u32[]{:S(2)}, u32[]{:S(2)}) collective-permute-start(bf16[9,72,128]{2,1,0:T(8,128)(2,1)S(1)} %get-tuple-element.81), channel_id=1, source_target_pairs={{0,2},{1,3},{2,0},{3,1},{4,6},{5,7},{6,4},{7,5},{8,10},{9,11},{10,... | collective-permute-start | bytes 497672 | tf_op jit(solution)/shard_map/ppermute | solution.py:585
  55.2 8.1 %collective-permute-start.16 = (bf16[9,72,128]{2,1,0:T(8,128)(2,1)S(1)}, bf16[9,72,128]{2,1,0:T(8,128)(2,1)S(1)}, u32[]{:S(2)}, u32[]{:S(2)}) collective-permute-start(bf16[9,72,128]{2,1,0:T(8,128)(2,1)S(1)} %get-tuple-element.83), channel_id=1, source_target_pairs={{0,3},{1,2},{2,1},{3,0},{4,7},{5,6},{6,5},{7,4},{8,11},{9,10},{10,... | collective-permute-start | bytes 497672 | tf_op jit(solution)/shard_map/ppermute | solution.py:585

commit v4 on v3

--- a/solution.py
+++ b/solution.py
@@ -681,11 +681,16 @@
         along_y[r] = flip(mode_grad, "gy", groups_y, r)
     gathered = list(along_y)
     for r in range(1, groups_x):
-        gathered += [flip(value, "gx", groups_x, r) for value in along_y]
-
-    got, before = [spectra[0]], ()
+        for k, value in enumerate(along_y):
+            if k == 1:
+                gathered.append(flip(mode_grad, group_axes, groups, r * groups_y + k))
+            else:
+                gathered.append(flip(value, "gx", groups_x, r))
+
+    got = [spectra[0]]
     for r in range(1, scenes):
-        value, before = lax.optimization_barrier((spectra[r], along_y[-1]))
+        after = mode_grad if r == 2 else along_y[1] if r == 3 else along_y[-1]
+        value, _ = lax.optimization_barrier((spectra[r], after))
         got.append(flip(value, "scene", scenes, r))
     spectra = got
     grad_field = inverse(

time: 66.6 us -> 64.8 us (0.973)
  waiting for transfers between devices: 9.27 us -> 7.41 us
    ppermute x23, waiting for transfers between devices: 9.27 us -> 7.41 us  [flip(): return lax.ppermute(value, axes, [(i, i ^ r) for i in range(size)])]
  transfers between devices with their start and end apart: 23 -> 23, of which waited for: 8 -> 6; matrix products, arithmetic and copies ran while one was open for 2% -> 2% of each run, Pallas kernels for 19% -> 20%
where the time goes in v4:
time: 64.8 us; the launch traced here: 64.6 us
  starting transfers between devices  29.3 us (45%)
  Pallas kernels  23.3 us (36%)
  waiting for transfers between devices  7.41 us (11%)
  local copies, waits for them, and re-layouts  3.63 us (6%)
  between operations  0.99 us (2%)
    ppermute x23, starting transfers between devices, flip(): return lax.ppermute(value, axes, [(i, i ^ r) for i in range(size)])  29.3 us
    ppermute x23, waiting for transfers between devices, flip(): return lax.ppermute(value, axes, [(i, i ^ r) for i in range(size)])  7.41 us
    pallas_call x1, Pallas kernels, inverse(): pl.pallas_call(functools.partial(inverse_kernel, len(chunks), per_tile, h...  4.69 us
    pallas_call x2, Pallas kernels, along_z(): pl.pallas_call(along_z_kernel, out_shape=[jax.ShapeDtypeStruct((span, cel...  4.37 us
    pallas_call x1, Pallas kernels, local(): pl.pallas_call(local_kernel, out_shape=jax.ShapeDtypeStruct((cells_x, wid...  3.41 us
    pallas_call x1, Pallas kernels, mix(): pl.pallas_call(functools.partial(mix_kernel, len(chunks), groups_y, over,...  3.13 us
    pallas_call x1, Pallas kernels, outer(): pl.pallas_call(functools.partial(outer_kernel, len(spectra)), out_shape=j...  3.03 us
    pallas_call x1, Pallas kernels, first_plane(): pl.pallas_call(functools.partial(first_plane_kernel, block), out_shape=[j...  2.55 us
  transfers between devices with their start and end apart: 23, of which 6 were waited for; matrix products, arithmetic and copies ran while one was open for 2% of the time, Pallas kernels for 20%

profile of v4, /device:TPU:0, one launch (start us, length us, event | category | flops | bytes accessed | tf_op | source)
XLA Modules:
  0.0 64.6 jit_solution(17711402841508658557)
XLA Ops:
  0.7 0.1 stack.20.info_ref
  0.8 2.2 %copy-done = bf16[1,32,16,16,256]{4,3,2,1,0:T(8,128)(2,1)S(1)} copy-done((bf16[1,32,16,16,256]{4,3,2,1,0:T(8,128)(2,1)S(1)}, bf16[1,32,16,16,256]{4,3,2,1,0:T(8,128)(2,1)}, u32[]{:S(2)}) %copy-start) | copy-done | bytes 4194328
  2.9 2.2 %along_z.2 = (bf16[208,256]{1,0:T(8,128)(2,1)S(1)}, bf16[208,256]{1,0:T(8,128)(2,1)S(1)}, bf16[208,256]{1,0:T(8,128)(2,1)S(1)}, bf16[208,256]{1,0:T(8,128)(2,1)S(1)}) custom-call(s32[5]{0:T(128)S(1)} %stack.20.info_ref, bf16[32,256,256]{2,1,0:T(8,128)(2,1)S(1)} %bitcast.17), custom_call_target="tpu_custom_call" | custom-call | flops 872415232 | bytes 4194304 | tf_op jit(solution)/shard_map/along_z/pallas_call | solution.py:184
  5.1 3.1 %collective-permute-start = (bf16[208,256]{1,0:T(8,128)(2,1)S(1)}, bf16[208,256]{1,0:T(8,128)(2,1)S(1)}, u32[]{:S(2)}, u32[]{:S(2)}) collective-permute-start(bf16[208,256]{1,0:T(8,128)(2,1)S(1)} %get-tuple-element.47), channel_id=1, source_target_pairs={{0,4},{4,0},{8,12},{12,8},{16,20},{20,16},{24,28},{28,24},{1,5},{5... | collective-permute-start | bytes 319496 | tf_op jit(solution)/shard_map/ppermute | solution.py:585
  8.2 1.5 %collective-permute-start.1 = (bf16[208,256]{1,0:T(8,128)(2,1)S(1)}, bf16[208,256]{1,0:T(8,128)(2,1)S(1)}, u32[]{:S(2)}, u32[]{:S(2)}) collective-permute-start(bf16[208,256]{1,0:T(8,128)(2,1)S(1)} %get-tuple-element.48), channel_id=1, source_target_pairs={{0,16},{4,20},{8,24},{12,28},{16,0},{20,4},{24,8},{28,12},{1,17},{... | collective-permute-start | bytes 319496 | tf_op jit(solution)/shard_map/ppermute | solution.py:585
  9.7 0.1 collective-permute-start.2
  9.8 2.2 %along_z.3 = (bf16[208,256]{1,0:T(8,128)(2,1)S(1)}, bf16[208,256]{1,0:T(8,128)(2,1)S(1)}, bf16[208,256]{1,0:T(8,128)(2,1)S(1)}, bf16[208,256]{1,0:T(8,128)(2,1)S(1)}) custom-call(s32[5]{0:T(128)S(1)} %stack.20.info_ref, bf16[32,256,256]{2,1,0:T(8,128)(2,1)S(1)} %bitcast.22), custom_call_target="tpu_custom_call" | custom-call | flops 872415232 | bytes 4194304 | tf_op jit(solution)/shard_map/along_z/pallas_call | solution.py:184
  12.0 2.0 %collective-permute-start.3 = (bf16[208,256]{1,0:T(8,128)(2,1)S(1)}, bf16[208,256]{1,0:T(8,128)(2,1)S(1)}, u32[]{:S(2)}, u32[]{:S(2)}) collective-permute-start(bf16[208,256]{1,0:T(8,128)(2,1)S(1)} %get-tuple-element.54), channel_id=1, source_target_pairs={{0,4},{4,0},{8,12},{12,8},{16,20},{20,16},{24,28},{28,24},{1,5},{5... | collective-permute-start | bytes 319496 | tf_op jit(solution)/shard_map/ppermute | solution.py:585
  14.0 1.5 %collective-permute-start.4 = (bf16[208,256]{1,0:T(8,128)(2,1)S(1)}, bf16[208,256]{1,0:T(8,128)(2,1)S(1)}, u32[]{:S(2)}, u32[]{:S(2)}) collective-permute-start(bf16[208,256]{1,0:T(8,128)(2,1)S(1)} %get-tuple-element.55), channel_id=1, source_target_pairs={{0,16},{4,20},{8,24},{12,28},{16,0},{20,4},{24,8},{28,12},{1,17},{... | collective-permute-start | bytes 319496 | tf_op jit(solution)/shard_map/ppermute | solution.py:585
  15.5 0.0 copy-start.10
  15.5 0.1 collective-permute-start.5
  15.6 0.1 collective-permute-done.2.refs_3_
  15.8 2.5 %first_plane.1 = (f32[576,208]{1,0:T(8,128)S(1)}, bf16[4,2,576,512]{3,2,1,0:T(8,128)(2,1)S(1)}) custom-call(s32[5]{0:T(128)S(1)} %stack.20.info_ref, f32[576,512]{1,0:T(8,128)S(1)} %copy-done.12, f32[2,576,128]{2,1,0:T(8,128)S(1)} %copy-done.14, bf16[208,256]{1,0:T(8,128)(2,1)S(1)} %get-tuple-element.46.refs_0_, ...), custom_call_target="tpu_custom_call" | custom-call | flops 981467136 | bytes 1179648 | tf_op jit(solution)/shard_map/first_plane/pallas_call | solution.py:244
  18.3 1.5 %collective-permute-done.4.refs_2_ = bf16[208,256]{1,0:T(8,128)(2,1)S(1)} collective-permute-done((bf16[208,256]{1,0:T(8,128)(2,1)S(1)}, bf16[208,256]{1,0:T(8,128)(2,1)S(1)}, u32[]{:S(2)}, u32[]{:S(2)}) %collective-permute-start.4) | collective-permute-done | bytes 106528 | tf_op jit(solution)/shard_map/ppermute | solution.py:585
  19.8 1.4 %collective-permute-done.5.refs_3_ = bf16[208,256]{1,0:T(8,128)(2,1)S(1)} collective-permute-done((bf16[208,256]{1,0:T(8,128)(2,1)S(1)}, bf16[208,256]{1,0:T(8,128)(2,1)S(1)}, u32[]{:S(2)}, u32[]{:S(2)}) %collective-permute-start.5) | collective-permute-done | bytes 106528 | tf_op jit(solution)/shard_map/ppermute | solution.py:585
  21.2 2.2 %second_plane.1 = (bf16[240,128]{1,0:T(8,128)(2,1)S(1)}, bf16[240,128]{1,0:T(8,128)(2,1)S(1)}, bf16[240,128]{1,0:T(8,128)(2,1)S(1)}, bf16[240,128]{1,0:T(8,128)(...) custom-call(s32[5]{0:T(128)S(1)} %stack.20.info_ref, ...), custom_call_target="tpu_custom_call" | custom-call | flops 981467136 | bytes 4718592 | tf_op jit(solution)/shard_map/second_plane/pallas_call | solution.py:290
  23.3 0.5 collective-permute-start.6
  23.9 2.6 %collective-permute-start.7 = (bf16[240,128]{1,0:T(8,128)(2,1)S(1)}, bf16[240,128]{1,0:T(8,128)(2,1)S(1)}, u32[]{:S(2)}, u32[]{:S(2)}) collective-permute-start(bf16[240,128]{1,0:T(8,128)(2,1)S(1)} %get-tuple-element.59), channel_id=1, source_target_pairs={{0,8},{4,12},{8,0},{12,4},{16,24},{20,28},{24,16},{28,20},{1,9},{5... | collective-permute-start | bytes 184328 | tf_op jit(solution)/shard_map/ppermute | solution.py:585
  26.5 1.3 %collective-permute-start.8 = (bf16[240,128]{1,0:T(8,128)(2,1)S(1)}, bf16[240,128]{1,0:T(8,128)(2,1)S(1)}, u32[]{:S(2)}, u32[]{:S(2)}) collective-permute-start(bf16[240,128]{1,0:T(8,128)(2,1)S(1)} %get-tuple-element.60), channel_id=1, source_target_pairs={{0,12},{4,8},{8,4},{12,0},{16,28},{20,24},{24,20},{28,16},{1,13},{... | collective-permute-start | bytes 184328 | tf_op jit(solution)/shard_map/ppermute | solution.py:585
  27.8 1.9 %collective-permute-start.11 = (bf16[240,128]{1,0:T(8,128)(2,1)S(1)}, bf16[240,128]{1,0:T(8,128)(2,1)S(1)}, u32[]{:S(2)}, u32[]{:S(2)}) collective-permute-start(bf16[240,128]{1,0:T(8,128)(2,1)S(1)} %get-tuple-element.65), channel_id=1, source_target_pairs={{0,24},{4,28},{8,16},{12,20},{16,8},{20,12},{24,0},{28,4},{1,25},{... | collective-permute-start | bytes 184328 | tf_op jit(solution)/shard_map/ppermute | solution.py:585
  29.7 1.6 %collective-permute-start.12 = (bf16[240,128]{1,0:T(8,128)(2,1)S(1)}, bf16[240,128]{1,0:T(8,128)(2,1)S(1)}, u32[]{:S(2)}, u32[]{:S(2)}) collective-permute-start(bf16[240,128]{1,0:T(8,128)(2,1)S(1)} %get-tuple-element.66), channel_id=1, source_target_pairs={{0,28},{4,24},{8,20},{12,16},{16,12},{20,8},{24,4},{28,0},{1,29},{... | collective-permute-start | bytes 184328 | tf_op jit(solution)/shard_map/ppermute | solution.py:585
  31.3 0.8 %collective-permute-start.9 = (bf16[240,128]{1,0:T(8,128)(2,1)S(1)}, bf16[240,128]{1,0:T(8,128)(2,1)S(1)}, u32[]{:S(2)}, u32[]{:S(2)}) collective-permute-start(bf16[240,128]{1,0:T(8,128)(2,1)S(1)} %get-tuple-element.63), channel_id=1, source_target_pairs={{0,16},{4,20},{8,24},{12,28},{16,0},{20,4},{24,8},{28,12},{1,17},{... | collective-permute-start | bytes 184328 | tf_op jit(solution)/shard_map/ppermute | solution.py:585
  32.1 1.6 %collective-permute-start.10 = (bf16[240,128]{1,0:T(8,128)(2,1)S(1)}, bf16[240,128]{1,0:T(8,128)(2,1)S(1)}, u32[]{:S(2)}, u32[]{:S(2)}) collective-permute-start(bf16[240,128]{1,0:T(8,128)(2,1)S(1)} %get-tuple-element.64), channel_id=1, source_target_pairs={{0,20},{4,16},{8,28},{12,24},{16,4},{20,0},{24,12},{28,8},{1,21},{... | collective-permute-start | bytes 184328 | tf_op jit(solution)/shard_map/ppermute | solution.py:585
  33.7 3.4 %local.1.local_ref = bf16[16,512,256]{2,1,0:T(8,128)(2,1)S(1)} custom-call(bf16[512,32]{1,0:T(8,128)(2,1)S(1)} %copy-done.7, bf16[32,512]{1,0:T(8,128)(2,1)S(1)} %copy-done.9, bf16[32,32]{1,0:T(8,128)(2,1)S(1)} %copy-done.10, bf16[32,16,16,256]{3,2,1,0:T(8,128)(2,1)S(1)} %bitcast.18), custom_call_target="tpu_custom_call" | custom-call | flops 2147483648 | bytes 8388608 | tf_op jit(solution)/shard_map/local/pallas_call | solution.py:485
  37.1 0.0 copy-start.5
  37.1 0.0 copy-start.6
  37.1 0.0 copy-start.8
  37.1 0.0 copy-start.11
  37.1 0.0 slice-start
  37.2 0.0 slice-start.1
  37.2 1.3 %copy.23 = bf16[72,13,2,1024]{3,0,2,1:T(8,128)(2,1)S(1)} copy(bf16[72,13,2,1024]{3,2,1,0:T(2,128)(2,1)S(1)} %bitcast.24) | data formatting | bytes 7667712 | tf_op jit(solution)/shard_map/reshape | solution.py:657
  38.4 0.0 copy-start.3
  38.5 0.0 copy-start.4
  38.6 3.1 %mix.1 = (bf16[472,128]{1,0:T(8,128)(2,1)S(1)}, bf16[9,72,128]{2,1,0:T(8,128)(2,1)S(1)}, bf16[9,72,128]{2,1,0:T(8,128)(2,1)S(1)}, bf16[9,72,128]{2,1,0:T(8,128)(2,1)S(1)}, bf16[9,72,128]{2,1,0:T(8,128)(2,1)S(1)}) custom-call(s32[5]{0:T(128)S(1)} %stack.20.info_ref, f32[2,512]{1,0:T(2,128)S(1)} %copy-done.11, bf16[512,512]{1,0:T(8,128)(2,1)S(1)} %copy-done.5, ...), custom_call_target="tpu_custom_call" | custom-call | flops 528482304 | bytes 3833856 | tf_op jit(solution)/shard_map/mix/pallas_call | solution.py:394
  41.7 3.4 %collective-permute-start.18 = (bf16[472,128]{1,0:T(8,128)(2,1)S(1)}, bf16[472,128]{1,0:T(8,128)(2,1)S(1)}, u32[]{:S(2)}, u32[]{:S(2)}) collective-permute-start(bf16[472,128]{1,0:T(8,128)(2,1)S(1)} %get-tuple-element.78.refs_0_), channel_id=1, source_target_pairs={{0,8},{4,12},{8,0},{12,4},{1,9},{5,13},{9,1},{13,5},{2,10},{6,14},... | collective-permute-start | bytes 362504 | tf_op jit(solution)/shard_map/ppermute | solution.py:585
  45.1 0.1 collective-permute-start.13
  45.2 0.6 collective-permute-start.16
  45.8 0.8 %collective-permute-start.19 = (bf16[472,128]{1,0:T(8,128)(2,1)S(1)}, bf16[472,128]{1,0:T(8,128)(2,1)S(1)}, u32[]{:S(2)}, u32[]{:S(2)}) collective-permute-start(bf16[472,128]{1,0:T(8,128)(2,1)S(1)} %get-tuple-element.78.refs_0_), channel_id=1, source_target_pairs={{0,16},{16,0},{1,17},{17,1},{2,18},{18,2},{3,19},{19,3},{4,20},{20... | collective-permute-start | bytes 362504 | tf_op jit(solution)/shard_map/ppermute | solution.py:585
  46.6 2.1 %collective-permute-start.20 = (bf16[472,128]{1,0:T(8,128)(2,1)S(1)}, bf16[472,128]{1,0:T(8,128)(2,1)S(1)}, u32[]{:S(2)}, u32[]{:S(2)}) collective-permute-start(bf16[472,128]{1,0:T(8,128)(2,1)S(1)} %get-tuple-element.78.refs_0_), channel_id=1, source_target_pairs={{0,20},{4,16},{8,28},{12,24},{16,4},{20,0},{24,12},{28,8},{1,21},{... | collective-permute-start | bytes 362504 | tf_op jit(solution)/shard_map/ppermute | solution.py:585
  48.7 0.4 collective-permute-done.18.refs_2_
  49.1 0.8 %collective-permute-start.21 = (bf16[472,128]{1,0:T(8,128)(2,1)S(1)}, bf16[472,128]{1,0:T(8,128)(2,1)S(1)}, u32[]{:S(2)}, u32[]{:S(2)}) collective-permute-start(bf16[472,128]{1,0:T(8,128)(2,1)S(1)} %collective-permute-done.18.refs_2_), channel_id=1, source_target_pairs={{0,16},{16,0},{1,17},{17,1},{2,18},{18,2},{3,19},{19,3},{4,20},{20... | collective-permute-start | bytes 362504 | tf_op jit(solution)/shard_map/ppermute | solution.py:585
  49.9 2.0 %collective-permute-done.13.refs_3_ = bf16[472,128]{1,0:T(8,128)(2,1)S(1)} collective-permute-done((bf16[472,128]{1,0:T(8,128)(2,1)S(1)}, bf16[472,128]{1,0:T(8,128)(2,1)S(1)}, u32[]{:S(2)}, u32[]{:S(2)}) %collective-permute-start.13) | collective-permute-done | bytes 120864 | tf_op jit(solution)/shard_map/ppermute | solution.py:585
  52.0 0.8 %collective-permute-start.22 = (bf16[472,128]{1,0:T(8,128)(2,1)S(1)}, bf16[472,128]{1,0:T(8,128)(2,1)S(1)}, u32[]{:S(2)}, u32[]{:S(2)}) collective-permute-start(bf16[472,128]{1,0:T(8,128)(2,1)S(1)} %collective-permute-done.13.refs_3_), channel_id=1, source_target_pairs={{0,16},{16,0},{1,17},{17,1},{2,18},{18,2},{3,19},{19,3},{4,20},{20... | collective-permute-start | bytes 362504 | tf_op jit(solution)/shard_map/ppermute | solution.py:585
  52.7 1.5 %collective-permute-start.15 = (bf16[9,72,128]{2,1,0:T(8,128)(2,1)S(1)}, bf16[9,72,128]{2,1,0:T(8,128)(2,1)S(1)}, u32[]{:S(2)}, u32[]{:S(2)}) collective-permute-start(bf16[9,72,128]{2,1,0:T(8,128)(2,1)S(1)} %get-tuple-element.81), channel_id=1, source_target_pairs={{0,2},{1,3},{2,0},{3,1},{4,6},{5,7},{6,4},{7,5},{8,10},{9,11},{10,... | collective-permute-start | bytes 497672 | tf_op jit(solution)/shard_map/ppermute | solution.py:585
  54.3 0.6 collective-permute-start.17
  54.9 1.9 %collective-permute-done.22.refs_7_ = bf16[472,128]{1,0:T(8,128)(2,1)S(1)} collective-permute-done((bf16[472,128]{1,0:T(8,128)(2,1)S(1)}, bf16[472,128]{1,0:T(8,128)(2,1)S(1)}, u32[]{:S(2)}, u32[]{:S(2)}) %collective-permute-start.22) | collective-permute-done | bytes 120864 | tf_op jit(solution)/shard_map/ppermute | solution.py:585
  56.8 4.7 %inverse.1 = bf16[32,16,16,256]{3,2,1,0:T(8,128)(2,1)} custom-call(s32[5]{0:T(128)S(1)} %stack.20.info_ref, bf16[8,512,576]{2,1,0:T(8,128)(2,1)S(1)} %bitcast.21, bf16[896,1024]{1,0:T(8,128)(2,1)S(1)} %copy-done.3, bf16[256,1024]{1,0:T(8,128)(2,1)S(1)} %copy-done.4, bf16[16,512,256]{2,1,0:T(8,128)(2,1)S(1)} %local.1.local_ref, ...), custom_call_target="tpu_custom_call" | custom-call | flops 536870912 | bytes 8388608 | tf_op jit(solution)/shard_map/inverse/pallas_call | solution.py:565
  61.6 3.0 %outer.1 = f32[3744,128]{1,0:T(8,128)} custom-call(bf16[128,512]{1,0:T(8,128)(2,1)S(1)} %copy-done.8, bf16[8,128,512]{2,1,0:T(8,128)(2,1)S(1)} %copy-done.13, bf16[9,72,128]{2,1,0:T(8,128)(2,1)S(1)} %get-tuple-element.86.refs_0_, bf16[9,72,128]{2,1,0:T(8,128)(2,1)S(1)} %collective-permute-done.14.refs_1_, ...), custom_call_target="tpu_custom_call" | custom-call | flops 1019215872 | bytes 5308416 | tf_op jit(solution)/shard_map/outer/pallas_call | solution.py:447
  (45 shorter events, 0.1 us)
Async XLA Ops:
  0.8 2.2 %copy-start = (bf16[1,32,16,16,256]{4,3,2,1,0:T(8,128)(2,1)S(1)}, bf16[1,32,16,16,256]{4,3,2,1,0:T(8,128)(2,1)}, u32[]{:S(2)}) copy-start(bf16[1,32,16,16,256]{4,3,2,1,0:T(8,128)(2,1)} %param.17) | copy-start | bytes 12582916
  2.9 6.8 %copy-start.2 = (bf16[1,32,16,16,256]{4,3,2,1,0:T(8,128)(2,1)S(1)}, bf16[1,32,16,16,256]{4,3,2,1,0:T(8,128)(2,1)}, u32[]{:S(2)}) copy-start(bf16[1,32,16,16,256]{4,3,2,1,0:T(8,128)(2,1)} %param.16) | copy-start | bytes 12582916
  2.9 12.8 %copy-start.12 = (f32[576,512]{1,0:T(8,128)S(1)}, f32[576,512]{1,0:T(8,128)}, u32[]{:S(2)}) copy-start(f32[576,512]{1,0:T(8,128)} %constant.75.clone.base_ref) | copy-start | bytes 3538948
  2.9 12.8 %copy-start.14 = (f32[2,576,128]{2,1,0:T(8,128)S(1)}, f32[2,576,128]{2,1,0:T(8,128)}, u32[]{:S(2)}) copy-start(f32[2,576,128]{2,1,0:T(8,128)} %constant.76.clone.turn_ref) | copy-start | bytes 1769476
  5.1 10.3 %collective-permute-start = (bf16[208,256]{1,0:T(8,128)(2,1)S(1)}, bf16[208,256]{1,0:T(8,128)(2,1)S(1)}, u32[]{:S(2)}, u32[]{:S(2)}) collective-permute-start(bf16[208,256]{1,0:T(8,128)(2,1)S(1)} %get-tuple-element.47), channel_id=1, source_target_pairs={{0,4},{4,0},{8,12},{12,8},{16,20},{20,16},{24,28},{28,24},{1,5},{5... | collective-permute-start | bytes 319496 | tf_op jit(solution)/shard_map/ppermute | solution.py:585
  8.2 7.4 %collective-permute-start.1 = (bf16[208,256]{1,0:T(8,128)(2,1)S(1)}, bf16[208,256]{1,0:T(8,128)(2,1)S(1)}, u32[]{:S(2)}, u32[]{:S(2)}) collective-permute-start(bf16[208,256]{1,0:T(8,128)(2,1)S(1)} %get-tuple-element.48), channel_id=1, source_target_pairs={{0,16},{4,20},{8,24},{12,28},{16,0},{20,4},{24,8},{28,12},{1,17},{... | collective-permute-start | bytes 319496 | tf_op jit(solution)/shard_map/ppermute | solution.py:585
  9.7 6.0 %collective-permute-start.2 = (bf16[208,256]{1,0:T(8,128)(2,1)S(1)}, bf16[208,256]{1,0:T(8,128)(2,1)S(1)}, u32[]{:S(2)}, u32[]{:S(2)}) collective-permute-start(bf16[208,256]{1,0:T(8,128)(2,1)S(1)} %get-tuple-element.49), channel_id=1, source_target_pairs={{0,20},{4,16},{8,28},{12,24},{16,4},{20,0},{24,12},{28,8},{1,21},{... | collective-permute-start | bytes 319496 | tf_op jit(solution)/shard_map/ppermute | solution.py:585
  12.0 6.3 %collective-permute-start.3 = (bf16[208,256]{1,0:T(8,128)(2,1)S(1)}, bf16[208,256]{1,0:T(8,128)(2,1)S(1)}, u32[]{:S(2)}, u32[]{:S(2)}) collective-permute-start(bf16[208,256]{1,0:T(8,128)(2,1)S(1)} %get-tuple-element.54), channel_id=1, source_target_pairs={{0,4},{4,0},{8,12},{12,8},{16,20},{20,16},{24,28},{28,24},{1,5},{5... | collective-permute-start | bytes 319496 | tf_op jit(solution)/shard_map/ppermute | solution.py:585
  14.0 5.8 %collective-permute-start.4 = (bf16[208,256]{1,0:T(8,128)(2,1)S(1)}, bf16[208,256]{1,0:T(8,128)(2,1)S(1)}, u32[]{:S(2)}, u32[]{:S(2)}) collective-permute-start(bf16[208,256]{1,0:T(8,128)(2,1)S(1)} %get-tuple-element.55), channel_id=1, source_target_pairs={{0,16},{4,20},{8,24},{12,28},{16,0},{20,4},{24,8},{28,12},{1,17},{... | collective-permute-start | bytes 319496 | tf_op jit(solution)/shard_map/ppermute | solution.py:585
  15.5 18.2 %copy-start.1 = (bf16[1,32,16,16,256]{4,3,2,1,0:T(8,128)(2,1)S(1)}, bf16[1,32,16,16,256]{4,3,2,1,0:T(8,128)(2,1)}, u32[]{:S(2)}) copy-start(bf16[1,32,16,16,256]{4,3,2,1,0:T(8,128)(2,1)} %param.17) | copy-start | bytes 12582916
  15.5 18.2 %copy-start.7 = (bf16[512,32]{1,0:T(8,128)(2,1)S(1)}, bf16[512,32]{1,0:T(8,128)(2,1)}, u32[]{:S(2)}) copy-start(bf16[512,32]{1,0:T(8,128)(2,1)} %constant.84.clone.row_ref) | copy-start | bytes 98308
  15.5 18.2 %copy-start.9 = (bf16[32,512]{1,0:T(8,128)(2,1)S(1)}, bf16[32,512]{1,0:T(8,128)(2,1)}, u32[]{:S(2)}) copy-start(bf16[32,512]{1,0:T(8,128)(2,1)} %constant.85.clone.column_ref) | copy-start | bytes 98308
  15.5 18.2 %copy-start.10 = (bf16[32,32]{1,0:T(8,128)(2,1)S(1)}, bf16[32,32]{1,0:T(8,128)(2,1)}, u32[]{:S(2)}) copy-start(bf16[32,32]{1,0:T(8,128)(2,1)} %point_ref.1) | copy-start | bytes 6148
  15.5 5.7 %collective-permute-start.5 = (bf16[208,256]{1,0:T(8,128)(2,1)S(1)}, bf16[208,256]{1,0:T(8,128)(2,1)S(1)}, u32[]{:S(2)}, u32[]{:S(2)}) collective-permute-start(bf16[208,256]{1,0:T(8,128)(2,1)S(1)} %get-tuple-element.56), channel_id=1, source_target_pairs={{0,20},{4,16},{8,28},{12,24},{16,4},{20,0},{24,12},{28,8},{1,21},{... | collective-permute-start | bytes 319496 | tf_op jit(solution)/shard_map/ppermute | solution.py:585
  23.3 8.0 %collective-permute-start.6 = (bf16[240,128]{1,0:T(8,128)(2,1)S(1)}, bf16[240,128]{1,0:T(8,128)(2,1)S(1)}, u32[]{:S(2)}, u32[]{:S(2)}) collective-permute-start(bf16[240,128]{1,0:T(8,128)(2,1)S(1)} %get-tuple-element.58), channel_id=1, source_target_pairs={{0,4},{4,0},{8,12},{12,8},{16,20},{20,16},{24,28},{28,24},{1,5},{5... | collective-permute-start | bytes 184328 | tf_op jit(solution)/shard_map/ppermute | solution.py:585
  23.9 8.2 %collective-permute-start.7 = (bf16[240,128]{1,0:T(8,128)(2,1)S(1)}, bf16[240,128]{1,0:T(8,128)(2,1)S(1)}, u32[]{:S(2)}, u32[]{:S(2)}) collective-permute-start(bf16[240,128]{1,0:T(8,128)(2,1)S(1)} %get-tuple-element.59), channel_id=1, source_target_pairs={{0,8},{4,12},{8,0},{12,4},{16,24},{20,28},{24,16},{28,20},{1,9},{5... | collective-permute-start | bytes 184328 | tf_op jit(solution)/shard_map/ppermute | solution.py:585
  26.5 12.0 %collective-permute-start.8 = (bf16[240,128]{1,0:T(8,128)(2,1)S(1)}, bf16[240,128]{1,0:T(8,128)(2,1)S(1)}, u32[]{:S(2)}, u32[]{:S(2)}) collective-permute-start(bf16[240,128]{1,0:T(8,128)(2,1)S(1)} %get-tuple-element.60), channel_id=1, source_target_pairs={{0,12},{4,8},{8,4},{12,0},{16,28},{20,24},{24,20},{28,16},{1,13},{... | collective-permute-start | bytes 184328 | tf_op jit(solution)/shard_map/ppermute | solution.py:585
  27.8 10.7 %collective-permute-start.11 = (bf16[240,128]{1,0:T(8,128)(2,1)S(1)}, bf16[240,128]{1,0:T(8,128)(2,1)S(1)}, u32[]{:S(2)}, u32[]{:S(2)}) collective-permute-start(bf16[240,128]{1,0:T(8,128)(2,1)S(1)} %get-tuple-element.65), channel_id=1, source_target_pairs={{0,24},{4,28},{8,16},{12,20},{16,8},{20,12},{24,0},{28,4},{1,25},{... | collective-permute-start | bytes 184328 | tf_op jit(solution)/shard_map/ppermute | solution.py:585
  29.7 8.8 %collective-permute-start.12 = (bf16[240,128]{1,0:T(8,128)(2,1)S(1)}, bf16[240,128]{1,0:T(8,128)(2,1)S(1)}, u32[]{:S(2)}, u32[]{:S(2)}) collective-permute-start(bf16[240,128]{1,0:T(8,128)(2,1)S(1)} %get-tuple-element.66), channel_id=1, source_target_pairs={{0,28},{4,24},{8,20},{12,16},{16,12},{20,8},{24,4},{28,0},{1,29},{... | collective-permute-start | bytes 184328 | tf_op jit(solution)/shard_map/ppermute | solution.py:585
  31.3 7.2 %collective-permute-start.9 = (bf16[240,128]{1,0:T(8,128)(2,1)S(1)}, bf16[240,128]{1,0:T(8,128)(2,1)S(1)}, u32[]{:S(2)}, u32[]{:S(2)}) collective-permute-start(bf16[240,128]{1,0:T(8,128)(2,1)S(1)} %get-tuple-element.63), channel_id=1, source_target_pairs={{0,16},{4,20},{8,24},{12,28},{16,0},{20,4},{24,8},{28,12},{1,17},{... | collective-permute-start | bytes 184328 | tf_op jit(solution)/shard_map/ppermute | solution.py:585
  32.1 6.5 %collective-permute-start.10 = (bf16[240,128]{1,0:T(8,128)(2,1)S(1)}, bf16[240,128]{1,0:T(8,128)(2,1)S(1)}, u32[]{:S(2)}, u32[]{:S(2)}) collective-permute-start(bf16[240,128]{1,0:T(8,128)(2,1)S(1)} %get-tuple-element.64), channel_id=1, source_target_pairs={{0,20},{4,16},{8,28},{12,24},{16,4},{20,0},{24,12},{28,8},{1,21},{... | collective-permute-start | bytes 184328 | tf_op jit(solution)/shard_map/ppermute | solution.py:585
  33.7 3.5 %copy-start.15 = (bf16[12,6,13,2,1024]{4,3,2,1,0:T(2,128)(2,1)S(1)}, bf16[12,6,13,2,1024]{4,3,2,1,0:T(2,128)(2,1)}, u32[]{:S(2)}) copy-start(bf16[12,6,13,2,1024]{4,3,2,1,0:T(2,128)(2,1)} %param.18) | copy-start | bytes 11501572
  37.1 1.4 %copy-start.5 = (bf16[512,512]{1,0:T(8,128)(2,1)S(1)}, bf16[512,512]{1,0:T(8,128)(2,1)}, u32[]{:S(2)}) copy-start(bf16[512,512]{1,0:T(8,128)(2,1)} %constant.78.clone.refs_1_) | copy-start | bytes 1572868
  37.1 1.4 %copy-start.6 = (bf16[1024,128]{1,0:T(8,128)(2,1)S(1)}, bf16[1024,128]{1,0:T(8,128)(2,1)}, u32[]{:S(2)}) copy-start(bf16[1024,128]{1,0:T(8,128)(2,1)} %constant.82.clone.refs_3_) | copy-start | bytes 786436
  37.1 1.4 %copy-start.8 = (bf16[128,512]{1,0:T(8,128)(2,1)S(1)}, bf16[128,512]{1,0:T(8,128)(2,1)}, u32[]{:S(2)}) copy-start(bf16[128,512]{1,0:T(8,128)(2,1)} %constant.81.clone.refs_2_.spread_ref) | copy-start | bytes 393220
  37.1 1.4 %copy-start.11 = (f32[2,512]{1,0:T(2,128)S(1)}, f32[2,512]{1,0:T(2,128)}, u32[]{:S(2)}) copy-start(f32[2,512]{1,0:T(2,128)} %constant.86.clone.refs_0_) | copy-start | bytes 12292
  37.1 19.7 %slice-start = ((s8[5242880]{0:T(1024)(128)(4,1)}), s8[4194304]{0:T(1024)(128)(4,1)S(1)}, s32[]{:S(2)}) async-start(s8[5242880]{0:T(1024)(128)(4,1)} %bitcast.20), calls=%async_computation | async-start | bytes 8388608
  37.2 19.7 %slice-start.1 = ((s8[5242880]{0:T(1024)(128)(4,1)}), s8[1048576]{0:T(1024)(128)(4,1)S(1)}, s32[]{:S(2)}) async-start(s8[5242880]{0:T(1024)(128)(4,1)} %bitcast.20), calls=%async_computation.1 | async-start | bytes 2097152
  38.4 18.4 %copy-start.3 = (bf16[896,1024]{1,0:T(8,128)(2,1)S(1)}, bf16[896,1024]{1,0:T(8,128)(2,1)}, u32[]{:S(2)}) copy-start(bf16[896,1024]{1,0:T(8,128)(2,1)} %constant.80.clone.order_ref) | copy-start | bytes 5505028
  38.5 18.4 %copy-start.4 = (bf16[256,1024]{1,0:T(8,128)(2,1)S(1)}, bf16[256,1024]{1,0:T(8,128)(2,1)}, u32[]{:S(2)}) copy-start(bf16[256,1024]{1,0:T(8,128)(2,1)} %constant.79.clone.z_ref) | copy-start | bytes 1572868
  41.7 7.4 %collective-permute-start.18 = (bf16[472,128]{1,0:T(8,128)(2,1)S(1)}, bf16[472,128]{1,0:T(8,128)(2,1)S(1)}, u32[]{:S(2)}, u32[]{:S(2)}) collective-permute-start(bf16[472,128]{1,0:T(8,128)(2,1)S(1)} %get-tuple-element.78.refs_0_), channel_id=1, source_target_pairs={{0,8},{4,12},{8,0},{12,4},{1,9},{5,13},{9,1},{13,5},{2,10},{6,14},... | collective-permute-start | bytes 362504 | tf_op jit(solution)/shard_map/ppermute | solution.py:585
  45.1 6.8 %collective-permute-start.13 = (bf16[472,128]{1,0:T(8,128)(2,1)S(1)}, bf16[472,128]{1,0:T(8,128)(2,1)S(1)}, u32[]{:S(2)}, u32[]{:S(2)}) collective-permute-start(bf16[472,128]{1,0:T(8,128)(2,1)S(1)} %get-tuple-element.78.refs_0_), channel_id=1, source_target_pairs={{0,12},{4,8},{8,4},{12,0},{1,13},{5,9},{9,5},{13,1},{2,14},{6,10},... | collective-permute-start | bytes 362504 | tf_op jit(solution)/shard_map/ppermute | solution.py:585
  45.2 7.5 %collective-permute-start.16 = (bf16[472,128]{1,0:T(8,128)(2,1)S(1)}, bf16[472,128]{1,0:T(8,128)(2,1)S(1)}, u32[]{:S(2)}, u32[]{:S(2)}) collective-permute-start(bf16[472,128]{1,0:T(8,128)(2,1)S(1)} %get-tuple-element.78.refs_0_), channel_id=1, source_target_pairs={{0,4},{4,0},{8,12},{12,8},{1,5},{5,1},{9,13},{13,9},{2,6},{6,2},{1... | collective-permute-start | bytes 362504 | tf_op jit(solution)/shard_map/ppermute | solution.py:585
  45.8 8.5 %collective-permute-start.19 = (bf16[472,128]{1,0:T(8,128)(2,1)S(1)}, bf16[472,128]{1,0:T(8,128)(2,1)S(1)}, u32[]{:S(2)}, u32[]{:S(2)}) collective-permute-start(bf16[472,128]{1,0:T(8,128)(2,1)S(1)} %get-tuple-element.78.refs_0_), channel_id=1, source_target_pairs={{0,16},{16,0},{1,17},{17,1},{2,18},{18,2},{3,19},{19,3},{4,20},{20... | collective-permute-start | bytes 362504 | tf_op jit(solution)/shard_map/ppermute | solution.py:585
  46.6 7.7 %collective-permute-start.20 = (bf16[472,128]{1,0:T(8,128)(2,1)S(1)}, bf16[472,128]{1,0:T(8,128)(2,1)S(1)}, u32[]{:S(2)}, u32[]{:S(2)}) collective-permute-start(bf16[472,128]{1,0:T(8,128)(2,1)S(1)} %get-tuple-element.78.refs_0_), channel_id=1, source_target_pairs={{0,20},{4,16},{8,28},{12,24},{16,4},{20,0},{24,12},{28,8},{1,21},{... | collective-permute-start | bytes 362504 | tf_op jit(solution)/shard_map/ppermute | solution.py:585
  49.1 5.8 %collective-permute-start.21 = (bf16[472,128]{1,0:T(8,128)(2,1)S(1)}, bf16[472,128]{1,0:T(8,128)(2,1)S(1)}, u32[]{:S(2)}, u32[]{:S(2)}) collective-permute-start(bf16[472,128]{1,0:T(8,128)(2,1)S(1)} %collective-permute-done.18.refs_2_), channel_id=1, source_target_pairs={{0,16},{16,0},{1,17},{17,1},{2,18},{18,2},{3,19},{19,3},{4,20},{20... | collective-permute-start | bytes 362504 | tf_op jit(solution)/shard_map/ppermute | solution.py:585
  52.0 4.9 %collective-permute-start.22 = (bf16[472,128]{1,0:T(8,128)(2,1)S(1)}, bf16[472,128]{1,0:T(8,128)(2,1)S(1)}, u32[]{:S(2)}, u32[]{:S(2)}) collective-permute-start(bf16[472,128]{1,0:T(8,128)(2,1)S(1)} %collective-permute-done.13.refs_3_), channel_id=1, source_target_pairs={{0,16},{16,0},{1,17},{17,1},{2,18},{18,2},{3,19},{19,3},{4,20},{20... | collective-permute-start | bytes 362504 | tf_op jit(solution)/shard_map/ppermute | solution.py:585
  52.7 8.8 %collective-permute-start.15 = (bf16[9,72,128]{2,1,0:T(8,128)(2,1)S(1)}, bf16[9,72,128]{2,1,0:T(8,128)(2,1)S(1)}, u32[]{:S(2)}, u32[]{:S(2)}) collective-permute-start(bf16[9,72,128]{2,1,0:T(8,128)(2,1)S(1)} %get-tuple-element.81), channel_id=1, source_target_pairs={{0,2},{1,3},{2,0},{3,1},{4,6},{5,7},{6,4},{7,5},{8,10},{9,11},{10,... | collective-permute-start | bytes 497672 | tf_op jit(solution)/shard_map/ppermute | solution.py:585
  54.3 7.3 %copy-start.13 = (bf16[8,128,512]{2,1,0:T(8,128)(2,1)S(1)}, bf16[8,128,512]{2,1,0:T(8,128)(2,1)}, u32[]{:S(2)}) copy-start(bf16[8,128,512]{2,1,0:T(8,128)(2,1)} %constant.83.clone.pick_ref) | copy-start | bytes 3145732
  54.3 7.3 %collective-permute-start.14 = (bf16[9,72,128]{2,1,0:T(8,128)(2,1)S(1)}, bf16[9,72,128]{2,1,0:T(8,128)(2,1)S(1)}, u32[]{:S(2)}, u32[]{:S(2)}) collective-permute-start(bf16[9,72,128]{2,1,0:T(8,128)(2,1)S(1)} %get-tuple-element.79), channel_id=1, source_target_pairs={{0,1},{1,0},{2,3},{3,2},{4,5},{5,4},{6,7},{7,6},{8,9},{9,8},{10,11... | collective-permute-start | bytes 497672 | tf_op jit(solution)/shard_map/ppermute | solution.py:585
  54.3 7.3 %collective-permute-start.17 = (bf16[9,72,128]{2,1,0:T(8,128)(2,1)S(1)}, bf16[9,72,128]{2,1,0:T(8,128)(2,1)S(1)}, u32[]{:S(2)}, u32[]{:S(2)}) collective-permute-start(bf16[9,72,128]{2,1,0:T(8,128)(2,1)S(1)} %get-tuple-element.83), channel_id=1, source_target_pairs={{0,3},{1,2},{2,1},{3,0},{4,7},{5,6},{6,5},{7,4},{8,11},{9,10},{10,... | collective-permute-start | bytes 497672 | tf_op jit(solution)/shard_map/ppermute | solution.py:585

commit v5 on v4

--- a/solution.py
+++ b/solution.py
@@ -68,7 +68,7 @@
     )
     cosine = xp.where(real, xp.cos(theta), np.float32(0))
     sine = xp.where(real, xp.sin(theta), np.float32(0))
-    return xp.concatenate([cosine.T, sine.T], 0).astype(BF16)
+    return xp.stack(split16(xp.concatenate([cosine.T, sine.T], 0)))
 
 
 def quad_offset(t, groups_y):
@@ -306,7 +306,7 @@
 
 def mix_kernel(groups, groups_y, over, scale, info_ref, *refs):
     (scale_ref, regroup_ref), consts, refs = refs[:2], refs[2:5], refs[5:]
-    chunks, mode_ref, outs, held = refs[:groups], refs[groups], refs[groups + 1 : -1], refs[-1]
+    chunks, mode_ref, outs, (held, low_ref) = refs[:groups], refs[groups], refs[groups + 1 : -2], refs[-2:]
     rows = held.shape[2]
     parts = tail_parts(rows)
     room = LANES - over
@@ -327,18 +327,20 @@
     tiles = outs[0].shape[0] - 2
     for j in range(2):
         values = jnp.concatenate([held[g, j] for g in range(4)], 1) * scale_ref[j : j + 1]
-        sums = jnp.dot(
-            values.astype(jnp.bfloat16), regroup_ref[...], preferred_element_type=jnp.float32
-        ).astype(jnp.bfloat16)
+        high, low = (
+            jnp.dot(v, regroup_ref[...], preferred_element_type=jnp.float32).astype(jnp.bfloat16)
+            for v in split_rows(values)
+        )
         for k in range(4):
             if j * 4 + k < tiles:
+                low_ref[j * 4 + k] = low[:, k * LANES : (k + 1) * LANES]
                 for out in outs:
-                    out[j * 4 + k] = sums[:, k * LANES : (k + 1) * LANES]
+                    out[j * 4 + k] = high[:, k * LANES : (k + 1) * LANES]
     for r, out in enumerate(outs):
         for j in range(2):
             value = held[jnp.bitwise_xor(info_ref[4], r), 2 + j] * scale
             out[tiles + j] = value.astype(jnp.bfloat16)
-    mode_gradients(*consts, outs[0], mode_ref)
+    mode_gradients(*consts, outs[0], low_ref, mode_ref)
 
 
 def packed_rows(tiles, rows, used):
@@ -346,12 +348,18 @@
     return top, (tiles - 1) * rows + top
 
 
-def mode_gradients(spread_ref, gather_ref, w_ref, s_ref, out_ref):
+def split_rows(values):
+    high = values.astype(jnp.bfloat16)
+    return high, (values - high.astype(jnp.float32)).astype(jnp.bfloat16)
+
+
+def mode_gradients(spread_ref, gather_ref, w_ref, s_ref, low_ref, out_ref):
     tiles, rows = s_ref.shape[0] - 2, s_ref.shape[1]
     last, _, _, width = w_ref.shape
     half = spread_ref.shape[1] // (2 * LANES)
     for tile in range(tiles):
         wide = jnp.dot(s_ref[tile], spread_ref[...], preferred_element_type=jnp.float32)
+        wide += jnp.dot(low_ref[tile], spread_ref[...], preferred_element_type=jnp.float32)
         products = []
         for h in range(half):
             kz = tile * half + h
@@ -364,12 +372,12 @@
                 lane = slice(k * LANES, (k + 1) * LANES)
                 w_re = w_ref[kz, 0, :, lane].astype(jnp.float32)
                 w_im = w_ref[kz, 1, :, lane].astype(jnp.float32)
-                real.append((w_re * out_re + w_im * out_im).astype(jnp.bfloat16))
-                imag.append((w_re * out_im - w_im * out_re).astype(jnp.bfloat16))
+                real.append(w_re * out_re + w_im * out_im)
+                imag.append(w_re * out_im - w_im * out_re)
             products += [jnp.concatenate(real, 1), jnp.concatenate(imag, 1)]
-        sums = jnp.dot(
-            jnp.concatenate(products, 0), gather_ref[...], preferred_element_type=jnp.float32
-        )
+        high, low = split_rows(jnp.concatenate(products, 0))
+        sums = jnp.dot(high, gather_ref[...], preferred_element_type=jnp.float32)
+        sums += jnp.dot(low, gather_ref[...], preferred_element_type=jnp.float32)
         which = lax.broadcasted_iota(jnp.int32, (rows, LANES), 1) // (LANES // (2 * half))
         out = sums[:rows]
         for k in range(1, len(products)):
@@ -396,7 +404,10 @@
         out_shape=[modes] + [out] * scenes,
         in_specs=[IN_SMEM] + [IN_VMEM] * (5 + len(chunks)),
         out_specs=[IN_VMEM] * (1 + scenes),
-        scratch_shapes=[pltpu.VMEM((4, 4, rows, LANES), jnp.float32)],
+        scratch_shapes=[
+            pltpu.VMEM((4, 4, rows, LANES), jnp.float32),
+            pltpu.VMEM((tiles, rows, LANES), jnp.bfloat16),
+        ],
         compiler_params=params(24),
         cost_estimate=pl.CostEstimate(
             flops=8 * tiles * rows * gather.size, bytes_accessed=2 * weight.size, transcendentals=0
@@ -514,9 +525,9 @@
             value = jnp.concatenate([value[:, :middle], value[: rows - top, middle:]], 0)
             value = jnp.concatenate([value, jnp.zeros_like(value)], 1)
         modes[own, last * LANES :] = value
-    sums = jnp.dot(
-        t_ref[info_ref[3]], modes[...].astype(jnp.bfloat16), preferred_element_type=jnp.float32
-    )
+    gathered = modes[...].astype(jnp.bfloat16)
+    sums = jnp.dot(t_ref[info_ref[3], 0], gathered, preferred_element_type=jnp.float32)
+    sums += jnp.dot(t_ref[info_ref[3], 1], gathered, preferred_element_type=jnp.float32)
     cells = sums.shape[0] // 2
     cosine, sine = sums[:cells], sums[cells:]
     wide = sine.shape[1]
@@ -568,7 +579,7 @@
         in_specs=[IN_SMEM] + [IN_VMEM] * (4 + len(chunks)),
         out_specs=IN_HBM,
         scratch_shapes=[
-            pltpu.VMEM((table.shape[2], order.shape[0]), jnp.float32),
+            pltpu.VMEM((table.shape[3], order.shape[0]), jnp.float32),
             pltpu.VMEM((cells_x, cells_y, order.shape[1]), jnp.bfloat16),
             pltpu.VMEM(shape, jnp.bfloat16),
             pltpu.SemaphoreType.DMA((cells_x // here,)),

time: 64.8 us -> 67.5 us (1.042)
  Pallas kernels: 23.3 us -> 26.1 us
    pallas_call x1, Pallas kernels: 3.13 us -> 4.82 us  [mix(): pl.pallas_call(functools.partial(mix_kernel, len(chunks), groups_y, over,...]
    pallas_call x1, Pallas kernels: 4.69 us -> 5.64 us  [inverse(): pl.pallas_call(functools.partial(inverse_kernel, len(chunks), per_tile, h...]
    unnamed x36 -> x38, local copies, waits for them, and re-layouts: 2.28 us -> 2.29 us
where the time goes in v5:
time: 67.5 us; the launch traced here: 67.4 us
  starting transfers between devices  29.3 us (43%)
  Pallas kernels  26.1 us (39%)
  waiting for transfers between devices  7.39 us (11%)
  local copies, waits for them, and re-layouts  3.63 us (5%)
  between operations  0.99 us (1%)
    ppermute x23, starting transfers between devices, flip(): return lax.ppermute(value, axes, [(i, i ^ r) for i in range(size)])  29.3 us
    ppermute x23, waiting for transfers between devices, flip(): return lax.ppermute(value, axes, [(i, i ^ r) for i in range(size)])  7.39 us
    pallas_call x1, Pallas kernels, inverse(): pl.pallas_call(functools.partial(inverse_kernel, len(chunks), per_tile, h...  5.64 us
    pallas_call x1, Pallas kernels, mix(): pl.pallas_call(functools.partial(mix_kernel, len(chunks), groups_y, over,...  4.82 us
    pallas_call x2, Pallas kernels, along_z(): pl.pallas_call(along_z_kernel, out_shape=[jax.ShapeDtypeStruct((span, cel...  4.37 us
    pallas_call x1, Pallas kernels, local(): pl.pallas_call(local_kernel, out_shape=jax.ShapeDtypeStruct((cells_x, wid...  3.42 us
    pallas_call x1, Pallas kernels, outer(): pl.pallas_call(functools.partial(outer_kernel, len(spectra)), out_shape=j...  3.16 us
    pallas_call x1, Pallas kernels, first_plane(): pl.pallas_call(functools.partial(first_plane_kernel, block), out_shape=[j...  2.55 us
  transfers between devices with their start and end apart: 23, of which 6 were waited for; matrix products, arithmetic and copies ran while one was open for 2% of the time, Pallas kernels for 20%

profile of v5, /device:TPU:0, one launch (start us, length us, event | category | flops | bytes accessed | tf_op | source)
XLA Modules:
  0.0 67.4 jit_solution(2248950082717826996)
XLA Ops:
  0.7 0.1 stack.20.info_ref
  0.8 2.2 %copy-done = bf16[1,32,16,16,256]{4,3,2,1,0:T(8,128)(2,1)S(1)} copy-done((bf16[1,32,16,16,256]{4,3,2,1,0:T(8,128)(2,1)S(1)}, bf16[1,32,16,16,256]{4,3,2,1,0:T(8,128)(2,1)}, u32[]{:S(2)}) %copy-start) | copy-done | bytes 4194328
  2.9 2.2 %along_z.2 = (bf16[208,256]{1,0:T(8,128)(2,1)S(1)}, bf16[208,256]{1,0:T(8,128)(2,1)S(1)}, bf16[208,256]{1,0:T(8,128)(2,1)S(1)}, bf16[208,256]{1,0:T(8,128)(2,1)S(1)}) custom-call(s32[5]{0:T(128)S(1)} %stack.20.info_ref, bf16[32,256,256]{2,1,0:T(8,128)(2,1)S(1)} %bitcast.17), custom_call_target="tpu_custom_call" | custom-call | flops 872415232 | bytes 4194304 | tf_op jit(solution)/shard_map/along_z/pallas_call | solution.py:184
  5.1 3.1 %collective-permute-start = (bf16[208,256]{1,0:T(8,128)(2,1)S(1)}, bf16[208,256]{1,0:T(8,128)(2,1)S(1)}, u32[]{:S(2)}, u32[]{:S(2)}) collective-permute-start(bf16[208,256]{1,0:T(8,128)(2,1)S(1)} %get-tuple-element.47), channel_id=1, source_target_pairs={{0,4},{4,0},{8,12},{12,8},{16,20},{20,16},{24,28},{28,24},{1,5},{5... | collective-permute-start | bytes 319496 | tf_op jit(solution)/shard_map/ppermute | solution.py:596
  8.2 1.5 %collective-permute-start.1 = (bf16[208,256]{1,0:T(8,128)(2,1)S(1)}, bf16[208,256]{1,0:T(8,128)(2,1)S(1)}, u32[]{:S(2)}, u32[]{:S(2)}) collective-permute-start(bf16[208,256]{1,0:T(8,128)(2,1)S(1)} %get-tuple-element.48), channel_id=1, source_target_pairs={{0,16},{4,20},{8,24},{12,28},{16,0},{20,4},{24,8},{28,12},{1,17},{... | collective-permute-start | bytes 319496 | tf_op jit(solution)/shard_map/ppermute | solution.py:596
  9.7 0.1 collective-permute-start.2
  9.8 2.2 %along_z.3 = (bf16[208,256]{1,0:T(8,128)(2,1)S(1)}, bf16[208,256]{1,0:T(8,128)(2,1)S(1)}, bf16[208,256]{1,0:T(8,128)(2,1)S(1)}, bf16[208,256]{1,0:T(8,128)(2,1)S(1)}) custom-call(s32[5]{0:T(128)S(1)} %stack.20.info_ref, bf16[32,256,256]{2,1,0:T(8,128)(2,1)S(1)} %bitcast.22), custom_call_target="tpu_custom_call" | custom-call | flops 872415232 | bytes 4194304 | tf_op jit(solution)/shard_map/along_z/pallas_call | solution.py:184
  12.0 2.0 %collective-permute-start.3 = (bf16[208,256]{1,0:T(8,128)(2,1)S(1)}, bf16[208,256]{1,0:T(8,128)(2,1)S(1)}, u32[]{:S(2)}, u32[]{:S(2)}) collective-permute-start(bf16[208,256]{1,0:T(8,128)(2,1)S(1)} %get-tuple-element.54), channel_id=1, source_target_pairs={{0,4},{4,0},{8,12},{12,8},{16,20},{20,16},{24,28},{28,24},{1,5},{5... | collective-permute-start | bytes 319496 | tf_op jit(solution)/shard_map/ppermute | solution.py:596
  14.0 1.5 %collective-permute-start.4 = (bf16[208,256]{1,0:T(8,128)(2,1)S(1)}, bf16[208,256]{1,0:T(8,128)(2,1)S(1)}, u32[]{:S(2)}, u32[]{:S(2)}) collective-permute-start(bf16[208,256]{1,0:T(8,128)(2,1)S(1)} %get-tuple-element.55), channel_id=1, source_target_pairs={{0,16},{4,20},{8,24},{12,28},{16,0},{20,4},{24,8},{28,12},{1,17},{... | collective-permute-start | bytes 319496 | tf_op jit(solution)/shard_map/ppermute | solution.py:596
  15.5 0.1 collective-permute-start.5
  15.6 0.1 collective-permute-done.2.refs_3_
  15.8 2.5 %first_plane.1 = (f32[576,208]{1,0:T(8,128)S(1)}, bf16[4,2,576,512]{3,2,1,0:T(8,128)(2,1)S(1)}) custom-call(s32[5]{0:T(128)S(1)} %stack.20.info_ref, f32[576,512]{1,0:T(8,128)S(1)} %copy-done.12, f32[2,576,128]{2,1,0:T(8,128)S(1)} %copy-done.14, bf16[208,256]{1,0:T(8,128)(2,1)S(1)} %get-tuple-element.46.refs_0_, ...), custom_call_target="tpu_custom_call" | custom-call | flops 981467136 | bytes 1179648 | tf_op jit(solution)/shard_map/first_plane/pallas_call | solution.py:244
  18.3 1.5 %collective-permute-done.4.refs_2_ = bf16[208,256]{1,0:T(8,128)(2,1)S(1)} collective-permute-done((bf16[208,256]{1,0:T(8,128)(2,1)S(1)}, bf16[208,256]{1,0:T(8,128)(2,1)S(1)}, u32[]{:S(2)}, u32[]{:S(2)}) %collective-permute-start.4) | collective-permute-done | bytes 106528 | tf_op jit(solution)/shard_map/ppermute | solution.py:596
  19.8 1.4 %collective-permute-done.5.refs_3_ = bf16[208,256]{1,0:T(8,128)(2,1)S(1)} collective-permute-done((bf16[208,256]{1,0:T(8,128)(2,1)S(1)}, bf16[208,256]{1,0:T(8,128)(2,1)S(1)}, u32[]{:S(2)}, u32[]{:S(2)}) %collective-permute-start.5) | collective-permute-done | bytes 106528 | tf_op jit(solution)/shard_map/ppermute | solution.py:596
  21.2 2.2 %second_plane.1 = (bf16[240,128]{1,0:T(8,128)(2,1)S(1)}, bf16[240,128]{1,0:T(8,128)(2,1)S(1)}, bf16[240,128]{1,0:T(8,128)(2,1)S(1)}, bf16[240,128]{1,0:T(8,128)(...) custom-call(s32[5]{0:T(128)S(1)} %stack.20.info_ref, ...), custom_call_target="tpu_custom_call" | custom-call | flops 981467136 | bytes 4718592 | tf_op jit(solution)/shard_map/second_plane/pallas_call | solution.py:290
  23.3 0.5 collective-permute-start.6
  23.9 2.6 %collective-permute-start.7 = (bf16[240,128]{1,0:T(8,128)(2,1)S(1)}, bf16[240,128]{1,0:T(8,128)(2,1)S(1)}, u32[]{:S(2)}, u32[]{:S(2)}) collective-permute-start(bf16[240,128]{1,0:T(8,128)(2,1)S(1)} %get-tuple-element.59), channel_id=1, source_target_pairs={{0,8},{4,12},{8,0},{12,4},{16,24},{20,28},{24,16},{28,20},{1,9},{5... | collective-permute-start | bytes 184328 | tf_op jit(solution)/shard_map/ppermute | solution.py:596
  26.5 1.3 %collective-permute-start.8 = (bf16[240,128]{1,0:T(8,128)(2,1)S(1)}, bf16[240,128]{1,0:T(8,128)(2,1)S(1)}, u32[]{:S(2)}, u32[]{:S(2)}) collective-permute-start(bf16[240,128]{1,0:T(8,128)(2,1)S(1)} %get-tuple-element.60), channel_id=1, source_target_pairs={{0,12},{4,8},{8,4},{12,0},{16,28},{20,24},{24,20},{28,16},{1,13},{... | collective-permute-start | bytes 184328 | tf_op jit(solution)/shard_map/ppermute | solution.py:596
  27.8 1.9 %collective-permute-start.11 = (bf16[240,128]{1,0:T(8,128)(2,1)S(1)}, bf16[240,128]{1,0:T(8,128)(2,1)S(1)}, u32[]{:S(2)}, u32[]{:S(2)}) collective-permute-start(bf16[240,128]{1,0:T(8,128)(2,1)S(1)} %get-tuple-element.65), channel_id=1, source_target_pairs={{0,24},{4,28},{8,16},{12,20},{16,8},{20,12},{24,0},{28,4},{1,25},{... | collective-permute-start | bytes 184328 | tf_op jit(solution)/shard_map/ppermute | solution.py:596
  29.7 1.6 %collective-permute-start.12 = (bf16[240,128]{1,0:T(8,128)(2,1)S(1)}, bf16[240,128]{1,0:T(8,128)(2,1)S(1)}, u32[]{:S(2)}, u32[]{:S(2)}) collective-permute-start(bf16[240,128]{1,0:T(8,128)(2,1)S(1)} %get-tuple-element.66), channel_id=1, source_target_pairs={{0,28},{4,24},{8,20},{12,16},{16,12},{20,8},{24,4},{28,0},{1,29},{... | collective-permute-start | bytes 184328 | tf_op jit(solution)/shard_map/ppermute | solution.py:596
  31.3 0.8 %collective-permute-start.9 = (bf16[240,128]{1,0:T(8,128)(2,1)S(1)}, bf16[240,128]{1,0:T(8,128)(2,1)S(1)}, u32[]{:S(2)}, u32[]{:S(2)}) collective-permute-start(bf16[240,128]{1,0:T(8,128)(2,1)S(1)} %get-tuple-element.63), channel_id=1, source_target_pairs={{0,16},{4,20},{8,24},{12,28},{16,0},{20,4},{24,8},{28,12},{1,17},{... | collective-permute-start | bytes 184328 | tf_op jit(solution)/shard_map/ppermute | solution.py:596
  32.1 1.6 %collective-permute-start.10 = (bf16[240,128]{1,0:T(8,128)(2,1)S(1)}, bf16[240,128]{1,0:T(8,128)(2,1)S(1)}, u32[]{:S(2)}, u32[]{:S(2)}) collective-permute-start(bf16[240,128]{1,0:T(8,128)(2,1)S(1)} %get-tuple-element.64), channel_id=1, source_target_pairs={{0,20},{4,16},{8,28},{12,24},{16,4},{20,0},{24,12},{28,8},{1,21},{... | collective-permute-start | bytes 184328 | tf_op jit(solution)/shard_map/ppermute | solution.py:596
  33.7 0.0 slice-start
  33.7 0.0 slice-start.1
  33.7 3.4 %local.1.local_ref = bf16[16,512,256]{2,1,0:T(8,128)(2,1)S(1)} custom-call(bf16[512,32]{1,0:T(8,128)(2,1)S(1)} %copy-done.7, bf16[32,512]{1,0:T(8,128)(2,1)S(1)} %copy-done.9, bf16[32,32]{1,0:T(8,128)(2,1)S(1)} %copy-done.10, bf16[32,16,16,256]{3,2,1,0:T(8,128)(2,1)S(1)} %bitcast.18), custom_call_target="tpu_custom_call" | custom-call | flops 2147483648 | bytes 8388608 | tf_op jit(solution)/shard_map/local/pallas_call | solution.py:496
  37.1 0.0 copy-start.5
  37.1 0.0 copy-start.6
  37.1 0.0 copy-start.8
  37.2 0.0 copy-start.11
  37.2 0.0 slice-start.2
  37.2 1.3 %copy.23 = bf16[72,13,2,1024]{3,0,2,1:T(8,128)(2,1)S(1)} copy(bf16[72,13,2,1024]{3,2,1,0:T(2,128)(2,1)S(1)} %bitcast.24) | data formatting | bytes 7667712 | tf_op jit(solution)/shard_map/reshape | solution.py:668
  38.5 0.0 copy-start.3
  38.5 0.0 copy-start.4
  38.6 4.8 %mix.1 = (bf16[472,128]{1,0:T(8,128)(2,1)S(1)}, bf16[9,72,128]{2,1,0:T(8,128)(2,1)S(1)}, bf16[9,72,128]{2,1,0:T(8,128)(2,1)S(1)}, bf16[9,72,128]{2,1,0:T(8,128)(2,1)S(1)}, bf16[9,72,128]{2,1,0:T(8,128)(2,1)S(1)}) custom-call(s32[5]{0:T(128)S(1)} %stack.20.info_ref, f32[2,512]{1,0:T(2,128)S(1)} %copy-done.11, bf16[512,512]{1,0:T(8,128)(2,1)S(1)} %copy-done.5, ...), custom_call_target="tpu_custom_call" | custom-call | flops 528482304 | bytes 3833856 | tf_op jit(solution)/shard_map/mix/pallas_call | solution.py:402
  43.4 3.4 %collective-permute-start.18 = (bf16[472,128]{1,0:T(8,128)(2,1)S(1)}, bf16[472,128]{1,0:T(8,128)(2,1)S(1)}, u32[]{:S(2)}, u32[]{:S(2)}) collective-permute-start(bf16[472,128]{1,0:T(8,128)(2,1)S(1)} %get-tuple-element.78.refs_0_), channel_id=1, source_target_pairs={{0,8},{4,12},{8,0},{12,4},{1,9},{5,13},{9,1},{13,5},{2,10},{6,14},... | collective-permute-start | bytes 362504 | tf_op jit(solution)/shard_map/ppermute | solution.py:596
  46.8 0.1 collective-permute-start.13
  46.9 0.6 collective-permute-start.16
  47.5 0.8 %collective-permute-start.19 = (bf16[472,128]{1,0:T(8,128)(2,1)S(1)}, bf16[472,128]{1,0:T(8,128)(2,1)S(1)}, u32[]{:S(2)}, u32[]{:S(2)}) collective-permute-start(bf16[472,128]{1,0:T(8,128)(2,1)S(1)} %get-tuple-element.78.refs_0_), channel_id=1, source_target_pairs={{0,16},{16,0},{1,17},{17,1},{2,18},{18,2},{3,19},{19,3},{4,20},{20... | collective-permute-start | bytes 362504 | tf_op jit(solution)/shard_map/ppermute | solution.py:596
  48.2 2.1 %collective-permute-start.20 = (bf16[472,128]{1,0:T(8,128)(2,1)S(1)}, bf16[472,128]{1,0:T(8,128)(2,1)S(1)}, u32[]{:S(2)}, u32[]{:S(2)}) collective-permute-start(bf16[472,128]{1,0:T(8,128)(2,1)S(1)} %get-tuple-element.78.refs_0_), channel_id=1, source_target_pairs={{0,20},{4,16},{8,28},{12,24},{16,4},{20,0},{24,12},{28,8},{1,21},{... | collective-permute-start | bytes 362504 | tf_op jit(solution)/shard_map/ppermute | solution.py:596
  50.4 0.4 collective-permute-done.18.refs_2_
  50.8 0.8 %collective-permute-start.21 = (bf16[472,128]{1,0:T(8,128)(2,1)S(1)}, bf16[472,128]{1,0:T(8,128)(2,1)S(1)}, u32[]{:S(2)}, u32[]{:S(2)}) collective-permute-start(bf16[472,128]{1,0:T(8,128)(2,1)S(1)} %collective-permute-done.18.refs_2_), channel_id=1, source_target_pairs={{0,16},{16,0},{1,17},{17,1},{2,18},{18,2},{3,19},{19,3},{4,20},{20... | collective-permute-start | bytes 362504 | tf_op jit(solution)/shard_map/ppermute | solution.py:596
  51.6 2.0 %collective-permute-done.13.refs_3_ = bf16[472,128]{1,0:T(8,128)(2,1)S(1)} collective-permute-done((bf16[472,128]{1,0:T(8,128)(2,1)S(1)}, bf16[472,128]{1,0:T(8,128)(2,1)S(1)}, u32[]{:S(2)}, u32[]{:S(2)}) %collective-permute-start.13) | collective-permute-done | bytes 120864 | tf_op jit(solution)/shard_map/ppermute | solution.py:596
  53.6 0.8 %collective-permute-start.22 = (bf16[472,128]{1,0:T(8,128)(2,1)S(1)}, bf16[472,128]{1,0:T(8,128)(2,1)S(1)}, u32[]{:S(2)}, u32[]{:S(2)}) collective-permute-start(bf16[472,128]{1,0:T(8,128)(2,1)S(1)} %collective-permute-done.13.refs_3_), channel_id=1, source_target_pairs={{0,16},{16,0},{1,17},{17,1},{2,18},{18,2},{3,19},{19,3},{4,20},{20... | collective-permute-start | bytes 362504 | tf_op jit(solution)/shard_map/ppermute | solution.py:596
  54.4 1.5 %collective-permute-start.15 = (bf16[9,72,128]{2,1,0:T(8,128)(2,1)S(1)}, bf16[9,72,128]{2,1,0:T(8,128)(2,1)S(1)}, u32[]{:S(2)}, u32[]{:S(2)}) collective-permute-start(bf16[9,72,128]{2,1,0:T(8,128)(2,1)S(1)} %get-tuple-element.81), channel_id=1, source_target_pairs={{0,2},{1,3},{2,0},{3,1},{4,6},{5,7},{6,4},{7,5},{8,10},{9,11},{10,... | collective-permute-start | bytes 497672 | tf_op jit(solution)/shard_map/ppermute | solution.py:596
  56.0 0.6 collective-permute-start.17
  56.6 1.9 %collective-permute-done.22.refs_7_ = bf16[472,128]{1,0:T(8,128)(2,1)S(1)} collective-permute-done((bf16[472,128]{1,0:T(8,128)(2,1)S(1)}, bf16[472,128]{1,0:T(8,128)(2,1)S(1)}, u32[]{:S(2)}, u32[]{:S(2)}) %collective-permute-start.22) | collective-permute-done | bytes 120864 | tf_op jit(solution)/shard_map/ppermute | solution.py:596
  58.5 5.6 %inverse.1 = bf16[32,16,16,256]{3,2,1,0:T(8,128)(2,1)} custom-call(s32[5]{0:T(128)S(1)} %stack.20.info_ref, bf16[8,2,512,576]{3,2,1,0:T(8,128)(2,1)S(1)} %bitcast.21, bf16[896,1024]{1,0:T(8,128)(2,1)S(1)} %copy-done.3, bf16[256,1024]{1,0:T(8,128)(2,1)S(1)} %copy-done.4, bf16[16,512,256]{2,1,0:T(8,128)(2,1)S(1)} %local.1.local_ref, ...), custom_call_target="tpu_custom_call" | custom-call | flops 536870912 | bytes 8388608 | tf_op jit(solution)/shard_map/inverse/pallas_call | solution.py:576
  64.2 3.2 %outer.1 = f32[3744,128]{1,0:T(8,128)} custom-call(bf16[128,512]{1,0:T(8,128)(2,1)S(1)} %copy-done.8, bf16[8,128,512]{2,1,0:T(8,128)(2,1)S(1)} %copy-done.13, bf16[9,72,128]{2,1,0:T(8,128)(2,1)S(1)} %get-tuple-element.86.refs_0_, bf16[9,72,128]{2,1,0:T(8,128)(2,1)S(1)} %collective-permute-done.14.refs_1_, ...), custom_call_target="tpu_custom_call" | custom-call | flops 1019215872 | bytes 5308416 | tf_op jit(solution)/shard_map/outer/pallas_call | solution.py:458
  (47 shorter events, 0.1 us)
Async XLA Ops:
  0.8 2.2 %copy-start = (bf16[1,32,16,16,256]{4,3,2,1,0:T(8,128)(2,1)S(1)}, bf16[1,32,16,16,256]{4,3,2,1,0:T(8,128)(2,1)}, u32[]{:S(2)}) copy-start(bf16[1,32,16,16,256]{4,3,2,1,0:T(8,128)(2,1)} %param.17) | copy-start | bytes 12582916
  2.9 6.8 %copy-start.2 = (bf16[1,32,16,16,256]{4,3,2,1,0:T(8,128)(2,1)S(1)}, bf16[1,32,16,16,256]{4,3,2,1,0:T(8,128)(2,1)}, u32[]{:S(2)}) copy-start(bf16[1,32,16,16,256]{4,3,2,1,0:T(8,128)(2,1)} %param.16) | copy-start | bytes 12582916
  2.9 12.8 %copy-start.12 = (f32[576,512]{1,0:T(8,128)S(1)}, f32[576,512]{1,0:T(8,128)}, u32[]{:S(2)}) copy-start(f32[576,512]{1,0:T(8,128)} %constant.75.clone.base_ref) | copy-start | bytes 3538948
  2.9 12.8 %copy-start.14 = (f32[2,576,128]{2,1,0:T(8,128)S(1)}, f32[2,576,128]{2,1,0:T(8,128)}, u32[]{:S(2)}) copy-start(f32[2,576,128]{2,1,0:T(8,128)} %constant.76.clone.turn_ref) | copy-start | bytes 1769476
  5.1 10.3 %collective-permute-start = (bf16[208,256]{1,0:T(8,128)(2,1)S(1)}, bf16[208,256]{1,0:T(8,128)(2,1)S(1)}, u32[]{:S(2)}, u32[]{:S(2)}) collective-permute-start(bf16[208,256]{1,0:T(8,128)(2,1)S(1)} %get-tuple-element.47), channel_id=1, source_target_pairs={{0,4},{4,0},{8,12},{12,8},{16,20},{20,16},{24,28},{28,24},{1,5},{5... | collective-permute-start | bytes 319496 | tf_op jit(solution)/shard_map/ppermute | solution.py:596
  8.2 7.4 %collective-permute-start.1 = (bf16[208,256]{1,0:T(8,128)(2,1)S(1)}, bf16[208,256]{1,0:T(8,128)(2,1)S(1)}, u32[]{:S(2)}, u32[]{:S(2)}) collective-permute-start(bf16[208,256]{1,0:T(8,128)(2,1)S(1)} %get-tuple-element.48), channel_id=1, source_target_pairs={{0,16},{4,20},{8,24},{12,28},{16,0},{20,4},{24,8},{28,12},{1,17},{... | collective-permute-start | bytes 319496 | tf_op jit(solution)/shard_map/ppermute | solution.py:596
  9.7 6.0 %collective-permute-start.2 = (bf16[208,256]{1,0:T(8,128)(2,1)S(1)}, bf16[208,256]{1,0:T(8,128)(2,1)S(1)}, u32[]{:S(2)}, u32[]{:S(2)}) collective-permute-start(bf16[208,256]{1,0:T(8,128)(2,1)S(1)} %get-tuple-element.49), channel_id=1, source_target_pairs={{0,20},{4,16},{8,28},{12,24},{16,4},{20,0},{24,12},{28,8},{1,21},{... | collective-permute-start | bytes 319496 | tf_op jit(solution)/shard_map/ppermute | solution.py:596
  12.0 6.3 %collective-permute-start.3 = (bf16[208,256]{1,0:T(8,128)(2,1)S(1)}, bf16[208,256]{1,0:T(8,128)(2,1)S(1)}, u32[]{:S(2)}, u32[]{:S(2)}) collective-permute-start(bf16[208,256]{1,0:T(8,128)(2,1)S(1)} %get-tuple-element.54), channel_id=1, source_target_pairs={{0,4},{4,0},{8,12},{12,8},{16,20},{20,16},{24,28},{28,24},{1,5},{5... | collective-permute-start | bytes 319496 | tf_op jit(solution)/shard_map/ppermute | solution.py:596
  14.0 5.8 %collective-permute-start.4 = (bf16[208,256]{1,0:T(8,128)(2,1)S(1)}, bf16[208,256]{1,0:T(8,128)(2,1)S(1)}, u32[]{:S(2)}, u32[]{:S(2)}) collective-permute-start(bf16[208,256]{1,0:T(8,128)(2,1)S(1)} %get-tuple-element.55), channel_id=1, source_target_pairs={{0,16},{4,20},{8,24},{12,28},{16,0},{20,4},{24,8},{28,12},{1,17},{... | collective-permute-start | bytes 319496 | tf_op jit(solution)/shard_map/ppermute | solution.py:596
  15.5 18.2 %copy-start.1 = (bf16[1,32,16,16,256]{4,3,2,1,0:T(8,128)(2,1)S(1)}, bf16[1,32,16,16,256]{4,3,2,1,0:T(8,128)(2,1)}, u32[]{:S(2)}) copy-start(bf16[1,32,16,16,256]{4,3,2,1,0:T(8,128)(2,1)} %param.17) | copy-start | bytes 12582916
  15.5 18.2 %copy-start.7 = (bf16[512,32]{1,0:T(8,128)(2,1)S(1)}, bf16[512,32]{1,0:T(8,128)(2,1)}, u32[]{:S(2)}) copy-start(bf16[512,32]{1,0:T(8,128)(2,1)} %constant.84.clone.row_ref) | copy-start | bytes 98308
  15.5 18.2 %copy-start.9 = (bf16[32,512]{1,0:T(8,128)(2,1)S(1)}, bf16[32,512]{1,0:T(8,128)(2,1)}, u32[]{:S(2)}) copy-start(bf16[32,512]{1,0:T(8,128)(2,1)} %constant.85.clone.column_ref) | copy-start | bytes 98308
  15.5 18.2 %copy-start.10 = (bf16[32,32]{1,0:T(8,128)(2,1)S(1)}, bf16[32,32]{1,0:T(8,128)(2,1)}, u32[]{:S(2)}) copy-start(bf16[32,32]{1,0:T(8,128)(2,1)} %point_ref.1) | copy-start | bytes 6148
  15.5 5.7 %collective-permute-start.5 = (bf16[208,256]{1,0:T(8,128)(2,1)S(1)}, bf16[208,256]{1,0:T(8,128)(2,1)S(1)}, u32[]{:S(2)}, u32[]{:S(2)}) collective-permute-start(bf16[208,256]{1,0:T(8,128)(2,1)S(1)} %get-tuple-element.56), channel_id=1, source_target_pairs={{0,20},{4,16},{8,28},{12,24},{16,4},{20,0},{24,12},{28,8},{1,21},{... | collective-permute-start | bytes 319496 | tf_op jit(solution)/shard_map/ppermute | solution.py:596
  21.2 16.0 %copy-start.15 = (bf16[12,6,13,2,1024]{4,3,2,1,0:T(2,128)(2,1)S(1)}, bf16[12,6,13,2,1024]{4,3,2,1,0:T(2,128)(2,1)}, u32[]{:S(2)}) copy-start(bf16[12,6,13,2,1024]{4,3,2,1,0:T(2,128)(2,1)} %param.18) | copy-start | bytes 11501572
  23.3 8.0 %collective-permute-start.6 = (bf16[240,128]{1,0:T(8,128)(2,1)S(1)}, bf16[240,128]{1,0:T(8,128)(2,1)S(1)}, u32[]{:S(2)}, u32[]{:S(2)}) collective-permute-start(bf16[240,128]{1,0:T(8,128)(2,1)S(1)} %get-tuple-element.58), channel_id=1, source_target_pairs={{0,4},{4,0},{8,12},{12,8},{16,20},{20,16},{24,28},{28,24},{1,5},{5... | collective-permute-start | bytes 184328 | tf_op jit(solution)/shard_map/ppermute | solution.py:596
  23.9 8.2 %collective-permute-start.7 = (bf16[240,128]{1,0:T(8,128)(2,1)S(1)}, bf16[240,128]{1,0:T(8,128)(2,1)S(1)}, u32[]{:S(2)}, u32[]{:S(2)}) collective-permute-start(bf16[240,128]{1,0:T(8,128)(2,1)S(1)} %get-tuple-element.59), channel_id=1, source_target_pairs={{0,8},{4,12},{8,0},{12,4},{16,24},{20,28},{24,16},{28,20},{1,9},{5... | collective-permute-start | bytes 184328 | tf_op jit(solution)/shard_map/ppermute | solution.py:596
  26.5 12.0 %collective-permute-start.8 = (bf16[240,128]{1,0:T(8,128)(2,1)S(1)}, bf16[240,128]{1,0:T(8,128)(2,1)S(1)}, u32[]{:S(2)}, u32[]{:S(2)}) collective-permute-start(bf16[240,128]{1,0:T(8,128)(2,1)S(1)} %get-tuple-element.60), channel_id=1, source_target_pairs={{0,12},{4,8},{8,4},{12,0},{16,28},{20,24},{24,20},{28,16},{1,13},{... | collective-permute-start | bytes 184328 | tf_op jit(solution)/shard_map/ppermute | solution.py:596
  27.8 10.7 %collective-permute-start.11 = (bf16[240,128]{1,0:T(8,128)(2,1)S(1)}, bf16[240,128]{1,0:T(8,128)(2,1)S(1)}, u32[]{:S(2)}, u32[]{:S(2)}) collective-permute-start(bf16[240,128]{1,0:T(8,128)(2,1)S(1)} %get-tuple-element.65), channel_id=1, source_target_pairs={{0,24},{4,28},{8,16},{12,20},{16,8},{20,12},{24,0},{28,4},{1,25},{... | collective-permute-start | bytes 184328 | tf_op jit(solution)/shard_map/ppermute | solution.py:596
  29.7 8.8 %collective-permute-start.12 = (bf16[240,128]{1,0:T(8,128)(2,1)S(1)}, bf16[240,128]{1,0:T(8,128)(2,1)S(1)}, u32[]{:S(2)}, u32[]{:S(2)}) collective-permute-start(bf16[240,128]{1,0:T(8,128)(2,1)S(1)} %get-tuple-element.66), channel_id=1, source_target_pairs={{0,28},{4,24},{8,20},{12,16},{16,12},{20,8},{24,4},{28,0},{1,29},{... | collective-permute-start | bytes 184328 | tf_op jit(solution)/shard_map/ppermute | solution.py:596
  31.3 7.2 %collective-permute-start.9 = (bf16[240,128]{1,0:T(8,128)(2,1)S(1)}, bf16[240,128]{1,0:T(8,128)(2,1)S(1)}, u32[]{:S(2)}, u32[]{:S(2)}) collective-permute-start(bf16[240,128]{1,0:T(8,128)(2,1)S(1)} %get-tuple-element.63), channel_id=1, source_target_pairs={{0,16},{4,20},{8,24},{12,28},{16,0},{20,4},{24,8},{28,12},{1,17},{... | collective-permute-start | bytes 184328 | tf_op jit(solution)/shard_map/ppermute | solution.py:596
  32.1 6.5 %collective-permute-start.10 = (bf16[240,128]{1,0:T(8,128)(2,1)S(1)}, bf16[240,128]{1,0:T(8,128)(2,1)S(1)}, u32[]{:S(2)}, u32[]{:S(2)}) collective-permute-start(bf16[240,128]{1,0:T(8,128)(2,1)S(1)} %get-tuple-element.64), channel_id=1, source_target_pairs={{0,20},{4,16},{8,28},{12,24},{16,4},{20,0},{24,12},{28,8},{1,21},{... | collective-permute-start | bytes 184328 | tf_op jit(solution)/shard_map/ppermute | solution.py:596
  33.7 24.8 %slice-start = ((s8[10485760]{0:T(1024)(128)(4,1)}), s8[4194304]{0:T(1024)(128)(4,1)S(1)}, s32[]{:S(2)}) async-start(s8[10485760]{0:T(1024)(128)(4,1)} %bitcast.20), calls=%async_computation | async-start | bytes 8388608
  33.7 24.8 %slice-start.1 = ((s8[10485760]{0:T(1024)(128)(4,1)}), s8[4194304]{0:T(1024)(128)(4,1)S(1)}, s32[]{:S(2)}) async-start(s8[10485760]{0:T(1024)(128)(4,1)} %bitcast.20), calls=%async_computation.1 | async-start | bytes 8388608
  37.1 1.4 %copy-start.5 = (bf16[512,512]{1,0:T(8,128)(2,1)S(1)}, bf16[512,512]{1,0:T(8,128)(2,1)}, u32[]{:S(2)}) copy-start(bf16[512,512]{1,0:T(8,128)(2,1)} %constant.78.clone.refs_1_) | copy-start | bytes 1572868
  37.1 1.4 %copy-start.6 = (bf16[1024,128]{1,0:T(8,128)(2,1)S(1)}, bf16[1024,128]{1,0:T(8,128)(2,1)}, u32[]{:S(2)}) copy-start(bf16[1024,128]{1,0:T(8,128)(2,1)} %constant.82.clone.refs_3_) | copy-start | bytes 786436
  37.1 1.4 %copy-start.8 = (bf16[128,512]{1,0:T(8,128)(2,1)S(1)}, bf16[128,512]{1,0:T(8,128)(2,1)}, u32[]{:S(2)}) copy-start(bf16[128,512]{1,0:T(8,128)(2,1)} %constant.81.clone.refs_2_.spread_ref) | copy-start | bytes 393220
  37.2 1.4 %copy-start.11 = (f32[2,512]{1,0:T(2,128)S(1)}, f32[2,512]{1,0:T(2,128)}, u32[]{:S(2)}) copy-start(f32[2,512]{1,0:T(2,128)} %constant.86.clone.refs_0_) | copy-start | bytes 12292
  37.2 21.3 %slice-start.2 = ((s8[10485760]{0:T(1024)(128)(4,1)}), s8[2097152]{0:T(1024)(128)(4,1)S(1)}, s32[]{:S(2)}) async-start(s8[10485760]{0:T(1024)(128)(4,1)} %bitcast.20), calls=%async_computation.2 | async-start | bytes 4194304
  38.5 20.1 %copy-start.3 = (bf16[896,1024]{1,0:T(8,128)(2,1)S(1)}, bf16[896,1024]{1,0:T(8,128)(2,1)}, u32[]{:S(2)}) copy-start(bf16[896,1024]{1,0:T(8,128)(2,1)} %constant.80.clone.order_ref) | copy-start | bytes 5505028
  38.5 20.1 %copy-start.4 = (bf16[256,1024]{1,0:T(8,128)(2,1)S(1)}, bf16[256,1024]{1,0:T(8,128)(2,1)}, u32[]{:S(2)}) copy-start(bf16[256,1024]{1,0:T(8,128)(2,1)} %constant.79.clone.z_ref) | copy-start | bytes 1572868
  43.4 7.4 %collective-permute-start.18 = (bf16[472,128]{1,0:T(8,128)(2,1)S(1)}, bf16[472,128]{1,0:T(8,128)(2,1)S(1)}, u32[]{:S(2)}, u32[]{:S(2)}) collective-permute-start(bf16[472,128]{1,0:T(8,128)(2,1)S(1)} %get-tuple-element.78.refs_0_), channel_id=1, source_target_pairs={{0,8},{4,12},{8,0},{12,4},{1,9},{5,13},{9,1},{13,5},{2,10},{6,14},... | collective-permute-start | bytes 362504 | tf_op jit(solution)/shard_map/ppermute | solution.py:596
  46.8 6.8 %collective-permute-start.13 = (bf16[472,128]{1,0:T(8,128)(2,1)S(1)}, bf16[472,128]{1,0:T(8,128)(2,1)S(1)}, u32[]{:S(2)}, u32[]{:S(2)}) collective-permute-start(bf16[472,128]{1,0:T(8,128)(2,1)S(1)} %get-tuple-element.78.refs_0_), channel_id=1, source_target_pairs={{0,12},{4,8},{8,4},{12,0},{1,13},{5,9},{9,5},{13,1},{2,14},{6,10},... | collective-permute-start | bytes 362504 | tf_op jit(solution)/shard_map/ppermute | solution.py:596
  46.9 7.5 %collective-permute-start.16 = (bf16[472,128]{1,0:T(8,128)(2,1)S(1)}, bf16[472,128]{1,0:T(8,128)(2,1)S(1)}, u32[]{:S(2)}, u32[]{:S(2)}) collective-permute-start(bf16[472,128]{1,0:T(8,128)(2,1)S(1)} %get-tuple-element.78.refs_0_), channel_id=1, source_target_pairs={{0,4},{4,0},{8,12},{12,8},{1,5},{5,1},{9,13},{13,9},{2,6},{6,2},{1... | collective-permute-start | bytes 362504 | tf_op jit(solution)/shard_map/ppermute | solution.py:596
  47.5 8.5 %collective-permute-start.19 = (bf16[472,128]{1,0:T(8,128)(2,1)S(1)}, bf16[472,128]{1,0:T(8,128)(2,1)S(1)}, u32[]{:S(2)}, u32[]{:S(2)}) collective-permute-start(bf16[472,128]{1,0:T(8,128)(2,1)S(1)} %get-tuple-element.78.refs_0_), channel_id=1, source_target_pairs={{0,16},{16,0},{1,17},{17,1},{2,18},{18,2},{3,19},{19,3},{4,20},{20... | collective-permute-start | bytes 362504 | tf_op jit(solution)/shard_map/ppermute | solution.py:596
  48.2 7.7 %collective-permute-start.20 = (bf16[472,128]{1,0:T(8,128)(2,1)S(1)}, bf16[472,128]{1,0:T(8,128)(2,1)S(1)}, u32[]{:S(2)}, u32[]{:S(2)}) collective-permute-start(bf16[472,128]{1,0:T(8,128)(2,1)S(1)} %get-tuple-element.78.refs_0_), channel_id=1, source_target_pairs={{0,20},{4,16},{8,28},{12,24},{16,4},{20,0},{24,12},{28,8},{1,21},{... | collective-permute-start | bytes 362504 | tf_op jit(solution)/shard_map/ppermute | solution.py:596
  50.8 5.8 %collective-permute-start.21 = (bf16[472,128]{1,0:T(8,128)(2,1)S(1)}, bf16[472,128]{1,0:T(8,128)(2,1)S(1)}, u32[]{:S(2)}, u32[]{:S(2)}) collective-permute-start(bf16[472,128]{1,0:T(8,128)(2,1)S(1)} %collective-permute-done.18.refs_2_), channel_id=1, source_target_pairs={{0,16},{16,0},{1,17},{17,1},{2,18},{18,2},{3,19},{19,3},{4,20},{20... | collective-permute-start | bytes 362504 | tf_op jit(solution)/shard_map/ppermute | solution.py:596
  53.6 4.9 %collective-permute-start.22 = (bf16[472,128]{1,0:T(8,128)(2,1)S(1)}, bf16[472,128]{1,0:T(8,128)(2,1)S(1)}, u32[]{:S(2)}, u32[]{:S(2)}) collective-permute-start(bf16[472,128]{1,0:T(8,128)(2,1)S(1)} %collective-permute-done.13.refs_3_), channel_id=1, source_target_pairs={{0,16},{16,0},{1,17},{17,1},{2,18},{18,2},{3,19},{19,3},{4,20},{20... | collective-permute-start | bytes 362504 | tf_op jit(solution)/shard_map/ppermute | solution.py:596
  54.4 9.8 %collective-permute-start.15 = (bf16[9,72,128]{2,1,0:T(8,128)(2,1)S(1)}, bf16[9,72,128]{2,1,0:T(8,128)(2,1)S(1)}, u32[]{:S(2)}, u32[]{:S(2)}) collective-permute-start(bf16[9,72,128]{2,1,0:T(8,128)(2,1)S(1)} %get-tuple-element.81), channel_id=1, source_target_pairs={{0,2},{1,3},{2,0},{3,1},{4,6},{5,7},{6,4},{7,5},{8,10},{9,11},{10,... | collective-permute-start | bytes 497672 | tf_op jit(solution)/shard_map/ppermute | solution.py:596
  55.9 8.3 %copy-start.13 = (bf16[8,128,512]{2,1,0:T(8,128)(2,1)S(1)}, bf16[8,128,512]{2,1,0:T(8,128)(2,1)}, u32[]{:S(2)}) copy-start(bf16[8,128,512]{2,1,0:T(8,128)(2,1)} %constant.83.clone.pick_ref) | copy-start | bytes 3145732
  56.0 8.2 %collective-permute-start.14 = (bf16[9,72,128]{2,1,0:T(8,128)(2,1)S(1)}, bf16[9,72,128]{2,1,0:T(8,128)(2,1)S(1)}, u32[]{:S(2)}, u32[]{:S(2)}) collective-permute-start(bf16[9,72,128]{2,1,0:T(8,128)(2,1)S(1)} %get-tuple-element.79), channel_id=1, source_target_pairs={{0,1},{1,0},{2,3},{3,2},{4,5},{5,4},{6,7},{7,6},{8,9},{9,8},{10,11... | collective-permute-start | bytes 497672 | tf_op jit(solution)/shard_map/ppermute | solution.py:596
  56.0 8.2 %collective-permute-start.17 = (bf16[9,72,128]{2,1,0:T(8,128)(2,1)S(1)}, bf16[9,72,128]{2,1,0:T(8,128)(2,1)S(1)}, u32[]{:S(2)}, u32[]{:S(2)}) collective-permute-start(bf16[9,72,128]{2,1,0:T(8,128)(2,1)S(1)} %get-tuple-element.83), channel_id=1, source_target_pairs={{0,3},{1,2},{2,1},{3,0},{4,7},{5,6},{6,5},{7,4},{8,11},{9,10},{10,... | collective-permute-start | bytes 497672 | tf_op jit(solution)/shard_map/ppermute | solution.py:596

commit v6 on v5

--- a/solution.py
+++ b/solution.py
@@ -68,7 +68,7 @@
     )
     cosine = xp.where(real, xp.cos(theta), np.float32(0))
     sine = xp.where(real, xp.sin(theta), np.float32(0))
-    return xp.stack(split16(xp.concatenate([cosine.T, sine.T], 0)))
+    return xp.concatenate(split16(xp.concatenate([cosine.T, sine.T], 0)), 1)
 
 
 def quad_offset(t, groups_y):
@@ -357,9 +357,10 @@
     tiles, rows = s_ref.shape[0] - 2, s_ref.shape[1]
     last, _, _, width = w_ref.shape
     half = spread_ref.shape[1] // (2 * LANES)
+    twice = jnp.concatenate([spread_ref[...], spread_ref[...]], 0)
     for tile in range(tiles):
-        wide = jnp.dot(s_ref[tile], spread_ref[...], preferred_element_type=jnp.float32)
-        wide += jnp.dot(low_ref[tile], spread_ref[...], preferred_element_type=jnp.float32)
+        values = jnp.concatenate([s_ref[tile], low_ref[tile]], 1)
+        wide = jnp.dot(values, twice, preferred_element_type=jnp.float32)
         products = []
         for h in range(half):
             kz = tile * half + h
@@ -526,8 +527,8 @@
             value = jnp.concatenate([value, jnp.zeros_like(value)], 1)
         modes[own, last * LANES :] = value
     gathered = modes[...].astype(jnp.bfloat16)
-    sums = jnp.dot(t_ref[info_ref[3], 0], gathered, preferred_element_type=jnp.float32)
-    sums += jnp.dot(t_ref[info_ref[3], 1], gathered, preferred_element_type=jnp.float32)
+    gathered = jnp.concatenate([gathered, gathered], 0)
+    sums = jnp.dot(t_ref[info_ref[3]], gathered, preferred_element_type=jnp.float32)
     cells = sums.shape[0] // 2
     cosine, sine = sums[:cells], sums[cells:]
     wide = sine.shape[1]
@@ -579,7 +580,7 @@
         in_specs=[IN_SMEM] + [IN_VMEM] * (4 + len(chunks)),
         out_specs=IN_HBM,
         scratch_shapes=[
-            pltpu.VMEM((table.shape[3], order.shape[0]), jnp.float32),
+            pltpu.VMEM((table.shape[2] // 2, order.shape[0]), jnp.float32),
             pltpu.VMEM((cells_x, cells_y, order.shape[1]), jnp.bfloat16),
             pltpu.VMEM(shape, jnp.bfloat16),
             pltpu.SemaphoreType.DMA((cells_x // here,)),

time: 67.5 us -> 67.1 us (level)
  no operation moved by 1% of the time
where the time goes in v6:
time: 67.1 us; the launch traced here: 67 us
  starting transfers between devices  29.3 us (44%)
  Pallas kernels  25.7 us (38%)
  waiting for transfers between devices  7.39 us (11%)
  local copies, waits for them, and re-layouts  3.63 us (5%)
  between operations  0.99 us (1%)
    ppermute x23, starting transfers between devices, flip(): return lax.ppermute(value, axes, [(i, i ^ r) for i in range(size)])  29.3 us
    ppermute x23, waiting for transfers between devices, flip(): return lax.ppermute(value, axes, [(i, i ^ r) for i in range(size)])  7.39 us
    pallas_call x1, Pallas kernels, inverse(): pl.pallas_call(functools.partial(inverse_kernel, len(chunks), per_tile, h...  5.23 us
    pallas_call x1, Pallas kernels, mix(): pl.pallas_call(functools.partial(mix_kernel, len(chunks), groups_y, over,...  4.8 us
    pallas_call x2, Pallas kernels, along_z(): pl.pallas_call(along_z_kernel, out_shape=[jax.ShapeDtypeStruct((span, cel...  4.37 us
    pallas_call x1, Pallas kernels, local(): pl.pallas_call(local_kernel, out_shape=jax.ShapeDtypeStruct((cells_x, wid...  3.42 us
    pallas_call x1, Pallas kernels, outer(): pl.pallas_call(functools.partial(outer_kernel, len(spectra)), out_shape=j...  3.16 us
    pallas_call x1, Pallas kernels, first_plane(): pl.pallas_call(functools.partial(first_plane_kernel, block), out_shape=[j...  2.55 us
  transfers between devices with their start and end apart: 23, of which 6 were waited for; matrix products, arithmetic and copies ran while one was open for 2% of the time, Pallas kernels for 20%

profile of v6, /device:TPU:0, one launch (start us, length us, event | category | flops | bytes accessed | tf_op | source)
XLA Modules:
  0.0 67.0 jit_solution(5642057701870473355)
XLA Ops:
  0.7 0.1 stack.20.info_ref
  0.8 2.2 %copy-done = bf16[1,32,16,16,256]{4,3,2,1,0:T(8,128)(2,1)S(1)} copy-done((bf16[1,32,16,16,256]{4,3,2,1,0:T(8,128)(2,1)S(1)}, bf16[1,32,16,16,256]{4,3,2,1,0:T(8,128)(2,1)}, u32[]{:S(2)}) %copy-start) | copy-done | bytes 4194328
  2.9 2.2 %along_z.2 = (bf16[208,256]{1,0:T(8,128)(2,1)S(1)}, bf16[208,256]{1,0:T(8,128)(2,1)S(1)}, bf16[208,256]{1,0:T(8,128)(2,1)S(1)}, bf16[208,256]{1,0:T(8,128)(2,1)S(1)}) custom-call(s32[5]{0:T(128)S(1)} %stack.20.info_ref, bf16[32,256,256]{2,1,0:T(8,128)(2,1)S(1)} %bitcast.17), custom_call_target="tpu_custom_call" | custom-call | flops 872415232 | bytes 4194304 | tf_op jit(solution)/shard_map/along_z/pallas_call | solution.py:184
  5.1 3.1 %collective-permute-start = (bf16[208,256]{1,0:T(8,128)(2,1)S(1)}, bf16[208,256]{1,0:T(8,128)(2,1)S(1)}, u32[]{:S(2)}, u32[]{:S(2)}) collective-permute-start(bf16[208,256]{1,0:T(8,128)(2,1)S(1)} %get-tuple-element.47), channel_id=1, source_target_pairs={{0,4},{4,0},{8,12},{12,8},{16,20},{20,16},{24,28},{28,24},{1,5},{5... | collective-permute-start | bytes 319496 | tf_op jit(solution)/shard_map/ppermute | solution.py:597
  8.2 1.5 %collective-permute-start.1 = (bf16[208,256]{1,0:T(8,128)(2,1)S(1)}, bf16[208,256]{1,0:T(8,128)(2,1)S(1)}, u32[]{:S(2)}, u32[]{:S(2)}) collective-permute-start(bf16[208,256]{1,0:T(8,128)(2,1)S(1)} %get-tuple-element.48), channel_id=1, source_target_pairs={{0,16},{4,20},{8,24},{12,28},{16,0},{20,4},{24,8},{28,12},{1,17},{... | collective-permute-start | bytes 319496 | tf_op jit(solution)/shard_map/ppermute | solution.py:597
  9.7 0.1 collective-permute-start.2
  9.8 2.2 %along_z.3 = (bf16[208,256]{1,0:T(8,128)(2,1)S(1)}, bf16[208,256]{1,0:T(8,128)(2,1)S(1)}, bf16[208,256]{1,0:T(8,128)(2,1)S(1)}, bf16[208,256]{1,0:T(8,128)(2,1)S(1)}) custom-call(s32[5]{0:T(128)S(1)} %stack.20.info_ref, bf16[32,256,256]{2,1,0:T(8,128)(2,1)S(1)} %bitcast.22), custom_call_target="tpu_custom_call" | custom-call | flops 872415232 | bytes 4194304 | tf_op jit(solution)/shard_map/along_z/pallas_call | solution.py:184
  12.0 2.0 %collective-permute-start.3 = (bf16[208,256]{1,0:T(8,128)(2,1)S(1)}, bf16[208,256]{1,0:T(8,128)(2,1)S(1)}, u32[]{:S(2)}, u32[]{:S(2)}) collective-permute-start(bf16[208,256]{1,0:T(8,128)(2,1)S(1)} %get-tuple-element.54), channel_id=1, source_target_pairs={{0,4},{4,0},{8,12},{12,8},{16,20},{20,16},{24,28},{28,24},{1,5},{5... | collective-permute-start | bytes 319496 | tf_op jit(solution)/shard_map/ppermute | solution.py:597
  14.0 1.5 %collective-permute-start.4 = (bf16[208,256]{1,0:T(8,128)(2,1)S(1)}, bf16[208,256]{1,0:T(8,128)(2,1)S(1)}, u32[]{:S(2)}, u32[]{:S(2)}) collective-permute-start(bf16[208,256]{1,0:T(8,128)(2,1)S(1)} %get-tuple-element.55), channel_id=1, source_target_pairs={{0,16},{4,20},{8,24},{12,28},{16,0},{20,4},{24,8},{28,12},{1,17},{... | collective-permute-start | bytes 319496 | tf_op jit(solution)/shard_map/ppermute | solution.py:597
  15.5 0.1 collective-permute-start.5
  15.6 0.1 collective-permute-done.2.refs_3_
  15.8 2.5 %first_plane.1 = (f32[576,208]{1,0:T(8,128)S(1)}, bf16[4,2,576,512]{3,2,1,0:T(8,128)(2,1)S(1)}) custom-call(s32[5]{0:T(128)S(1)} %stack.20.info_ref, f32[576,512]{1,0:T(8,128)S(1)} %copy-done.12, f32[2,576,128]{2,1,0:T(8,128)S(1)} %copy-done.14, bf16[208,256]{1,0:T(8,128)(2,1)S(1)} %get-tuple-element.46.refs_0_, ...), custom_call_target="tpu_custom_call" | custom-call | flops 981467136 | bytes 1179648 | tf_op jit(solution)/shard_map/first_plane/pallas_call | solution.py:244
  18.3 1.5 %collective-permute-done.4.refs_2_ = bf16[208,256]{1,0:T(8,128)(2,1)S(1)} collective-permute-done((bf16[208,256]{1,0:T(8,128)(2,1)S(1)}, bf16[208,256]{1,0:T(8,128)(2,1)S(1)}, u32[]{:S(2)}, u32[]{:S(2)}) %collective-permute-start.4) | collective-permute-done | bytes 106528 | tf_op jit(solution)/shard_map/ppermute | solution.py:597
  19.8 1.4 %collective-permute-done.5.refs_3_ = bf16[208,256]{1,0:T(8,128)(2,1)S(1)} collective-permute-done((bf16[208,256]{1,0:T(8,128)(2,1)S(1)}, bf16[208,256]{1,0:T(8,128)(2,1)S(1)}, u32[]{:S(2)}, u32[]{:S(2)}) %collective-permute-start.5) | collective-permute-done | bytes 106528 | tf_op jit(solution)/shard_map/ppermute | solution.py:597
  21.2 2.2 %second_plane.1 = (bf16[240,128]{1,0:T(8,128)(2,1)S(1)}, bf16[240,128]{1,0:T(8,128)(2,1)S(1)}, bf16[240,128]{1,0:T(8,128)(2,1)S(1)}, bf16[240,128]{1,0:T(8,128)(...) custom-call(s32[5]{0:T(128)S(1)} %stack.20.info_ref, ...), custom_call_target="tpu_custom_call" | custom-call | flops 981467136 | bytes 4718592 | tf_op jit(solution)/shard_map/second_plane/pallas_call | solution.py:290
  23.3 0.5 collective-permute-start.6
  23.9 2.6 %collective-permute-start.7 = (bf16[240,128]{1,0:T(8,128)(2,1)S(1)}, bf16[240,128]{1,0:T(8,128)(2,1)S(1)}, u32[]{:S(2)}, u32[]{:S(2)}) collective-permute-start(bf16[240,128]{1,0:T(8,128)(2,1)S(1)} %get-tuple-element.59), channel_id=1, source_target_pairs={{0,8},{4,12},{8,0},{12,4},{16,24},{20,28},{24,16},{28,20},{1,9},{5... | collective-permute-start | bytes 184328 | tf_op jit(solution)/shard_map/ppermute | solution.py:597
  26.5 1.3 %collective-permute-start.8 = (bf16[240,128]{1,0:T(8,128)(2,1)S(1)}, bf16[240,128]{1,0:T(8,128)(2,1)S(1)}, u32[]{:S(2)}, u32[]{:S(2)}) collective-permute-start(bf16[240,128]{1,0:T(8,128)(2,1)S(1)} %get-tuple-element.60), channel_id=1, source_target_pairs={{0,12},{4,8},{8,4},{12,0},{16,28},{20,24},{24,20},{28,16},{1,13},{... | collective-permute-start | bytes 184328 | tf_op jit(solution)/shard_map/ppermute | solution.py:597
  27.8 1.9 %collective-permute-start.11 = (bf16[240,128]{1,0:T(8,128)(2,1)S(1)}, bf16[240,128]{1,0:T(8,128)(2,1)S(1)}, u32[]{:S(2)}, u32[]{:S(2)}) collective-permute-start(bf16[240,128]{1,0:T(8,128)(2,1)S(1)} %get-tuple-element.65), channel_id=1, source_target_pairs={{0,24},{4,28},{8,16},{12,20},{16,8},{20,12},{24,0},{28,4},{1,25},{... | collective-permute-start | bytes 184328 | tf_op jit(solution)/shard_map/ppermute | solution.py:597
  29.7 1.6 %collective-permute-start.12 = (bf16[240,128]{1,0:T(8,128)(2,1)S(1)}, bf16[240,128]{1,0:T(8,128)(2,1)S(1)}, u32[]{:S(2)}, u32[]{:S(2)}) collective-permute-start(bf16[240,128]{1,0:T(8,128)(2,1)S(1)} %get-tuple-element.66), channel_id=1, source_target_pairs={{0,28},{4,24},{8,20},{12,16},{16,12},{20,8},{24,4},{28,0},{1,29},{... | collective-permute-start | bytes 184328 | tf_op jit(solution)/shard_map/ppermute | solution.py:597
  31.3 0.8 %collective-permute-start.9 = (bf16[240,128]{1,0:T(8,128)(2,1)S(1)}, bf16[240,128]{1,0:T(8,128)(2,1)S(1)}, u32[]{:S(2)}, u32[]{:S(2)}) collective-permute-start(bf16[240,128]{1,0:T(8,128)(2,1)S(1)} %get-tuple-element.63), channel_id=1, source_target_pairs={{0,16},{4,20},{8,24},{12,28},{16,0},{20,4},{24,8},{28,12},{1,17},{... | collective-permute-start | bytes 184328 | tf_op jit(solution)/shard_map/ppermute | solution.py:597
  32.1 1.6 %collective-permute-start.10 = (bf16[240,128]{1,0:T(8,128)(2,1)S(1)}, bf16[240,128]{1,0:T(8,128)(2,1)S(1)}, u32[]{:S(2)}, u32[]{:S(2)}) collective-permute-start(bf16[240,128]{1,0:T(8,128)(2,1)S(1)} %get-tuple-element.64), channel_id=1, source_target_pairs={{0,20},{4,16},{8,28},{12,24},{16,4},{20,0},{24,12},{28,8},{1,21},{... | collective-permute-start | bytes 184328 | tf_op jit(solution)/shard_map/ppermute | solution.py:597
  33.7 0.0 slice-start
  33.7 0.0 slice-start.1
  33.7 3.4 %local.1.local_ref = bf16[16,512,256]{2,1,0:T(8,128)(2,1)S(1)} custom-call(bf16[512,32]{1,0:T(8,128)(2,1)S(1)} %copy-done.7, bf16[32,512]{1,0:T(8,128)(2,1)S(1)} %copy-done.9, bf16[32,32]{1,0:T(8,128)(2,1)S(1)} %copy-done.10, bf16[32,16,16,256]{3,2,1,0:T(8,128)(2,1)S(1)} %bitcast.18), custom_call_target="tpu_custom_call" | custom-call | flops 2147483648 | bytes 8388608 | tf_op jit(solution)/shard_map/local/pallas_call | solution.py:497
  37.1 0.0 copy-start.4
  37.1 0.0 copy-start.6
  37.1 0.0 copy-start.8
  37.2 0.0 copy-start.11
  37.2 0.0 slice-start.2
  37.2 1.3 %copy.23 = bf16[72,13,2,1024]{3,0,2,1:T(8,128)(2,1)S(1)} copy(bf16[72,13,2,1024]{3,2,1,0:T(2,128)(2,1)S(1)} %bitcast.24) | data formatting | bytes 7667712 | tf_op jit(solution)/shard_map/reshape | solution.py:669
  38.5 0.0 copy-start.3
  38.5 0.0 copy-start.5
  38.6 4.8 %mix.1 = (bf16[472,128]{1,0:T(8,128)(2,1)S(1)}, bf16[9,72,128]{2,1,0:T(8,128)(2,1)S(1)}, bf16[9,72,128]{2,1,0:T(8,128)(2,1)S(1)}, bf16[9,72,128]{2,1,0:T(8,128)(2,1)S(1)}, bf16[9,72,128]{2,1,0:T(8,128)(2,1)S(1)}) custom-call(s32[5]{0:T(128)S(1)} %stack.20.info_ref, f32[2,512]{1,0:T(2,128)S(1)} %copy-done.11, bf16[512,512]{1,0:T(8,128)(2,1)S(1)} %copy-done.4, ...), custom_call_target="tpu_custom_call" | custom-call | flops 528482304 | bytes 3833856 | tf_op jit(solution)/shard_map/mix/pallas_call | solution.py:403
  43.4 3.4 %collective-permute-start.18 = (bf16[472,128]{1,0:T(8,128)(2,1)S(1)}, bf16[472,128]{1,0:T(8,128)(2,1)S(1)}, u32[]{:S(2)}, u32[]{:S(2)}) collective-permute-start(bf16[472,128]{1,0:T(8,128)(2,1)S(1)} %get-tuple-element.78.refs_0_), channel_id=1, source_target_pairs={{0,8},{4,12},{8,0},{12,4},{1,9},{5,13},{9,1},{13,5},{2,10},{6,14},... | collective-permute-start | bytes 362504 | tf_op jit(solution)/shard_map/ppermute | solution.py:597
  46.8 0.1 collective-permute-start.13
  46.9 0.6 collective-permute-start.16
  47.4 0.8 %collective-permute-start.19 = (bf16[472,128]{1,0:T(8,128)(2,1)S(1)}, bf16[472,128]{1,0:T(8,128)(2,1)S(1)}, u32[]{:S(2)}, u32[]{:S(2)}) collective-permute-start(bf16[472,128]{1,0:T(8,128)(2,1)S(1)} %get-tuple-element.78.refs_0_), channel_id=1, source_target_pairs={{0,16},{16,0},{1,17},{17,1},{2,18},{18,2},{3,19},{19,3},{4,20},{20... | collective-permute-start | bytes 362504 | tf_op jit(solution)/shard_map/ppermute | solution.py:597
  48.2 2.1 %collective-permute-start.20 = (bf16[472,128]{1,0:T(8,128)(2,1)S(1)}, bf16[472,128]{1,0:T(8,128)(2,1)S(1)}, u32[]{:S(2)}, u32[]{:S(2)}) collective-permute-start(bf16[472,128]{1,0:T(8,128)(2,1)S(1)} %get-tuple-element.78.refs_0_), channel_id=1, source_target_pairs={{0,20},{4,16},{8,28},{12,24},{16,4},{20,0},{24,12},{28,8},{1,21},{... | collective-permute-start | bytes 362504 | tf_op jit(solution)/shard_map/ppermute | solution.py:597
  50.4 0.4 collective-permute-done.18.refs_2_
  50.8 0.8 %collective-permute-start.21 = (bf16[472,128]{1,0:T(8,128)(2,1)S(1)}, bf16[472,128]{1,0:T(8,128)(2,1)S(1)}, u32[]{:S(2)}, u32[]{:S(2)}) collective-permute-start(bf16[472,128]{1,0:T(8,128)(2,1)S(1)} %collective-permute-done.18.refs_2_), channel_id=1, source_target_pairs={{0,16},{16,0},{1,17},{17,1},{2,18},{18,2},{3,19},{19,3},{4,20},{20... | collective-permute-start | bytes 362504 | tf_op jit(solution)/shard_map/ppermute | solution.py:597
  51.6 2.0 %collective-permute-done.13.refs_3_ = bf16[472,128]{1,0:T(8,128)(2,1)S(1)} collective-permute-done((bf16[472,128]{1,0:T(8,128)(2,1)S(1)}, bf16[472,128]{1,0:T(8,128)(2,1)S(1)}, u32[]{:S(2)}, u32[]{:S(2)}) %collective-permute-start.13) | collective-permute-done | bytes 120864 | tf_op jit(solution)/shard_map/ppermute | solution.py:597
  53.6 0.8 %collective-permute-start.22 = (bf16[472,128]{1,0:T(8,128)(2,1)S(1)}, bf16[472,128]{1,0:T(8,128)(2,1)S(1)}, u32[]{:S(2)}, u32[]{:S(2)}) collective-permute-start(bf16[472,128]{1,0:T(8,128)(2,1)S(1)} %collective-permute-done.13.refs_3_), channel_id=1, source_target_pairs={{0,16},{16,0},{1,17},{17,1},{2,18},{18,2},{3,19},{19,3},{4,20},{20... | collective-permute-start | bytes 362504 | tf_op jit(solution)/shard_map/ppermute | solution.py:597
  54.4 1.5 %collective-permute-start.15 = (bf16[9,72,128]{2,1,0:T(8,128)(2,1)S(1)}, bf16[9,72,128]{2,1,0:T(8,128)(2,1)S(1)}, u32[]{:S(2)}, u32[]{:S(2)}) collective-permute-start(bf16[9,72,128]{2,1,0:T(8,128)(2,1)S(1)} %get-tuple-element.81), channel_id=1, source_target_pairs={{0,2},{1,3},{2,0},{3,1},{4,6},{5,7},{6,4},{7,5},{8,10},{9,11},{10,... | collective-permute-start | bytes 497672 | tf_op jit(solution)/shard_map/ppermute | solution.py:597
  55.9 0.6 collective-permute-start.17
  56.6 1.9 %collective-permute-done.22.refs_7_ = bf16[472,128]{1,0:T(8,128)(2,1)S(1)} collective-permute-done((bf16[472,128]{1,0:T(8,128)(2,1)S(1)}, bf16[472,128]{1,0:T(8,128)(2,1)S(1)}, u32[]{:S(2)}, u32[]{:S(2)}) %collective-permute-start.22) | collective-permute-done | bytes 120864 | tf_op jit(solution)/shard_map/ppermute | solution.py:597
  58.5 5.2 %inverse.1 = bf16[32,16,16,256]{3,2,1,0:T(8,128)(2,1)} custom-call(s32[5]{0:T(128)S(1)} %stack.20.info_ref, bf16[8,512,1152]{2,1,0:T(8,128)(2,1)S(1)} %bitcast.21, bf16[896,1024]{1,0:T(8,128)(2,1)S(1)} %copy-done.3, bf16[256,1024]{1,0:T(8,128)(2,1)S(1)} %copy-done.5, bf16[16,512,256]{2,1,0:T(8,128)(2,1)S(1)} %local.1.local_ref, ...), custom_call_target="tpu_custom_call" | custom-call | flops 536870912 | bytes 8388608 | tf_op jit(solution)/shard_map/inverse/pallas_call | solution.py:577
  63.8 3.2 %outer.1 = f32[3744,128]{1,0:T(8,128)} custom-call(bf16[128,512]{1,0:T(8,128)(2,1)S(1)} %copy-done.8, bf16[8,128,512]{2,1,0:T(8,128)(2,1)S(1)} %copy-done.13, bf16[9,72,128]{2,1,0:T(8,128)(2,1)S(1)} %get-tuple-element.86.refs_0_, bf16[9,72,128]{2,1,0:T(8,128)(2,1)S(1)} %collective-permute-done.14.refs_1_, ...), custom_call_target="tpu_custom_call" | custom-call | flops 1019215872 | bytes 5308416 | tf_op jit(solution)/shard_map/outer/pallas_call | solution.py:459
  (47 shorter events, 0.1 us)
Async XLA Ops:
  0.8 2.2 %copy-start = (bf16[1,32,16,16,256]{4,3,2,1,0:T(8,128)(2,1)S(1)}, bf16[1,32,16,16,256]{4,3,2,1,0:T(8,128)(2,1)}, u32[]{:S(2)}) copy-start(bf16[1,32,16,16,256]{4,3,2,1,0:T(8,128)(2,1)} %param.17) | copy-start | bytes 12582916
  2.9 6.8 %copy-start.2 = (bf16[1,32,16,16,256]{4,3,2,1,0:T(8,128)(2,1)S(1)}, bf16[1,32,16,16,256]{4,3,2,1,0:T(8,128)(2,1)}, u32[]{:S(2)}) copy-start(bf16[1,32,16,16,256]{4,3,2,1,0:T(8,128)(2,1)} %param.16) | copy-start | bytes 12582916
  2.9 12.8 %copy-start.12 = (f32[576,512]{1,0:T(8,128)S(1)}, f32[576,512]{1,0:T(8,128)}, u32[]{:S(2)}) copy-start(f32[576,512]{1,0:T(8,128)} %constant.75.clone.base_ref) | copy-start | bytes 3538948
  2.9 12.8 %copy-start.14 = (f32[2,576,128]{2,1,0:T(8,128)S(1)}, f32[2,576,128]{2,1,0:T(8,128)}, u32[]{:S(2)}) copy-start(f32[2,576,128]{2,1,0:T(8,128)} %constant.76.clone.turn_ref) | copy-start | bytes 1769476
  5.1 10.3 %collective-permute-start = (bf16[208,256]{1,0:T(8,128)(2,1)S(1)}, bf16[208,256]{1,0:T(8,128)(2,1)S(1)}, u32[]{:S(2)}, u32[]{:S(2)}) collective-permute-start(bf16[208,256]{1,0:T(8,128)(2,1)S(1)} %get-tuple-element.47), channel_id=1, source_target_pairs={{0,4},{4,0},{8,12},{12,8},{16,20},{20,16},{24,28},{28,24},{1,5},{5... | collective-permute-start | bytes 319496 | tf_op jit(solution)/shard_map/ppermute | solution.py:597
  8.2 7.4 %collective-permute-start.1 = (bf16[208,256]{1,0:T(8,128)(2,1)S(1)}, bf16[208,256]{1,0:T(8,128)(2,1)S(1)}, u32[]{:S(2)}, u32[]{:S(2)}) collective-permute-start(bf16[208,256]{1,0:T(8,128)(2,1)S(1)} %get-tuple-element.48), channel_id=1, source_target_pairs={{0,16},{4,20},{8,24},{12,28},{16,0},{20,4},{24,8},{28,12},{1,17},{... | collective-permute-start | bytes 319496 | tf_op jit(solution)/shard_map/ppermute | solution.py:597
  9.7 6.0 %collective-permute-start.2 = (bf16[208,256]{1,0:T(8,128)(2,1)S(1)}, bf16[208,256]{1,0:T(8,128)(2,1)S(1)}, u32[]{:S(2)}, u32[]{:S(2)}) collective-permute-start(bf16[208,256]{1,0:T(8,128)(2,1)S(1)} %get-tuple-element.49), channel_id=1, source_target_pairs={{0,20},{4,16},{8,28},{12,24},{16,4},{20,0},{24,12},{28,8},{1,21},{... | collective-permute-start | bytes 319496 | tf_op jit(solution)/shard_map/ppermute | solution.py:597
  12.0 6.3 %collective-permute-start.3 = (bf16[208,256]{1,0:T(8,128)(2,1)S(1)}, bf16[208,256]{1,0:T(8,128)(2,1)S(1)}, u32[]{:S(2)}, u32[]{:S(2)}) collective-permute-start(bf16[208,256]{1,0:T(8,128)(2,1)S(1)} %get-tuple-element.54), channel_id=1, source_target_pairs={{0,4},{4,0},{8,12},{12,8},{16,20},{20,16},{24,28},{28,24},{1,5},{5... | collective-permute-start | bytes 319496 | tf_op jit(solution)/shard_map/ppermute | solution.py:597
  14.0 5.8 %collective-permute-start.4 = (bf16[208,256]{1,0:T(8,128)(2,1)S(1)}, bf16[208,256]{1,0:T(8,128)(2,1)S(1)}, u32[]{:S(2)}, u32[]{:S(2)}) collective-permute-start(bf16[208,256]{1,0:T(8,128)(2,1)S(1)} %get-tuple-element.55), channel_id=1, source_target_pairs={{0,16},{4,20},{8,24},{12,28},{16,0},{20,4},{24,8},{28,12},{1,17},{... | collective-permute-start | bytes 319496 | tf_op jit(solution)/shard_map/ppermute | solution.py:597
  15.5 18.2 %copy-start.1 = (bf16[1,32,16,16,256]{4,3,2,1,0:T(8,128)(2,1)S(1)}, bf16[1,32,16,16,256]{4,3,2,1,0:T(8,128)(2,1)}, u32[]{:S(2)}) copy-start(bf16[1,32,16,16,256]{4,3,2,1,0:T(8,128)(2,1)} %param.17) | copy-start | bytes 12582916
  15.5 18.2 %copy-start.7 = (bf16[512,32]{1,0:T(8,128)(2,1)S(1)}, bf16[512,32]{1,0:T(8,128)(2,1)}, u32[]{:S(2)}) copy-start(bf16[512,32]{1,0:T(8,128)(2,1)} %constant.84.clone.row_ref) | copy-start | bytes 98308
  15.5 18.2 %copy-start.9 = (bf16[32,512]{1,0:T(8,128)(2,1)S(1)}, bf16[32,512]{1,0:T(8,128)(2,1)}, u32[]{:S(2)}) copy-start(bf16[32,512]{1,0:T(8,128)(2,1)} %constant.85.clone.column_ref) | copy-start | bytes 98308
  15.5 18.2 %copy-start.10 = (bf16[32,32]{1,0:T(8,128)(2,1)S(1)}, bf16[32,32]{1,0:T(8,128)(2,1)}, u32[]{:S(2)}) copy-start(bf16[32,32]{1,0:T(8,128)(2,1)} %point_ref.1) | copy-start | bytes 6148
  15.5 5.7 %collective-permute-start.5 = (bf16[208,256]{1,0:T(8,128)(2,1)S(1)}, bf16[208,256]{1,0:T(8,128)(2,1)S(1)}, u32[]{:S(2)}, u32[]{:S(2)}) collective-permute-start(bf16[208,256]{1,0:T(8,128)(2,1)S(1)} %get-tuple-element.56), channel_id=1, source_target_pairs={{0,20},{4,16},{8,28},{12,24},{16,4},{20,0},{24,12},{28,8},{1,21},{... | collective-permute-start | bytes 319496 | tf_op jit(solution)/shard_map/ppermute | solution.py:597
  21.2 16.0 %copy-start.15 = (bf16[12,6,13,2,1024]{4,3,2,1,0:T(2,128)(2,1)S(1)}, bf16[12,6,13,2,1024]{4,3,2,1,0:T(2,128)(2,1)}, u32[]{:S(2)}) copy-start(bf16[12,6,13,2,1024]{4,3,2,1,0:T(2,128)(2,1)} %param.18) | copy-start | bytes 11501572
  23.3 8.0 %collective-permute-start.6 = (bf16[240,128]{1,0:T(8,128)(2,1)S(1)}, bf16[240,128]{1,0:T(8,128)(2,1)S(1)}, u32[]{:S(2)}, u32[]{:S(2)}) collective-permute-start(bf16[240,128]{1,0:T(8,128)(2,1)S(1)} %get-tuple-element.58), channel_id=1, source_target_pairs={{0,4},{4,0},{8,12},{12,8},{16,20},{20,16},{24,28},{28,24},{1,5},{5... | collective-permute-start | bytes 184328 | tf_op jit(solution)/shard_map/ppermute | solution.py:597
  23.9 8.2 %collective-permute-start.7 = (bf16[240,128]{1,0:T(8,128)(2,1)S(1)}, bf16[240,128]{1,0:T(8,128)(2,1)S(1)}, u32[]{:S(2)}, u32[]{:S(2)}) collective-permute-start(bf16[240,128]{1,0:T(8,128)(2,1)S(1)} %get-tuple-element.59), channel_id=1, source_target_pairs={{0,8},{4,12},{8,0},{12,4},{16,24},{20,28},{24,16},{28,20},{1,9},{5... | collective-permute-start | bytes 184328 | tf_op jit(solution)/shard_map/ppermute | solution.py:597
  26.5 12.0 %collective-permute-start.8 = (bf16[240,128]{1,0:T(8,128)(2,1)S(1)}, bf16[240,128]{1,0:T(8,128)(2,1)S(1)}, u32[]{:S(2)}, u32[]{:S(2)}) collective-permute-start(bf16[240,128]{1,0:T(8,128)(2,1)S(1)} %get-tuple-element.60), channel_id=1, source_target_pairs={{0,12},{4,8},{8,4},{12,0},{16,28},{20,24},{24,20},{28,16},{1,13},{... | collective-permute-start | bytes 184328 | tf_op jit(solution)/shard_map/ppermute | solution.py:597
  27.8 10.7 %collective-permute-start.11 = (bf16[240,128]{1,0:T(8,128)(2,1)S(1)}, bf16[240,128]{1,0:T(8,128)(2,1)S(1)}, u32[]{:S(2)}, u32[]{:S(2)}) collective-permute-start(bf16[240,128]{1,0:T(8,128)(2,1)S(1)} %get-tuple-element.65), channel_id=1, source_target_pairs={{0,24},{4,28},{8,16},{12,20},{16,8},{20,12},{24,0},{28,4},{1,25},{... | collective-permute-start | bytes 184328 | tf_op jit(solution)/shard_map/ppermute | solution.py:597
  29.7 8.8 %collective-permute-start.12 = (bf16[240,128]{1,0:T(8,128)(2,1)S(1)}, bf16[240,128]{1,0:T(8,128)(2,1)S(1)}, u32[]{:S(2)}, u32[]{:S(2)}) collective-permute-start(bf16[240,128]{1,0:T(8,128)(2,1)S(1)} %get-tuple-element.66), channel_id=1, source_target_pairs={{0,28},{4,24},{8,20},{12,16},{16,12},{20,8},{24,4},{28,0},{1,29},{... | collective-permute-start | bytes 184328 | tf_op jit(solution)/shard_map/ppermute | solution.py:597
  31.3 7.2 %collective-permute-start.9 = (bf16[240,128]{1,0:T(8,128)(2,1)S(1)}, bf16[240,128]{1,0:T(8,128)(2,1)S(1)}, u32[]{:S(2)}, u32[]{:S(2)}) collective-permute-start(bf16[240,128]{1,0:T(8,128)(2,1)S(1)} %get-tuple-element.63), channel_id=1, source_target_pairs={{0,16},{4,20},{8,24},{12,28},{16,0},{20,4},{24,8},{28,12},{1,17},{... | collective-permute-start | bytes 184328 | tf_op jit(solution)/shard_map/ppermute | solution.py:597
  32.1 6.5 %collective-permute-start.10 = (bf16[240,128]{1,0:T(8,128)(2,1)S(1)}, bf16[240,128]{1,0:T(8,128)(2,1)S(1)}, u32[]{:S(2)}, u32[]{:S(2)}) collective-permute-start(bf16[240,128]{1,0:T(8,128)(2,1)S(1)} %get-tuple-element.64), channel_id=1, source_target_pairs={{0,20},{4,16},{8,28},{12,24},{16,4},{20,0},{24,12},{28,8},{1,21},{... | collective-permute-start | bytes 184328 | tf_op jit(solution)/shard_map/ppermute | solution.py:597
  33.7 24.8 %slice-start = ((s8[9437184]{0:T(1024)(128)(4,1)}), s8[4194304]{0:T(1024)(128)(4,1)S(1)}, s32[]{:S(2)}) async-start(s8[9437184]{0:T(1024)(128)(4,1)} %bitcast.20), calls=%async_computation | async-start | bytes 8388608
  33.7 24.8 %slice-start.1 = ((s8[9437184]{0:T(1024)(128)(4,1)}), s8[4194304]{0:T(1024)(128)(4,1)S(1)}, s32[]{:S(2)}) async-start(s8[9437184]{0:T(1024)(128)(4,1)} %bitcast.20), calls=%async_computation.1 | async-start | bytes 8388608
  37.1 1.4 %copy-start.4 = (bf16[512,512]{1,0:T(8,128)(2,1)S(1)}, bf16[512,512]{1,0:T(8,128)(2,1)}, u32[]{:S(2)}) copy-start(bf16[512,512]{1,0:T(8,128)(2,1)} %constant.78.clone.refs_1_) | copy-start | bytes 1572868
  37.1 1.4 %copy-start.6 = (bf16[1024,128]{1,0:T(8,128)(2,1)S(1)}, bf16[1024,128]{1,0:T(8,128)(2,1)}, u32[]{:S(2)}) copy-start(bf16[1024,128]{1,0:T(8,128)(2,1)} %constant.82.clone.refs_3_) | copy-start | bytes 786436
  37.1 1.4 %copy-start.8 = (bf16[128,512]{1,0:T(8,128)(2,1)S(1)}, bf16[128,512]{1,0:T(8,128)(2,1)}, u32[]{:S(2)}) copy-start(bf16[128,512]{1,0:T(8,128)(2,1)} %constant.81.clone.refs_2_.spread_ref) | copy-start | bytes 393220
  37.2 1.4 %copy-start.11 = (f32[2,512]{1,0:T(2,128)S(1)}, f32[2,512]{1,0:T(2,128)}, u32[]{:S(2)}) copy-start(f32[2,512]{1,0:T(2,128)} %constant.86.clone.refs_0_) | copy-start | bytes 12292
  37.2 21.3 %slice-start.2 = ((s8[9437184]{0:T(1024)(128)(4,1)}), s8[1048576]{0:T(1024)(128)(4,1)S(1)}, s32[]{:S(2)}) async-start(s8[9437184]{0:T(1024)(128)(4,1)} %bitcast.20), calls=%async_computation.2 | async-start | bytes 2097152
  38.5 20.0 %copy-start.3 = (bf16[896,1024]{1,0:T(8,128)(2,1)S(1)}, bf16[896,1024]{1,0:T(8,128)(2,1)}, u32[]{:S(2)}) copy-start(bf16[896,1024]{1,0:T(8,128)(2,1)} %constant.80.clone.order_ref) | copy-start | bytes 5505028
  38.5 20.0 %copy-start.5 = (bf16[256,1024]{1,0:T(8,128)(2,1)S(1)}, bf16[256,1024]{1,0:T(8,128)(2,1)}, u32[]{:S(2)}) copy-start(bf16[256,1024]{1,0:T(8,128)(2,1)} %constant.79.clone.z_ref) | copy-start | bytes 1572868
  43.4 7.4 %collective-permute-start.18 = (bf16[472,128]{1,0:T(8,128)(2,1)S(1)}, bf16[472,128]{1,0:T(8,128)(2,1)S(1)}, u32[]{:S(2)}, u32[]{:S(2)}) collective-permute-start(bf16[472,128]{1,0:T(8,128)(2,1)S(1)} %get-tuple-element.78.refs_0_), channel_id=1, source_target_pairs={{0,8},{4,12},{8,0},{12,4},{1,9},{5,13},{9,1},{13,5},{2,10},{6,14},... | collective-permute-start | bytes 362504 | tf_op jit(solution)/shard_map/ppermute | solution.py:597
  46.8 6.8 %collective-permute-start.13 = (bf16[472,128]{1,0:T(8,128)(2,1)S(1)}, bf16[472,128]{1,0:T(8,128)(2,1)S(1)}, u32[]{:S(2)}, u32[]{:S(2)}) collective-permute-start(bf16[472,128]{1,0:T(8,128)(2,1)S(1)} %get-tuple-element.78.refs_0_), channel_id=1, source_target_pairs={{0,12},{4,8},{8,4},{12,0},{1,13},{5,9},{9,5},{13,1},{2,14},{6,10},... | collective-permute-start | bytes 362504 | tf_op jit(solution)/shard_map/ppermute | solution.py:597
  46.9 7.5 %collective-permute-start.16 = (bf16[472,128]{1,0:T(8,128)(2,1)S(1)}, bf16[472,128]{1,0:T(8,128)(2,1)S(1)}, u32[]{:S(2)}, u32[]{:S(2)}) collective-permute-start(bf16[472,128]{1,0:T(8,128)(2,1)S(1)} %get-tuple-element.78.refs_0_), channel_id=1, source_target_pairs={{0,4},{4,0},{8,12},{12,8},{1,5},{5,1},{9,13},{13,9},{2,6},{6,2},{1... | collective-permute-start | bytes 362504 | tf_op jit(solution)/shard_map/ppermute | solution.py:597
  47.4 8.5 %collective-permute-start.19 = (bf16[472,128]{1,0:T(8,128)(2,1)S(1)}, bf16[472,128]{1,0:T(8,128)(2,1)S(1)}, u32[]{:S(2)}, u32[]{:S(2)}) collective-permute-start(bf16[472,128]{1,0:T(8,128)(2,1)S(1)} %get-tuple-element.78.refs_0_), channel_id=1, source_target_pairs={{0,16},{16,0},{1,17},{17,1},{2,18},{18,2},{3,19},{19,3},{4,20},{20... | collective-permute-start | bytes 362504 | tf_op jit(solution)/shard_map/ppermute | solution.py:597
  48.2 7.7 %collective-permute-start.20 = (bf16[472,128]{1,0:T(8,128)(2,1)S(1)}, bf16[472,128]{1,0:T(8,128)(2,1)S(1)}, u32[]{:S(2)}, u32[]{:S(2)}) collective-permute-start(bf16[472,128]{1,0:T(8,128)(2,1)S(1)} %get-tuple-element.78.refs_0_), channel_id=1, source_target_pairs={{0,20},{4,16},{8,28},{12,24},{16,4},{20,0},{24,12},{28,8},{1,21},{... | collective-permute-start | bytes 362504 | tf_op jit(solution)/shard_map/ppermute | solution.py:597
  50.8 5.8 %collective-permute-start.21 = (bf16[472,128]{1,0:T(8,128)(2,1)S(1)}, bf16[472,128]{1,0:T(8,128)(2,1)S(1)}, u32[]{:S(2)}, u32[]{:S(2)}) collective-permute-start(bf16[472,128]{1,0:T(8,128)(2,1)S(1)} %collective-permute-done.18.refs_2_), channel_id=1, source_target_pairs={{0,16},{16,0},{1,17},{17,1},{2,18},{18,2},{3,19},{19,3},{4,20},{20... | collective-permute-start | bytes 362504 | tf_op jit(solution)/shard_map/ppermute | solution.py:597
  53.6 4.9 %collective-permute-start.22 = (bf16[472,128]{1,0:T(8,128)(2,1)S(1)}, bf16[472,128]{1,0:T(8,128)(2,1)S(1)}, u32[]{:S(2)}, u32[]{:S(2)}) collective-permute-start(bf16[472,128]{1,0:T(8,128)(2,1)S(1)} %collective-permute-done.13.refs_3_), channel_id=1, source_target_pairs={{0,16},{16,0},{1,17},{17,1},{2,18},{18,2},{3,19},{19,3},{4,20},{20... | collective-permute-start | bytes 362504 | tf_op jit(solution)/shard_map/ppermute | solution.py:597
  54.4 9.4 %collective-permute-start.15 = (bf16[9,72,128]{2,1,0:T(8,128)(2,1)S(1)}, bf16[9,72,128]{2,1,0:T(8,128)(2,1)S(1)}, u32[]{:S(2)}, u32[]{:S(2)}) collective-permute-start(bf16[9,72,128]{2,1,0:T(8,128)(2,1)S(1)} %get-tuple-element.81), channel_id=1, source_target_pairs={{0,2},{1,3},{2,0},{3,1},{4,6},{5,7},{6,4},{7,5},{8,10},{9,11},{10,... | collective-permute-start | bytes 497672 | tf_op jit(solution)/shard_map/ppermute | solution.py:597
  55.9 7.9 %copy-start.13 = (bf16[8,128,512]{2,1,0:T(8,128)(2,1)S(1)}, bf16[8,128,512]{2,1,0:T(8,128)(2,1)}, u32[]{:S(2)}) copy-start(bf16[8,128,512]{2,1,0:T(8,128)(2,1)} %constant.83.clone.pick_ref) | copy-start | bytes 3145732
  55.9 7.8 %collective-permute-start.14 = (bf16[9,72,128]{2,1,0:T(8,128)(2,1)S(1)}, bf16[9,72,128]{2,1,0:T(8,128)(2,1)S(1)}, u32[]{:S(2)}, u32[]{:S(2)}) collective-permute-start(bf16[9,72,128]{2,1,0:T(8,128)(2,1)S(1)} %get-tuple-element.79), channel_id=1, source_target_pairs={{0,1},{1,0},{2,3},{3,2},{4,5},{5,4},{6,7},{7,6},{8,9},{9,8},{10,11... | collective-permute-start | bytes 497672 | tf_op jit(solution)/shard_map/ppermute | solution.py:597
  55.9 7.8 %collective-permute-start.17 = (bf16[9,72,128]{2,1,0:T(8,128)(2,1)S(1)}, bf16[9,72,128]{2,1,0:T(8,128)(2,1)S(1)}, u32[]{:S(2)}, u32[]{:S(2)}) collective-permute-start(bf16[9,72,128]{2,1,0:T(8,128)(2,1)S(1)} %get-tuple-element.83), channel_id=1, source_target_pairs={{0,3},{1,2},{2,1},{3,0},{4,7},{5,6},{6,5},{7,4},{8,11},{9,10},{10,... | collective-permute-start | bytes 497672 | tf_op jit(solution)/shard_map/ppermute | solution.py:597
